TPU v7x, 32 devices: a whole 2x2x4 slice. The times are simulated.
32 devices in a mesh: groups: 2 (over x), expert: 4 (over y, core), dp: 4 (over z).
Axes of the slice: x: 2, y: 2, z: 4, core: 2. Of those that a mesh axis runs over, the one named last changes fastest.
Arguments:
- tokens: bfloat16 [4096, 3584], P(('groups', 'expert', 'dp')), parts along dimension 0, may hold values from -6 to 6
- routes: int32 [4096, 1], P(('groups', 'expert', 'dp')), parts along dimension 0, may hold values from 0 to 3; in each aligned block of 128 rows (0 to 127, 128 to 255, ...) at most 48 rows name the same one
- gates: float32 [4096, 1], P(('groups', 'expert', 'dp')), parts along dimension 0, may hold values from 0.25 to 1
- gate_weight: bfloat16 [4, 3584, 1024], P('expert', 'dp'), may hold values from -0.09375 to 0.09375
- up_weight: bfloat16 [4, 3584, 1024], P('expert', 'dp'), may hold values from -0.09375 to 0.09375
- down_weight: bfloat16 [4, 3584, 1024], P('expert', 'dp'), may hold values from -0.1875 to 0.1875
- cotangent: bfloat16 [4096, 3584], P(('groups', 'expert', 'dp')), parts along dimension 0, may hold values from -6 to 6
Outputs:
- mixed: bfloat16 [4096, 3584], P(('groups', 'expert', 'dp')), parts along dimension 0
- token_grad: bfloat16 [4096, 3584], P(('groups', 'expert', 'dp')), parts along dimension 0
- gate_grad: bfloat16 [8, 3584, 1024], P(('groups', 'expert'), 'dp'), parts along dimension 0
- up_grad: bfloat16 [8, 3584, 1024], P(('groups', 'expert'), 'dp'), parts along dimension 0
- down_grad: bfloat16 [8, 3584, 1024], P(('groups', 'expert'), 'dp'), parts along dimension 0
There are 2 independent parts, one for each index of `groups`. A program takes and returns all parts, laid end to end along the dimension named above; an argument that names none is the same for every part. Nothing has to cross between parts.
Inputs may be any that keep to these rules, and one draw needn't show every extreme that they name: Each token is routed to exactly one expert. The routes of one device's 128 tokens name one expert at most 48 times, and in every draw some expert is named exactly 48 times by some device.
All inputs are finite; a program needn't handle non-finite values.
Results may differ from a plain program's by a relative error of at most 0.0058.
Values may be sent and summed in bfloat16 or wider, within the bound.
No kernel may reach another device: no remote copies, remote signals or barrier semaphores. Data moves between devices by JAX's collectives and lax.ppermute only.
A program may use at most 256 MiB of HBM per device.

v0:
```python
import jax
import jax.numpy as jnp
from jax import lax
from jax.sharding import PartitionSpec as P


def route_places(routes, experts, capacity):
    flat_ids = routes.reshape(-1)
    onehot = (flat_ids[:, None] == jnp.arange(experts, dtype=jnp.int32)[None, :]).astype(jnp.int32)
    before = jnp.cumsum(onehot, axis=0) - onehot
    slot_pos = jnp.sum(before * onehot, axis=1)
    return flat_ids * capacity + slot_pos


def across(left, right):
    return lax.dot_general(
        left, right, (((1,), (1,)), ((), ())), preferred_element_type=jnp.float32
    )


def over_rows(left, right):
    return lax.dot_general(
        left, right, (((0,), (0,)), ((), ())), preferred_element_type=jnp.float32
    )


def shards(tokens, routes, gates, gate_weight, up_weight, down_weight, cotangent):
    n_exp = lax.axis_size("expert") * gate_weight.shape[0]
    tok_count, topk = routes.shape
    width = tokens.shape[1]
    hidden_units = gate_weight.shape[2]
    capacity = 3 * tok_count * topk // (2 * n_exp)
    flat_count = tok_count * topk
    dest = route_places(routes, n_exp, capacity)
    owner = jnp.arange(flat_count, dtype=jnp.int32) // topk
    gate_flat = gates.reshape(-1)
    weighted_tok = (gate_flat[:, None] * cotangent[owner].astype(jnp.float32)).astype(jnp.bfloat16)
    empty = jnp.zeros((n_exp * capacity, width), jnp.bfloat16)
    send_rows = empty.at[dest].set(tokens[owner]).reshape(n_exp, capacity, width)
    send_grads = empty.at[dest].set(weighted_tok).reshape(n_exp, capacity, width)
    got_rows, got_grads = (
        lax.all_to_all(send_rows, "expert", split_axis=0, concat_axis=0, tiled=True),
        lax.all_to_all(send_grads, "expert", split_axis=0, concat_axis=0, tiled=True),
    )
    rows = got_rows.reshape(-1, width)
    weighted = got_grads.reshape(-1, width)
    local_gate = gate_weight[0]
    local_up = up_weight[0]
    local_down = down_weight[0]
    col_rows, col_grads = (
        lax.all_to_all(rows, "dp", split_axis=1, concat_axis=0, tiled=True),
        lax.all_to_all(weighted, "dp", split_axis=1, concat_axis=0, tiled=True),
    )
    summed_pre = lax.psum_scatter(
        jnp.concatenate(
            [
                jnp.dot(col_rows, local_gate, preferred_element_type=jnp.float32),
                jnp.dot(col_rows, local_up, preferred_element_type=jnp.float32),
                jnp.dot(col_grads, local_down, preferred_element_type=jnp.float32),
            ],
            axis=1,
        ),
        "dp",
        scatter_dimension=0,
        tiled=True,
    )
    pre_gate = summed_pre[:, :hidden_units]
    pre_up = summed_pre[:, hidden_units : 2 * hidden_units]
    hidden_grad = summed_pre[:, 2 * hidden_units :]
    sig = jax.nn.sigmoid(pre_gate)
    active = pre_gate * sig
    hidden = (active * pre_up).astype(jnp.bfloat16)
    pg_grad = (hidden_grad * pre_up * sig * (1.0 + pre_gate * (1.0 - sig))).astype(jnp.bfloat16)
    pu_grad = (hidden_grad * active).astype(jnp.bfloat16)
    all_hidden, all_pg, all_pu = (
        lax.all_gather(hidden, "dp", axis=0, tiled=True),
        lax.all_gather(pg_grad, "dp", axis=0, tiled=True),
        lax.all_gather(pu_grad, "dp", axis=0, tiled=True),
    )
    out_cols = across(all_hidden, local_down).astype(jnp.bfloat16)
    grad_cols = (across(all_pg, local_gate) + across(all_pu, local_up)).astype(jnp.bfloat16)
    expert_out, row_grad = (
        lax.all_to_all(out_cols, "dp", split_axis=0, concat_axis=1, tiled=True),
        lax.all_to_all(grad_cols, "dp", split_axis=0, concat_axis=1, tiled=True),
    )
    gate_grad = over_rows(col_rows, all_pg).astype(jnp.bfloat16)
    up_grad = over_rows(col_rows, all_pu).astype(jnp.bfloat16)
    down_grad = over_rows(col_grads, all_hidden).astype(jnp.bfloat16)
    back_out, back_grad = (
        lax.all_to_all(
            expert_out.reshape(-1, capacity, width),
            "expert",
            split_axis=0,
            concat_axis=0,
            tiled=True,
        ),
        lax.all_to_all(
            row_grad.reshape(-1, capacity, width), "expert", split_axis=0, concat_axis=0, tiled=True
        ),
    )
    picked_out = back_out.reshape(-1, width)[dest].astype(jnp.float32)
    mixed = jnp.sum(
        (picked_out * gate_flat[:, None]).reshape(tok_count, topk, width), axis=1
    ).astype(jnp.bfloat16)
    picked_grad = back_grad.reshape(-1, width)[dest].astype(jnp.float32)
    token_grad = jnp.sum(picked_grad.reshape(tok_count, topk, width), axis=1).astype(jnp.bfloat16)
    return (mixed, token_grad, gate_grad[None], up_grad[None], down_grad[None])


def solution(mesh):
    return jax.shard_map(
        shards,
        mesh=mesh,
        in_specs=(
            P(("groups", "expert", "dp"), None),
            P(("groups", "expert", "dp"), None),
            P(("groups", "expert", "dp"), None),
            P("expert", "dp", None),
            P("expert", "dp", None),
            P("expert", "dp", None),
            P(("groups", "expert", "dp"), None),
        ),
        out_specs=(
            P(("groups", "expert", "dp"), None),
            P(("groups", "expert", "dp"), None),
            P(("groups", "expert"), "dp", None),
            P(("groups", "expert"), "dp", None),
            P(("groups", "expert"), "dp", None),
        ),
        check_vma=False,
    )
```

profile of v0, /device:TPU:0, one launch (start us, length us, event | category | flops | bytes accessed | tf_op | source)
XLA Modules:
  0.0 547.8 jit_solution(3790403735120411118)
XLA Ops:
  9.7 5.8 %scatter_custom_fusion = bf16[192,3584]{1,0:T(8,128)(2,1)} fusion(s32[128]{0:T(128)S(1)} %fusion.25, bf16[128,3584]{1,0:T(8,128)(2,1)} %param.7, s32[1024]{0:T(1024)S(1)} %pad_clamp_fusion.1, bf16[]{:T(256)} %constant.24.clone.1), kind=kCustom, calls=%fused_computation.27 | custom fusion | bytes 1376768 | tf_op jit(solution)/shard_map/scatter | solution.py:39
  15.6 4.4 all-to-all-start
  20.0 5.9 %scatter_custom_fusion.1 = bf16[192,3584]{1,0:T(8,128)(2,1)} fusion(s32[128]{0:T(128)S(1)} %fusion.25, f32[128]{0:T(128)S(1)} %bitcast.70, bf16[]{:T(256)} %constant.24.clone.1, bf16[128,3584]{1,0:T(8,128)(2,1)} %param.13, s32[1024]{0:T(1024)S(1)} %pad_clamp_fusion.1), kind=kCustom, calls=%fused_computation.26 | custom fusion | flops 1376256 | bytes 2298370 | tf_op jit(solution)/shard_map/scatter | solution.py:40
  25.9 12.0 %all-to-all-done = bf16[4,48,3584]{2,1,0:T(8,128)(2,1)S(1)} async-done(((bf16[4,48,3584]{2,1,0:T(8,128)(2,1)}), bf16[4,48,3584]{2,1,0:T(8,128)(2,1)S(1)}, u32[]{:S(2)}, u32[]{:S(2)}) %all-to-all-start) | async-done | bytes 1376288 | tf_op jit(solution)/shard_map/all_to_all | solution.py:42
  48.8 11.7 %all-to-all-done.2 = bf16[4,48,3584]{2,1,0:T(8,128)(2,1)S(1)} async-done(((bf16[4,48,3584]{2,1,0:T(8,128)(2,1)}), bf16[4,48,3584]{2,1,0:T(8,128)(2,1)S(1)}, u32[]{:S(2)}, u32[]{:S(2)}) %all-to-all-start.2) | async-done | bytes 1376288 | tf_op jit(solution)/shard_map/all_to_all | solution.py:43
  60.5 5.6 %all-to-all-start.1 = ((bf16[192,4,896]{2,0,1:T(8,128)(2,1)}), bf16[192,4,896]{2,0,1:T(8,128)(2,1)}, u32[]{:S(2)}, u32[]{:S(2)}) async-start(bf16[192,4,896]{2,0,1:T(8,128)(2,1)} %copy.18), calls=%async_computation.1 | async-start | bytes 2752512 | tf_op jit(solution)/shard_map/all_to_all | solution.py:51
  69.9 28.8 %all-to-all-done.1 = bf16[192,4,896]{2,0,1:T(8,128)(2,1)} async-done(((bf16[192,4,896]{2,0,1:T(8,128)(2,1)}), bf16[192,4,896]{2,0,1:T(8,128)(2,1)}, u32[]{:S(2)}, u32[]{:S(2)}) %all-to-all-start.1) | async-done | bytes 1376288 | tf_op jit(solution)/shard_map/all_to_all | solution.py:51
  102.5 5.3 fusion.10
  107.9 4.8 fusion.6
  112.7 21.8 %all-to-all-done.3 = bf16[192,4,896]{2,0,1:T(8,128)(2,1)S(1)} async-done(((bf16[192,4,896]{2,0,1:T(8,128)(2,1)}), bf16[192,4,896]{2,0,1:T(8,128)(2,1)S(1)}, u32[]{:S(2)}, u32[]{:S(2)}) %all-to-all-start.3) | async-done | bytes 1376288 | tf_op jit(solution)/shard_map/all_to_all | solution.py:52
  134.5 5.4 fusion.2
  140.0 8.6 %pad_maximum_fusion = f32[768,3072]{1,0:T(8,128)} fusion(f32[768,1024]{1,0:T(8,128)} %fusion.2, f32[768,1024]{1,0:T(8,128)} %fusion.6, f32[768,1024]{1,0:T(8,128)} %fusion.10), kind=kLoop, calls=%fused_computation.6 | loop fusion | flops 4718592 | bytes 18874368 | tf_op jit(solution)/shard_map/concatenate | solution.py:55
  148.7 159.6 %reduce-scatter.2.cloned.1.call-done = f32[192,3072]{1,0:T(8,128)} async-done(((f32[768,3072]{1,0:T(8,128)}), f32[192,3072]{1,0:T(8,128)}) %reduce-scatter.2.cloned.1.call-update) | async-done | bytes 2359312 | tf_op jit(solution)/shard_map/reduce_scatter | solution.py:54
  312.7 36.8 %all-gather.8.cloned.1.call-done = bf16[768,1024]{1,0:T(8,128)(2,1)} async-done(((bf16[192,1024]{1,0:T(8,128)(2,1)}), bf16[768,1024]{1,0:T(8,128)(2,1)}) %all-gather.8.cloned.1.call-update) | async-done | bytes 1572880 | tf_op jit(solution)/shard_map/all_gather | solution.py:78
  349.5 4.8 fusion.4
  354.2 33.4 %all-gather.6.cloned.1.call-done = bf16[768,1024]{1,0:T(8,128)(2,1)} async-done(((bf16[192,1024]{1,0:T(8,128)(2,1)}), bf16[768,1024]{1,0:T(8,128)(2,1)}) %all-gather.6.cloned.1.call-update) | async-done | bytes 1572880 | tf_op jit(solution)/shard_map/all_gather | solution.py:77
  387.6 5.7 %add_convert_fusion = bf16[768,896]{1,0:T(8,128)(2,1)} fusion(f32[768,896]{1,0:T(8,128)} %fusion.4, bf16[768,1024]{1,0:T(8,128)(2,1)} %all-gather.6.cloned.1.call-done, bf16[1,896,1024]{2,1,0:T(8,128)(2,1)} %param.10), kind=kOutput, calls=%fused_computation.7 | convolution fusion | flops 1410662400 | bytes 7536640 | tf_op jit(solution)/shard_map/dot_general | solution.py:16
  396.9 55.9 %all-gather.4.cloned.1.call-done = bf16[768,1024]{1,0:T(8,128)(2,1)} async-done(((bf16[192,1024]{1,0:T(8,128)(2,1)}), bf16[768,1024]{1,0:T(8,128)(2,1)}) %all-gather.4.cloned.1.call-update) | async-done | bytes 1572880 | tf_op jit(solution)/shard_map/all_gather | solution.py:76
  452.8 4.9 fusion.12
  466.9 27.1 %all-to-all-done.4 = bf16[4,192,896]{2,1,0:T(8,128)(2,1)S(1)} async-done(((bf16[4,192,896]{2,1,0:T(8,128)(2,1)}), bf16[4,192,896]{2,1,0:T(8,128)(2,1)S(1)}, u32[]{:S(2)}, u32[]{:S(2)}) %all-to-all-start.4) | async-done | bytes 1376288 | tf_op jit(solution)/shard_map/all_to_all | solution.py:83
  503.4 12.1 %all-to-all-done.7 = bf16[4,48,3584]{2,1,0:T(8,128)(2,1)S(1)} async-done(((bf16[4,48,3584]{2,1,0:T(8,128)(2,1)}), bf16[4,48,3584]{2,1,0:T(8,128)(2,1)S(1)}, u32[]{:S(2)}, u32[]{:S(2)}) %all-to-all-start.7) | async-done | bytes 1376288 | tf_op jit(solution)/shard_map/all_to_all | solution.py:97
  519.0 4.8 convert_bitcast_fusion.1
  523.8 4.4 convert_bitcast_fusion.2
  533.1 3.9 all-to-all-done.5
  (51 shorter events, 60.4 us)
Async XLA Ops:
  7.2 100.7 %copy-start = (bf16[1,896,1024]{2,1,0:T(8,128)(2,1)S(1)}, bf16[1,896,1024]{2,1,0:T(8,128)(2,1)}, u32[]{:S(2)}) copy-start(bf16[1,896,1024]{2,1,0:T(8,128)(2,1)} %param.11) | copy-start | bytes 5505028
  15.6 4.4 copy-start.5
  15.6 22.3 %all-to-all-start = ((bf16[4,48,3584]{2,1,0:T(8,128)(2,1)}), bf16[4,48,3584]{2,1,0:T(8,128)(2,1)S(1)}, u32[]{:S(2)}, u32[]{:S(2)}) async-start(bf16[4,48,3584]{2,1,0:T(8,128)(2,1)} %bitcast.64), calls=%async_computation | async-start | bytes 2752512 | tf_op jit(solution)/shard_map/all_to_all | solution.py:42
  37.9 1.1 copy-start.2
  39.0 21.5 %all-to-all-start.2 = ((bf16[4,48,3584]{2,1,0:T(8,128)(2,1)}), bf16[4,48,3584]{2,1,0:T(8,128)(2,1)S(1)}, u32[]{:S(2)}, u32[]{:S(2)}) async-start(bf16[4,48,3584]{2,1,0:T(8,128)(2,1)} %bitcast.63), calls=%async_computation.2 | async-start | bytes 2752512 | tf_op jit(solution)/shard_map/all_to_all | solution.py:43
  60.5 38.3 %all-to-all-start.1 = ((bf16[192,4,896]{2,0,1:T(8,128)(2,1)}), bf16[192,4,896]{2,0,1:T(8,128)(2,1)}, u32[]{:S(2)}, u32[]{:S(2)}) async-start(bf16[192,4,896]{2,0,1:T(8,128)(2,1)} %copy.18), calls=%async_computation.1 | async-start | bytes 2752512 | tf_op jit(solution)/shard_map/all_to_all | solution.py:51
  98.8 35.8 %all-to-all-start.3 = ((bf16[192,4,896]{2,0,1:T(8,128)(2,1)}), bf16[192,4,896]{2,0,1:T(8,128)(2,1)S(1)}, u32[]{:S(2)}, u32[]{:S(2)}) async-start(bf16[192,4,896]{2,0,1:T(8,128)(2,1)} %copy.19), calls=%async_computation.3 | async-start | bytes 2752512 | tf_op jit(solution)/shard_map/all_to_all | solution.py:52
  102.3 206.0 %reduce-scatter.2.cloned.1.call-start = ((), (), s32[]{:S(2)}) async-start(), calls=%async_computation.9 | async-start | bytes 11796480 | tf_op jit(solution)/shard_map/reduce_scatter | solution.py:54
  134.5 5.4 copy-start.3
  148.6 200.9 %all-gather.8.cloned.1.call-start = ((), (), s32[]{:S(2)}) async-start(), calls=%async_computation.12 | async-start | bytes 1966080 | tf_op jit(solution)/shard_map/all_gather | solution.py:78
  311.4 76.2 %all-gather.6.cloned.1.call-start = ((), (), s32[]{:S(2)}) async-start(), calls=%async_computation.11 | async-start | bytes 1966080 | tf_op jit(solution)/shard_map/all_gather | solution.py:77
  312.1 140.7 %all-gather.4.cloned.1.call-start = ((), (), s32[]{:S(2)}) async-start(), calls=%async_computation.10 | async-start | bytes 1966080 | tf_op jit(solution)/shard_map/all_gather | solution.py:76
  393.3 64.4 %all-to-all-start.6 = ((bf16[4,192,896]{2,1,0:T(8,128)(2,1)}), bf16[4,192,896]{2,1,0:T(8,128)(2,1)S(1)}, u32[]{:S(2)}, u32[]{:S(2)}) async-start(bf16[4,192,896]{2,1,0:T(8,128)(2,1)} %bitcast.17), calls=%async_computation.7 | async-start | bytes 2752512 | tf_op jit(solution)/shard_map/all_to_all | solution.py:84
  457.7 36.3 %all-to-all-start.4 = ((bf16[4,192,896]{2,1,0:T(8,128)(2,1)}), bf16[4,192,896]{2,1,0:T(8,128)(2,1)S(1)}, u32[]{:S(2)}, u32[]{:S(2)}) async-start(bf16[4,192,896]{2,1,0:T(8,128)(2,1)} %bitcast.67), calls=%async_computation.5 | async-start | bytes 2752512 | tf_op jit(solution)/shard_map/all_to_all | solution.py:83
  494.0 21.5 %all-to-all-start.7 = ((bf16[4,48,3584]{2,1,0:T(8,128)(2,1)}), bf16[4,48,3584]{2,1,0:T(8,128)(2,1)S(1)}, u32[]{:S(2)}, u32[]{:S(2)}) async-start(bf16[4,48,3584]{2,1,0:T(8,128)(2,1)} %reshape.65), calls=%async_computation.8 | async-start | bytes 2752512 | tf_op jit(solution)/shard_map/all_to_all | solution.py:97
  515.5 21.5 %all-to-all-start.5 = ((bf16[4,48,3584]{2,1,0:T(8,128)(2,1)}), bf16[4,48,3584]{2,1,0:T(8,128)(2,1)S(1)}, u32[]{:S(2)}, u32[]{:S(2)}) async-start(bf16[4,48,3584]{2,1,0:T(8,128)(2,1)} %reshape.63), calls=%async_computation.6 | async-start | bytes 2752512 | tf_op jit(solution)/shard_map/all_to_all | solution.py:90
  519.0 4.8 copy-start.6
  523.8 4.4 copy-start.4
  523.8 4.4 copy-start.7
  536.9 4.4 copy-start.1
Sparse Core Ops, SparseCore 0:
  148.7 159.5 reduce-scatter.1
  311.5 37.9 all-gather.7
  351.6 35.9 all-gather.5
  389.6 63.1 all-gather.3
where the time goes:
time: 549 us; the launch traced here: 548 us
  waiting for transfers between devices  404 us (74%)
  matrix products  43 us (8%)
  local copies, waits for them, and re-layouts  32.4 us (6%)
  starting transfers between devices  31.8 us (6%)
  other arithmetic  22.5 us (4%)
  between operations  13.9 us (3%)
    reduce_scatter x1, waiting for transfers between devices, shards(): lax.psum_scatter(jnp.concatenate([jnp.dot(col_rows, local_gate, preferred...  160 us
    all_gather x1, waiting for transfers between devices, shards(): lax.all_gather(hidden, 'dp', axis=0, tiled=True)  55.9 us
    all_gather x1, waiting for transfers between devices, shards(): lax.all_gather(pu_grad, 'dp', axis=0, tiled=True)  36.8 us
    all_gather x1, waiting for transfers between devices, shards(): lax.all_gather(pg_grad, 'dp', axis=0, tiled=True)  33.4 us
    all_to_all x1, waiting for transfers between devices, shards(): lax.all_to_all(rows, 'dp', split_axis=1, concat_axis=0, tiled=True)  28.8 us
    all_to_all x1, waiting for transfers between devices, shards(): lax.all_to_all(out_cols, 'dp', split_axis=0, concat_axis=1, tiled=True)  27.1 us
    all_to_all x1, waiting for transfers between devices, shards(): lax.all_to_all(weighted, 'dp', split_axis=1, concat_axis=0, tiled=True)  21.8 us
    dot_general x3, matrix products, across(): lax.dot_general(left, right, (((1,), (1,)), ((), ())), preferred_element_...  15.4 us
  transfers between devices with their start and end apart: 12, of which 11 were waited for; matrix products, arithmetic and copies ran while one was open for 11% of the time, Pallas kernels for 0%

commit v1 on v0

v1 whole, which is shorter than its diff:
```python
import jax
import jax.numpy as jnp
from jax import lax
from jax.sharding import PartitionSpec as P

F32 = jnp.float32
BF16 = jnp.bfloat16


def route_places(routes, experts, capacity):
    flat_ids = routes.reshape(-1)
    onehot = (flat_ids[:, None] == jnp.arange(experts, dtype=jnp.int32)[None, :]).astype(jnp.int32)
    before = jnp.cumsum(onehot, axis=0) - onehot
    slot_pos = jnp.sum(before * onehot, axis=1)
    return flat_ids * capacity + slot_pos


def across(left, right):
    return lax.dot_general(left, right, (((1,), (1,)), ((), ())), preferred_element_type=F32)


def over_rows(left, right):
    return lax.dot_general(left, right, (((0,), (0,)), ((), ())), preferred_element_type=F32)


def swap(value, axis, distance):
    count = lax.axis_size(axis)
    return lax.ppermute(value, axis, [(i, i ^ distance) for i in range(count)])


def line_sum(partial, axis):
    count = lax.axis_size(axis)
    total = partial
    for hop in range(count // 2 - 1):
        pairs = [(hop, hop + 1), (count - 1 - hop, count - 2 - hop)]
        total = partial + lax.ppermute(total.astype(BF16), axis, pairs).astype(F32)
    mid = count // 2
    return total + lax.ppermute(total.astype(BF16), axis, [(mid - 1, mid), (mid, mid - 1)]).astype(F32)


def line_spread(value, axis):
    count = lax.axis_size(axis)
    here = lax.axis_index(axis)
    for hop in reversed(range(count // 2 - 1)):
        pairs = [(hop + 1, hop), (count - 2 - hop, count - 1 - hop)]
        sent = lax.ppermute(value, axis, pairs)
        value = jnp.where((here == hop) | (here == count - 1 - hop), sent, value)
    return value


def shards(tokens, routes, gates, gate_weight, up_weight, down_weight, cotangent):
    n_exp = lax.axis_size("expert") * gate_weight.shape[0]
    n_dp = lax.axis_size("dp")
    me = lax.axis_index("expert")
    here = lax.axis_index("dp")
    tok_count, topk = routes.shape
    width = tokens.shape[1]
    part = width // n_dp
    hidden_units = gate_weight.shape[2]
    capacity = 3 * tok_count * topk // (2 * n_exp)
    chunk = n_dp * capacity
    w_gate, w_up, w_down = gate_weight[0], up_weight[0], down_weight[0]
    w_both = jnp.concatenate([w_gate, w_up], axis=1)

    codes = lax.all_gather(route_places(routes, n_exp, capacity), "dp")
    blocks = here ^ jnp.arange(n_dp, dtype=jnp.int32)
    codes = codes[blocks]
    places = ((codes // capacity) ^ me) * chunk + blocks[:, None] * capacity + codes % capacity
    places = places.reshape(-1)
    select = (jnp.arange(n_exp * chunk, dtype=jnp.int32)[:, None] == places[None, :]).astype(BF16)

    def columns(value, distance):
        return lax.dynamic_slice(value, (0, (here ^ distance) * part), (tok_count, part))

    def dispatch(pieces):
        gathered = jnp.concatenate(pieces, axis=0)
        rows = jnp.dot(select, gathered, preferred_element_type=F32).astype(BF16)
        rows = rows.reshape(n_exp, chunk, part)
        return [rows[0]] + [swap(rows[k], "expert", k) for k in range(1, n_exp)]

    weighted = (gates * cotangent.astype(F32)).astype(BF16)
    order = [0] + list(range(n_dp - 1, 0, -1))
    by_distance = {k: columns(tokens, k) if k == 0 else swap(columns(tokens, k), "dp", k) for k in order}
    rows = dispatch([by_distance[k] for k in range(n_dp)])
    by_distance = {k: columns(weighted, k) if k == 0 else swap(columns(weighted, k), "dp", k) for k in order}
    grads = dispatch([by_distance[k] for k in range(n_dp)])

    hidden, pg, pu, out, back = [], [], [], [], []
    for k in range(n_exp):
        pre = line_sum(jnp.dot(rows[k], w_both, preferred_element_type=F32), "dp")
        pre_gate, pre_up = pre[:, :hidden_units], pre[:, hidden_units:]
        sig = jax.nn.sigmoid(pre_gate)
        active = pre_gate * sig
        hidden.append(line_spread((active * pre_up).astype(BF16), "dp"))
        hidden_grad = line_sum(jnp.dot(grads[k], w_down, preferred_element_type=F32), "dp")
        pg_grad = (hidden_grad * pre_up * sig * (1.0 + pre_gate * (1.0 - sig))).astype(BF16)
        pu_grad = (hidden_grad * active).astype(BF16)
        both = line_spread(jnp.concatenate([pg_grad, pu_grad], axis=1), "dp")
        pg.append(both[:, :hidden_units])
        pu.append(both[:, hidden_units:])
        out_k = across(hidden[k], w_down).astype(BF16)
        back_k = across(both, w_both).astype(BF16)
        out.append(out_k if k == 0 else swap(out_k, "expert", k))
        back.append(back_k if k == 0 else swap(back_k, "expert", k))

    def give_back(parts_, scale):
        picked = over_rows(select, jnp.concatenate(parts_, axis=0)).astype(BF16).reshape(n_dp, tok_count, part)
        result = jnp.zeros((tok_count, width), BF16)
        for k in order:
            piece = picked[k] if k == 0 else swap(picked[k], "dp", k)
            if scale is not None:
                piece = (piece.astype(F32) * scale).astype(BF16)
            result = lax.dynamic_update_slice(result, piece, (0, (here ^ k) * part))
        return result

    mixed = give_back(out, gates)
    token_grad = give_back(back, None)
    all_rows, all_grads = jnp.concatenate(rows, axis=0), jnp.concatenate(grads, axis=0)
    gate_grad = over_rows(all_rows, jnp.concatenate(pg, axis=0)).astype(BF16)
    up_grad = over_rows(all_rows, jnp.concatenate(pu, axis=0)).astype(BF16)
    down_grad = over_rows(all_grads, jnp.concatenate(hidden, axis=0)).astype(BF16)
    return (mixed, token_grad, gate_grad[None], up_grad[None], down_grad[None])


def solution(mesh):
    rows = P(("groups", "expert", "dp"), None)
    weights = P("expert", "dp", None)
    grads = P(("groups", "expert"), "dp", None)
    return jax.shard_map(
        shards,
        mesh=mesh,
        in_specs=(rows, rows, rows, weights, weights, weights, rows),
        out_specs=(rows, rows, grads, grads, grads),
        check_vma=False,
    )
```

time: 549 us -> 383 us (0.70)
  waiting for transfers between devices: 404 us -> 231 us
  starting transfers between devices: 31.8 us -> 84.6 us
  local copies, waits for them, and re-layouts: 32.4 us -> 4.69 us
  blocking collectives: 0 us -> 22.8 us
  other arithmetic: 22.5 us -> 7.45 us
  matrix products: 43 us -> 30.1 us
  between operations: 13.9 us -> 1.65 us
    ppermute x0 -> x48, waiting for transfers between devices: none -> 231 us  [the longest x8 139 us: line_spread(): sent = lax.ppermute(value, axis, pairs)]
    reduce_scatter x1 -> x0, waiting for transfers between devices: 160 us -> none  [shards(): lax.psum_scatter(jnp.concatenate([jnp.dot(col_rows, local_gate, preferred...]
    all_gather x3 -> x0, waiting for transfers between devices: 126 us -> none  [the longest x1 55.9 us: shards(): lax.all_gather(hidden, 'dp', axis=0, tiled=True)]
    all_to_all x8 -> x0, waiting for transfers between devices: 117 us -> none  [the longest x1 28.8 us: shards(): lax.all_to_all(rows, 'dp', split_axis=1, concat_axis=0, tiled=True)]
    ppermute x0 -> x48, starting transfers between devices: none -> 84.6 us  [the longest x24 40.9 us: swap(): return lax.ppermute(value, axis, [(i, i ^ distance) for i in range(count)])]
    all_to_all x8 -> x0, starting transfers between devices: 31.5 us -> none  [the longest x1 5.6 us: shards(): lax.all_to_all(rows, 'dp', split_axis=1, concat_axis=0, tiled=True)]
    all_gather x0 -> x1, blocking collectives: none -> 22.8 us  [shards(): codes = lax.all_gather(route_places(routes, n_exp, capacity), 'dp')]
    all_to_all x6 -> x0, local copies, waits for them, and re-layouts: 14.3 us -> none  [the longest x2 6.24 us: shards(): lax.all_to_all(rows, 'dp', split_axis=1, concat_axis=0, tiled=True)]
  transfers between devices with their start and end apart: 12 -> 48, of which waited for: 11 -> 19; matrix products, arithmetic and copies ran while one was open for 11% -> 10% of each run, Pallas kernels for 0% -> 0%
where the time goes in v1:
time: 383 us; the launch traced here: 382 us
  waiting for transfers between devices  231 us (60%)
  starting transfers between devices  84.6 us (22%)
  matrix products  30.1 us (8%)
  blocking collectives  22.8 us (6%)
  other arithmetic  7.45 us (2%)
  local copies, waits for them, and re-layouts  4.69 us (1%)
    ppermute x8, waiting for transfers between devices, line_spread(): sent = lax.ppermute(value, axis, pairs)  139 us
    ppermute x8, waiting for transfers between devices, line_sum(): total = partial + lax.ppermute(total.astype(BF16), axis, pairs).astype(F32)  50.5 us
    ppermute x24, waiting for transfers between devices, swap(): return lax.ppermute(value, axis, [(i, i ^ distance) for i in range(count)])  41.8 us
    ppermute x24, starting transfers between devices, swap(): return lax.ppermute(value, axis, [(i, i ^ distance) for i in range(count)])  40.9 us
    ppermute x8, starting transfers between devices, line_sum(): total = partial + lax.ppermute(total.astype(BF16), axis, pairs).astype(F32)  27.3 us
    all_gather x1, blocking collectives, shards(): codes = lax.all_gather(route_places(routes, n_exp, capacity), 'dp')  22.8 us
    dot_general x5, matrix products, over_rows(): lax.dot_general(left, right, (((0,), (0,)), ((), ())), preferred_element_...  10.7 us
    ppermute x8, starting transfers between devices, line_spread(): sent = lax.ppermute(value, axis, pairs)  10.5 us
  transfers between devices with their start and end apart: 48, of which 19 were waited for; matrix products, arithmetic and copies ran while one was open for 10% of the time, Pallas kernels for 0%

profile of v1, /device:TPU:0, one launch (start us, length us, event | category | flops | bytes accessed | tf_op | source)
XLA Modules:
  0.0 382.5 jit_solution(14253661947272427016)
XLA Ops:
  9.9 3.5 collective-permute-start.25
  13.9 22.8 %all-gather = s32[4,1,128]{2,1,0:T(1,128)S(1)} all-gather(s32[1,1,128]{2,1,0:T(1,128)S(1)} %fusion.117), channel_id=1, replica_groups=mesh['groups'=2,'expert'=4,'dp'=4] {'dp'}, dimensions={0}, use_global_device_ids=true | all-gather | bytes 2560 | tf_op jit(solution)/shard_map/all_gather | solution.py:65
  37.3 6.7 %collective-permute-start.26 = (bf16[128,896]{1,0:T(8,128)(2,1)S(1)}, bf16[128,896]{1,0:T(8,128)(2,1)S(1)}, u32[]{:S(2)}, u32[]{:S(2)}) collective-permute-start(bf16[128,896]{1,0:T(8,128)(2,1)S(1)} %get-tuple-element.30), channel_id=1, source_target_pairs={{0,3},{1,2},{2,1},{3,0},{4,7},{5,6},{6,5},{7,4},{8,11},{9,10},{10,... | collective-permute-start | bytes 688136 | tf_op jit(solution)/shard_map/ppermute | solution.py:28
  53.5 4.6 %collective-permute-start.27 = (bf16[192,1024]{1,0:T(8,128)(2,1)S(1)}, bf16[192,1024]{1,0:T(8,128)(2,1)S(1)}, u32[]{:S(2)}, u32[]{:S(2)}) collective-permute-start(bf16[192,1024]{1,0:T(8,128)(2,1)S(1)} %get-tuple-element.63), channel_id=1, source_target_pairs={{0,1},{3,2},{4,5},{7,6},{8,9},{11,10},{12,13},{15,14},{16,17},{19,... | collective-permute-start | bytes 1179656 | tf_op jit(solution)/shard_map/ppermute | solution.py:36
  64.8 4.0 %collective-permute-done.16 = bf16[192,896]{1,0:T(8,128)(2,1)S(1)} collective-permute-done((bf16[192,896]{1,0:T(8,128)(2,1)S(1)}, bf16[192,896]{1,0:T(8,128)(2,1)S(1)}, u32[]{:S(2)}, u32[]{:S(2)}) %collective-permute-start.16) | collective-permute-done | bytes 344096 | tf_op jit(solution)/shard_map/ppermute | solution.py:28
  71.6 5.1 %collective-permute-start.7 = (bf16[192,2048]{1,0:T(8,128)(2,1)S(1)}, bf16[192,2048]{1,0:T(8,128)(2,1)S(1)}, u32[]{:S(2)}, u32[]{:S(2)}) collective-permute-start(bf16[192,2048]{1,0:T(8,128)(2,1)S(1)} %get-tuple-element.57), channel_id=1, source_target_pairs={{0,1},{3,2},{4,5},{7,6},{8,9},{11,10},{12,13},{15,14},{16,17},{19,... | collective-permute-start | bytes 2359304 | tf_op jit(solution)/shard_map/ppermute | solution.py:36
  77.3 3.8 collective-permute-start.31
  87.8 15.3 %collective-permute-done.31 = bf16[192,1024]{1,0:T(8,128)(2,1)S(1)} collective-permute-done((bf16[192,1024]{1,0:T(8,128)(2,1)S(1)}, bf16[192,1024]{1,0:T(8,128)(2,1)S(1)}, u32[]{:S(2)}, u32[]{:S(2)}) %collective-permute-start.31) | collective-permute-done | bytes 393248 | tf_op jit(solution)/shard_map/ppermute | solution.py:36
  103.1 4.4 %collective-permute-start.41 = (bf16[192,1024]{1,0:T(8,128)(2,1)S(1)}, bf16[192,1024]{1,0:T(8,128)(2,1)S(1)}, u32[]{:S(2)}, u32[]{:S(2)}) collective-permute-start(bf16[192,1024]{1,0:T(8,128)(2,1)S(1)} %get-tuple-element.51), channel_id=1, source_target_pairs={{0,1},{3,2},{4,5},{7,6},{8,9},{11,10},{12,13},{15,14},{16,17},{19,... | collective-permute-start | bytes 1179656 | tf_op jit(solution)/shard_map/ppermute | solution.py:36
  107.6 20.8 %collective-permute-done.36 = bf16[192,1024]{1,0:T(8,128)(2,1)S(1)} collective-permute-done((bf16[192,1024]{1,0:T(8,128)(2,1)S(1)}, bf16[192,1024]{1,0:T(8,128)(2,1)S(1)}, u32[]{:S(2)}, u32[]{:S(2)}) %collective-permute-start.36) | collective-permute-done | bytes 393248 | tf_op jit(solution)/shard_map/ppermute | solution.py:36
  128.4 4.4 %collective-permute-start.17 = (bf16[192,2048]{1,0:T(8,128)(2,1)S(1)}, bf16[192,2048]{1,0:T(8,128)(2,1)S(1)}, u32[]{:S(2)}, u32[]{:S(2)}) collective-permute-start(bf16[192,2048]{1,0:T(8,128)(2,1)S(1)} %get-tuple-element.49), channel_id=1, source_target_pairs={{0,1},{3,2},{4,5},{7,6},{8,9},{11,10},{12,13},{15,14},{16,17},{19,... | collective-permute-start | bytes 2359304 | tf_op jit(solution)/shard_map/ppermute | solution.py:36
  132.9 3.9 %collective-permute-done.41 = bf16[192,1024]{1,0:T(8,128)(2,1)S(1)} collective-permute-done((bf16[192,1024]{1,0:T(8,128)(2,1)S(1)}, bf16[192,1024]{1,0:T(8,128)(2,1)S(1)}, u32[]{:S(2)}, u32[]{:S(2)}) %collective-permute-start.41) | collective-permute-done | bytes 393248 | tf_op jit(solution)/shard_map/ppermute | solution.py:36
  140.3 10.6 %collective-permute-done.17 = bf16[192,2048]{1,0:T(8,128)(2,1)S(1)} collective-permute-done((bf16[192,2048]{1,0:T(8,128)(2,1)S(1)}, bf16[192,2048]{1,0:T(8,128)(2,1)S(1)}, u32[]{:S(2)}, u32[]{:S(2)}) %collective-permute-start.17) | collective-permute-done | bytes 786464 | tf_op jit(solution)/shard_map/ppermute | solution.py:36
  164.6 75.7 %collective-permute-done.5 = bf16[192,1024]{1,0:T(8,128)(2,1)S(1)} collective-permute-done((bf16[192,1024]{1,0:T(8,128)(2,1)S(1)}, bf16[192,1024]{1,0:T(8,128)(2,1)S(1)}, u32[]{:S(2)}, u32[]{:S(2)}) %collective-permute-start.5) | collective-permute-done | bytes 393248 | tf_op jit(solution)/shard_map/ppermute | solution.py:46
  242.5 23.2 %collective-permute-done.9 = bf16[192,1024]{1,0:T(8,128)(2,1)S(1)} collective-permute-done((bf16[192,1024]{1,0:T(8,128)(2,1)S(1)}, bf16[192,1024]{1,0:T(8,128)(2,1)S(1)}, u32[]{:S(2)}, u32[]{:S(2)}) %collective-permute-start.9) | collective-permute-done | bytes 393248 | tf_op jit(solution)/shard_map/ppermute | solution.py:46
  267.7 6.3 %collective-permute-done.14 = bf16[192,1024]{1,0:T(8,128)(2,1)S(1)} collective-permute-done((bf16[192,1024]{1,0:T(8,128)(2,1)S(1)}, bf16[192,1024]{1,0:T(8,128)(2,1)S(1)}, u32[]{:S(2)}, u32[]{:S(2)}) %collective-permute-start.14) | collective-permute-done | bytes 393248 | tf_op jit(solution)/shard_map/ppermute | solution.py:46
  274.9 7.6 %collective-permute-done.19 = bf16[192,1024]{1,0:T(8,128)(2,1)S(1)} collective-permute-done((bf16[192,1024]{1,0:T(8,128)(2,1)S(1)}, bf16[192,1024]{1,0:T(8,128)(2,1)S(1)}, u32[]{:S(2)}, u32[]{:S(2)}) %collective-permute-start.19) | collective-permute-done | bytes 393248 | tf_op jit(solution)/shard_map/ppermute | solution.py:46
  290.2 6.4 %collective-permute-done.20 = bf16[192,896]{1,0:T(8,128)(2,1)S(1)} collective-permute-done((bf16[192,896]{1,0:T(8,128)(2,1)S(1)}, bf16[192,896]{1,0:T(8,128)(2,1)S(1)}, u32[]{:S(2)}, u32[]{:S(2)}) %collective-permute-start.20) | collective-permute-done | bytes 344096 | tf_op jit(solution)/shard_map/ppermute | solution.py:28
  302.6 17.9 %collective-permute-done.38 = bf16[192,2048]{1,0:T(8,128)(2,1)S(1)} collective-permute-done((bf16[192,2048]{1,0:T(8,128)(2,1)S(1)}, bf16[192,2048]{1,0:T(8,128)(2,1)S(1)}, u32[]{:S(2)}, u32[]{:S(2)}) %collective-permute-start.38) | collective-permute-done | bytes 786464 | tf_op jit(solution)/shard_map/ppermute | solution.py:46
  323.6 8.2 %collective-permute-done.43 = bf16[192,2048]{1,0:T(8,128)(2,1)S(1)} collective-permute-done((bf16[192,2048]{1,0:T(8,128)(2,1)S(1)}, bf16[192,2048]{1,0:T(8,128)(2,1)S(1)}, u32[]{:S(2)}, u32[]{:S(2)}) %collective-permute-start.43) | collective-permute-done | bytes 786464 | tf_op jit(solution)/shard_map/ppermute | solution.py:46
  332.2 9.3 %collective-permute-start.39 = (bf16[192,896]{1,0:T(8,128)(2,1)S(1)}, bf16[192,896]{1,0:T(8,128)(2,1)S(1)}, u32[]{:S(2)}, u32[]{:S(2)}) collective-permute-start(bf16[192,896]{1,0:T(8,128)(2,1)S(1)} %convolution_convert_fusion.3), channel_id=1, source_target_pairs={{0,8},{4,12},{8,0},{12,4},{1,9},{5,13},{9,1},{13,5},{2,10},{6,14},... | collective-permute-start | bytes 1032200 | tf_op jit(solution)/shard_map/ppermute | solution.py:28
  350.2 8.7 %collective-permute-done.44 = bf16[192,896]{1,0:T(8,128)(2,1)S(1)} collective-permute-done((bf16[192,896]{1,0:T(8,128)(2,1)S(1)}, bf16[192,896]{1,0:T(8,128)(2,1)S(1)}, u32[]{:S(2)}, u32[]{:S(2)}) %collective-permute-start.44) | collective-permute-done | bytes 344096 | tf_op jit(solution)/shard_map/ppermute | solution.py:28
  364.7 5.8 %collective-permute-done.45 = bf16[128,896]{1,0:T(8,128)(2,1)S(1)} collective-permute-done((bf16[128,896]{1,0:T(8,128)(2,1)S(1)}, bf16[128,896]{1,0:T(8,128)(2,1)S(1)}, u32[]{:S(2)}, u32[]{:S(2)}) %collective-permute-start.45) | collective-permute-done | bytes 229408 | tf_op jit(solution)/shard_map/ppermute | solution.py:28
  370.6 10.9 %collective-permute-done.46 = bf16[128,896]{1,0:T(8,128)(2,1)S(1)} collective-permute-done((bf16[128,896]{1,0:T(8,128)(2,1)S(1)}, bf16[128,896]{1,0:T(8,128)(2,1)S(1)}, u32[]{:S(2)}, u32[]{:S(2)}) %collective-permute-start.46) | collective-permute-done | bytes 229408 | tf_op jit(solution)/shard_map/ppermute | solution.py:28
  (170 shorter events, 91.0 us)
Async XLA Ops:
  3.0 34.4 %collective-permute-start = (bf16[128,896]{1,0:T(8,128)(2,1)}, bf16[128,896]{1,0:T(8,128)(2,1)}, u32[]{:S(2)}, u32[]{:S(2)}) collective-permute-start(bf16[128,896]{1,0:T(8,128)(2,1)} %get-tuple-element.38), channel_id=1, source_target_pairs={{0,1},{1,0},{2,3},{3,2},{4,5},{5,4},{6,7},{7,6},{8,9},{9,8},{10,11... | collective-permute-start | bytes 688136 | tf_op jit(solution)/shard_map/ppermute | solution.py:28
  6.0 38.1 %collective-permute-start.1 = (bf16[128,896]{1,0:T(8,128)(2,1)}, bf16[128,896]{1,0:T(8,128)(2,1)}, u32[]{:S(2)}, u32[]{:S(2)}) collective-permute-start(bf16[128,896]{1,0:T(8,128)(2,1)} %get-tuple-element.40), channel_id=1, source_target_pairs={{0,2},{1,3},{2,0},{3,1},{4,6},{5,7},{6,4},{7,5},{8,10},{9,11},{10,... | collective-permute-start | bytes 688136 | tf_op jit(solution)/shard_map/ppermute | solution.py:28
  8.6 35.5 %collective-permute-start.2 = (bf16[128,896]{1,0:T(8,128)(2,1)S(1)}, bf16[128,896]{1,0:T(8,128)(2,1)}, u32[]{:S(2)}, u32[]{:S(2)}) collective-permute-start(bf16[128,896]{1,0:T(8,128)(2,1)S(1)} %get-tuple-element.39), channel_id=1, source_target_pairs={{0,3},{1,2},{2,1},{3,0},{4,7},{5,6},{6,5},{7,4},{8,11},{9,10},{10,... | collective-permute-start | bytes 688136 | tf_op jit(solution)/shard_map/ppermute | solution.py:28
  8.9 40.2 %collective-permute-start.24 = (bf16[128,896]{1,0:T(8,128)(2,1)S(1)}, bf16[128,896]{1,0:T(8,128)(2,1)}, u32[]{:S(2)}, u32[]{:S(2)}) collective-permute-start(bf16[128,896]{1,0:T(8,128)(2,1)S(1)} %get-tuple-element.32), channel_id=1, source_target_pairs={{0,1},{1,0},{2,3},{3,2},{4,5},{5,4},{6,7},{7,6},{8,9},{9,8},{10,11... | collective-permute-start | bytes 688136 | tf_op jit(solution)/shard_map/ppermute | solution.py:28
  9.9 39.3 %collective-permute-start.25 = (bf16[128,896]{1,0:T(8,128)(2,1)S(1)}, bf16[128,896]{1,0:T(8,128)(2,1)}, u32[]{:S(2)}, u32[]{:S(2)}) collective-permute-start(bf16[128,896]{1,0:T(8,128)(2,1)S(1)} %get-tuple-element.31), channel_id=1, source_target_pairs={{0,2},{1,3},{2,0},{3,1},{4,6},{5,7},{6,4},{7,5},{8,10},{9,11},{10,... | collective-permute-start | bytes 688136 | tf_op jit(solution)/shard_map/ppermute | solution.py:28
  47.4 90.1 %collective-permute-start.3 = (bf16[192,2048]{1,0:T(8,128)(2,1)S(1)}, bf16[192,2048]{1,0:T(8,128)(2,1)S(1)}, u32[]{:S(2)}, u32[]{:S(2)}) collective-permute-start(bf16[192,2048]{1,0:T(8,128)(2,1)S(1)} %get-tuple-element.61), channel_id=1, source_target_pairs={{0,1},{3,2},{4,5},{7,6},{8,9},{11,10},{12,13},{15,14},{16,17},{19,... | collective-permute-start | bytes 2359304 | tf_op jit(solution)/shard_map/ppermute | solution.py:36
  53.5 32.8 %collective-permute-start.27 = (bf16[192,1024]{1,0:T(8,128)(2,1)S(1)}, bf16[192,1024]{1,0:T(8,128)(2,1)S(1)}, u32[]{:S(2)}, u32[]{:S(2)}) collective-permute-start(bf16[192,1024]{1,0:T(8,128)(2,1)S(1)} %get-tuple-element.63), channel_id=1, source_target_pairs={{0,1},{3,2},{4,5},{7,6},{8,9},{11,10},{12,13},{15,14},{16,17},{19,... | collective-permute-start | bytes 1179656 | tf_op jit(solution)/shard_map/ppermute | solution.py:36
  71.6 66.8 %collective-permute-start.7 = (bf16[192,2048]{1,0:T(8,128)(2,1)S(1)}, bf16[192,2048]{1,0:T(8,128)(2,1)S(1)}, u32[]{:S(2)}, u32[]{:S(2)}) collective-permute-start(bf16[192,2048]{1,0:T(8,128)(2,1)S(1)} %get-tuple-element.57), channel_id=1, source_target_pairs={{0,1},{3,2},{4,5},{7,6},{8,9},{11,10},{12,13},{15,14},{16,17},{19,... | collective-permute-start | bytes 2359304 | tf_op jit(solution)/shard_map/ppermute | solution.py:36
  77.3 25.7 %collective-permute-start.31 = (bf16[192,1024]{1,0:T(8,128)(2,1)S(1)}, bf16[192,1024]{1,0:T(8,128)(2,1)S(1)}, u32[]{:S(2)}, u32[]{:S(2)}) collective-permute-start(bf16[192,1024]{1,0:T(8,128)(2,1)S(1)} %get-tuple-element.59), channel_id=1, source_target_pairs={{0,1},{3,2},{4,5},{7,6},{8,9},{11,10},{12,13},{15,14},{16,17},{19,... | collective-permute-start | bytes 1179656 | tf_op jit(solution)/shard_map/ppermute | solution.py:36
  83.5 55.8 %collective-permute-start.12 = (bf16[192,2048]{1,0:T(8,128)(2,1)S(1)}, bf16[192,2048]{1,0:T(8,128)(2,1)S(1)}, u32[]{:S(2)}, u32[]{:S(2)}) collective-permute-start(bf16[192,2048]{1,0:T(8,128)(2,1)S(1)} %get-tuple-element.53), channel_id=1, source_target_pairs={{0,1},{3,2},{4,5},{7,6},{8,9},{11,10},{12,13},{15,14},{16,17},{19,... | collective-permute-start | bytes 2359304 | tf_op jit(solution)/shard_map/ppermute | solution.py:36
  86.4 42.0 %collective-permute-start.36 = (bf16[192,1024]{1,0:T(8,128)(2,1)S(1)}, bf16[192,1024]{1,0:T(8,128)(2,1)S(1)}, u32[]{:S(2)}, u32[]{:S(2)}) collective-permute-start(bf16[192,1024]{1,0:T(8,128)(2,1)S(1)} %get-tuple-element.55), channel_id=1, source_target_pairs={{0,1},{3,2},{4,5},{7,6},{8,9},{11,10},{12,13},{15,14},{16,17},{19,... | collective-permute-start | bytes 1179656 | tf_op jit(solution)/shard_map/ppermute | solution.py:36
  103.1 33.7 %collective-permute-start.41 = (bf16[192,1024]{1,0:T(8,128)(2,1)S(1)}, bf16[192,1024]{1,0:T(8,128)(2,1)S(1)}, u32[]{:S(2)}, u32[]{:S(2)}) collective-permute-start(bf16[192,1024]{1,0:T(8,128)(2,1)S(1)} %get-tuple-element.51), channel_id=1, source_target_pairs={{0,1},{3,2},{4,5},{7,6},{8,9},{11,10},{12,13},{15,14},{16,17},{19,... | collective-permute-start | bytes 1179656 | tf_op jit(solution)/shard_map/ppermute | solution.py:36
  128.4 22.5 %collective-permute-start.17 = (bf16[192,2048]{1,0:T(8,128)(2,1)S(1)}, bf16[192,2048]{1,0:T(8,128)(2,1)S(1)}, u32[]{:S(2)}, u32[]{:S(2)}) collective-permute-start(bf16[192,2048]{1,0:T(8,128)(2,1)S(1)} %get-tuple-element.49), channel_id=1, source_target_pairs={{0,1},{3,2},{4,5},{7,6},{8,9},{11,10},{12,13},{15,14},{16,17},{19,... | collective-permute-start | bytes 2359304 | tf_op jit(solution)/shard_map/ppermute | solution.py:36
  155.4 84.9 %collective-permute-start.5 = (bf16[192,1024]{1,0:T(8,128)(2,1)S(1)}, bf16[192,1024]{1,0:T(8,128)(2,1)S(1)}, u32[]{:S(2)}, u32[]{:S(2)}) collective-permute-start(bf16[192,1024]{1,0:T(8,128)(2,1)S(1)} %get-tuple-element.13), channel_id=1, source_target_pairs={{1,0},{2,3},{5,4},{6,7},{9,8},{10,11},{13,12},{14,15},{17,16},{18,... | collective-permute-start | bytes 1179656 | tf_op jit(solution)/shard_map/ppermute | solution.py:46
  157.1 129.1 %collective-permute-start.29 = (bf16[192,2048]{1,0:T(8,128)(2,1)S(1)}, bf16[192,2048]{1,0:T(8,128)(2,1)S(1)}, u32[]{:S(2)}, u32[]{:S(2)}) collective-permute-start(bf16[192,2048]{1,0:T(8,128)(2,1)S(1)} %pad_maximum_fusion.2), channel_id=1, source_target_pairs={{1,0},{2,3},{5,4},{6,7},{9,8},{10,11},{13,12},{14,15},{17,16},{18,... | collective-permute-start | bytes 2359304 | tf_op jit(solution)/shard_map/ppermute | solution.py:46
  159.0 106.6 %collective-permute-start.9 = (bf16[192,1024]{1,0:T(8,128)(2,1)S(1)}, bf16[192,1024]{1,0:T(8,128)(2,1)S(1)}, u32[]{:S(2)}, u32[]{:S(2)}) collective-permute-start(bf16[192,1024]{1,0:T(8,128)(2,1)S(1)} %get-tuple-element.14), channel_id=1, source_target_pairs={{1,0},{2,3},{5,4},{6,7},{9,8},{10,11},{13,12},{14,15},{17,16},{18,... | collective-permute-start | bytes 1179656 | tf_op jit(solution)/shard_map/ppermute | solution.py:46
  160.9 113.2 %collective-permute-start.14 = (bf16[192,1024]{1,0:T(8,128)(2,1)S(1)}, bf16[192,1024]{1,0:T(8,128)(2,1)S(1)}, u32[]{:S(2)}, u32[]{:S(2)}) collective-permute-start(bf16[192,1024]{1,0:T(8,128)(2,1)S(1)} %get-tuple-element.15), channel_id=1, source_target_pairs={{1,0},{2,3},{5,4},{6,7},{9,8},{10,11},{13,12},{14,15},{17,16},{18,... | collective-permute-start | bytes 1179656 | tf_op jit(solution)/shard_map/ppermute | solution.py:46
  163.1 119.4 %collective-permute-start.19 = (bf16[192,1024]{1,0:T(8,128)(2,1)S(1)}, bf16[192,1024]{1,0:T(8,128)(2,1)S(1)}, u32[]{:S(2)}, u32[]{:S(2)}) collective-permute-start(bf16[192,1024]{1,0:T(8,128)(2,1)S(1)} %get-tuple-element.16), channel_id=1, source_target_pairs={{1,0},{2,3},{5,4},{6,7},{9,8},{10,11},{13,12},{14,15},{17,16},{18,... | collective-permute-start | bytes 1179656 | tf_op jit(solution)/shard_map/ppermute | solution.py:46
  240.3 58.6 %collective-permute-start.33 = (bf16[192,2048]{1,0:T(8,128)(2,1)S(1)}, bf16[192,2048]{1,0:T(8,128)(2,1)S(1)}, u32[]{:S(2)}, u32[]{:S(2)}) collective-permute-start(bf16[192,2048]{1,0:T(8,128)(2,1)S(1)} %pad_maximum_fusion.3), channel_id=1, source_target_pairs={{1,0},{2,3},{5,4},{6,7},{9,8},{10,11},{13,12},{14,15},{17,16},{18,... | collective-permute-start | bytes 2359304 | tf_op jit(solution)/shard_map/ppermute | solution.py:46
  265.6 54.9 %collective-permute-start.38 = (bf16[192,2048]{1,0:T(8,128)(2,1)S(1)}, bf16[192,2048]{1,0:T(8,128)(2,1)S(1)}, u32[]{:S(2)}, u32[]{:S(2)}) collective-permute-start(bf16[192,2048]{1,0:T(8,128)(2,1)S(1)} %pad_maximum_fusion.4), channel_id=1, source_target_pairs={{1,0},{2,3},{5,4},{6,7},{9,8},{10,11},{13,12},{14,15},{17,16},{18,... | collective-permute-start | bytes 2359304 | tf_op jit(solution)/shard_map/ppermute | solution.py:46
  287.9 43.9 %collective-permute-start.43 = (bf16[192,2048]{1,0:T(8,128)(2,1)S(1)}, bf16[192,2048]{1,0:T(8,128)(2,1)S(1)}, u32[]{:S(2)}, u32[]{:S(2)}) collective-permute-start(bf16[192,2048]{1,0:T(8,128)(2,1)S(1)} %pad_maximum_fusion.5), channel_id=1, source_target_pairs={{1,0},{2,3},{5,4},{6,7},{9,8},{10,11},{13,12},{14,15},{17,16},{18,... | collective-permute-start | bytes 2359304 | tf_op jit(solution)/shard_map/ppermute | solution.py:46
  297.9 50.8 %collective-permute-start.21 = (bf16[128,896]{1,0:T(8,128)(2,1)S(1)}, bf16[128,896]{1,0:T(8,128)(2,1)S(1)}, u32[]{:S(2)}, u32[]{:S(2)}) collective-permute-start(bf16[128,896]{1,0:T(8,128)(2,1)S(1)} %get-tuple-element.35), channel_id=1, source_target_pairs={{0,3},{1,2},{2,1},{3,0},{4,7},{5,6},{6,5},{7,4},{8,11},{9,10},{10,... | collective-permute-start | bytes 688136 | tf_op jit(solution)/shard_map/ppermute | solution.py:28
  298.8 50.1 %collective-permute-start.22 = (bf16[128,896]{1,0:T(8,128)(2,1)S(1)}, bf16[128,896]{1,0:T(8,128)(2,1)S(1)}, u32[]{:S(2)}, u32[]{:S(2)}) collective-permute-start(bf16[128,896]{1,0:T(8,128)(2,1)S(1)} %get-tuple-element.34), channel_id=1, source_target_pairs={{0,2},{1,3},{2,0},{3,1},{4,6},{5,7},{6,4},{7,5},{8,10},{9,11},{10,... | collective-permute-start | bytes 688136 | tf_op jit(solution)/shard_map/ppermute | solution.py:28
  298.9 62.7 %collective-permute-start.23 = (bf16[128,896]{1,0:T(8,128)(2,1)S(1)}, bf16[128,896]{1,0:T(8,128)(2,1)S(1)}, u32[]{:S(2)}, u32[]{:S(2)}) collective-permute-start(bf16[128,896]{1,0:T(8,128)(2,1)S(1)} %get-tuple-element.33), channel_id=1, source_target_pairs={{0,1},{1,0},{2,3},{3,2},{4,5},{5,4},{6,7},{7,6},{8,9},{9,8},{10,11... | collective-permute-start | bytes 688136 | tf_op jit(solution)/shard_map/ppermute | solution.py:28
  (33 other events, 425.6 us)

commit v2 on v1

v2 whole, which is shorter than its diff:
```python
import jax
import jax.numpy as jnp
from jax import lax
from jax.sharding import PartitionSpec as P

F32 = jnp.float32
BF16 = jnp.bfloat16
GROUPS = 4


def route_places(routes, experts, capacity):
    flat_ids = routes.reshape(-1)
    onehot = (flat_ids[:, None] == jnp.arange(experts, dtype=jnp.int32)[None, :]).astype(jnp.int32)
    before = jnp.cumsum(onehot, axis=0) - onehot
    slot_pos = jnp.sum(before * onehot, axis=1)
    return flat_ids * capacity + slot_pos


def across(left, right):
    return lax.dot_general(left, right, (((1,), (1,)), ((), ())), preferred_element_type=F32)


def over_rows(left, right):
    return lax.dot_general(left, right, (((0,), (0,)), ((), ())), preferred_element_type=F32)


def joined(values, axis=0):
    return values[0] if len(values) == 1 else jnp.concatenate(values, axis=axis)


class Queue:
    def __init__(self, axis, depth):
        self.axis, self.depth, self.arrived = axis, depth, []

    def send(self, value, pairs):
        if self.depth and len(self.arrived) >= self.depth:
            value, _ = lax.optimization_barrier((value, self.arrived[-self.depth]))
        got = lax.ppermute(value, self.axis, pairs)
        self.arrived.append(got)
        return got

    def swap(self, value, distance):
        count = lax.axis_size(self.axis)
        return self.send(value, [(i, i ^ distance) for i in range(count)])


class Line:
    def __init__(self, axis):
        self.count = lax.axis_size(axis)
        self.inward, self.middle, self.outward = Queue(axis, 1), Queue(axis, 2), Queue(axis, 1)

    def __call__(self, own):
        count, mid = self.count, self.count // 2
        total = own
        for hop in range(mid - 1):
            pairs = [(hop, hop + 1), (count - 1 - hop, count - 2 - hop)]
            total = total + self.inward.send(total.astype(BF16), pairs).astype(F32)
        got = self.middle.send(total.astype(BF16), [(mid - 1, mid), (mid, mid - 1)])
        for hop in reversed(range(mid - 1)):
            pairs = [(hop + 1, hop), (count - 2 - hop, count - 1 - hop)]
            got = got + self.outward.send((own + got.astype(F32)).astype(BF16), pairs)
        return total + got.astype(F32)


def shards(tokens, routes, gates, gate_weight, up_weight, down_weight, cotangent):
    n_exp = lax.axis_size("expert") * gate_weight.shape[0]
    n_dp = lax.axis_size("dp")
    me = lax.axis_index("expert")
    here = lax.axis_index("dp")
    tok_count, topk = routes.shape
    width = tokens.shape[1]
    part = width // n_dp
    hidden_units = gate_weight.shape[2]
    capacity = 3 * tok_count * topk // (2 * n_exp)
    chunk = n_dp * capacity
    per_group = n_exp // GROUPS
    w_gate, w_up, w_down = gate_weight[0], up_weight[0], down_weight[0]
    w_both = jnp.concatenate([w_gate, w_up], axis=1)
    distances = list(range(n_dp - 1, 0, -1))

    codes = lax.all_gather(route_places(routes, n_exp, capacity), "dp")
    blocks = here ^ jnp.arange(n_dp, dtype=jnp.int32)
    codes = codes[blocks]
    places = ((codes // capacity) ^ me) * chunk + blocks[:, None] * capacity + codes % capacity
    places = places.reshape(-1)
    select = (jnp.arange(n_exp * chunk, dtype=jnp.int32)[:, None] == places[None, :]).astype(BF16)

    features, experts = Queue("dp", n_dp - 1), Queue("expert", 0)

    def by_features(value):
        def columns(distance):
            return lax.dynamic_slice(value, (0, (here ^ distance) * part), (tok_count, part))

        got = {k: features.swap(columns(k), k) for k in distances}
        return jnp.concatenate([columns(0)] + [got[k] for k in range(1, n_dp)], axis=0)

    def dispatch(gathered):
        rows = jnp.dot(select, gathered, preferred_element_type=F32).astype(BF16)
        rows = rows.reshape(n_exp, chunk, part)
        rows = [rows[0]] + [experts.swap(rows[k], k) for k in range(1, n_exp)]
        return [joined(rows[g * per_group : (g + 1) * per_group]) for g in range(GROUPS)]

    rows = dispatch(by_features(tokens))
    grads = dispatch(by_features((gates * cotangent.astype(F32)).astype(BF16)))

    line = Line("dp")
    pre = [None] * GROUPS
    hid = [None] * GROUPS

    def first(g):
        pre[g] = line(jnp.dot(rows[g], w_both, preferred_element_type=F32))

    def second(g):
        hid[g] = line(jnp.dot(grads[g], w_down, preferred_element_type=F32))

    for step, g in ((first, 0), (second, 0), (first, 1), (second, 1), (first, 2), (first, 3), (second, 2), (second, 3)):
        step(g)

    hidden, both = [], []
    out, back = [], []
    for g in range(GROUPS):
        pre_gate, pre_up, hidden_grad = pre[g][:, :hidden_units], pre[g][:, hidden_units:], hid[g]
        sig = jax.nn.sigmoid(pre_gate)
        active = pre_gate * sig
        hidden.append((active * pre_up).astype(BF16))
        pg_grad = (hidden_grad * pre_up * sig * (1.0 + pre_gate * (1.0 - sig))).astype(BF16)
        pu_grad = (hidden_grad * active).astype(BF16)
        both.append(jnp.concatenate([pg_grad, pu_grad], axis=1))

    def returned(values, g):
        values = values.astype(BF16).reshape(per_group, chunk, part)
        values = [values[i] if k == 0 else experts.swap(values[i], k) for i, k in enumerate(range(g * per_group, (g + 1) * per_group))]
        return joined(values)

    for g in range(GROUPS):
        out.append(returned(across(hidden[g], w_down), g))
    for g in range(GROUPS):
        back.append(returned(across(both[g], w_both), g))

    def give_back(values, scale):
        picked = over_rows(select, jnp.concatenate(values, axis=0)).astype(BF16).reshape(n_dp, tok_count, part)
        result = jnp.zeros((tok_count, width), BF16)
        for k in [0] + distances:
            piece = picked[k] if k == 0 else features.swap(picked[k], k)
            if scale is not None:
                piece = (piece.astype(F32) * scale).astype(BF16)
            result = lax.dynamic_update_slice(result, piece, (0, (here ^ k) * part))
        return result

    mixed = give_back(out, gates)
    token_grad = give_back(back, None)
    all_rows, all_grads = jnp.concatenate(rows, axis=0), jnp.concatenate(grads, axis=0)
    all_both = over_rows(all_rows, jnp.concatenate(both, axis=0)).astype(BF16)
    down_grad = over_rows(all_grads, jnp.concatenate(hidden, axis=0)).astype(BF16)
    return (mixed, token_grad, all_both[:, :hidden_units][None], all_both[:, hidden_units:][None], down_grad[None])


def solution(mesh):
    rows = P(("groups", "expert", "dp"), None)
    weights = P("expert", "dp", None)
    grads = P(("groups", "expert"), "dp", None)
    return jax.shard_map(
        shards,
        mesh=mesh,
        in_specs=(rows, rows, rows, weights, weights, weights, rows),
        out_specs=(rows, rows, grads, grads, grads),
        check_vma=False,
    )
```

time: 383 us -> 294 us (0.77)
  waiting for transfers between devices: 231 us -> 137 us
  starting transfers between devices: 84.6 us -> 94.4 us
  blocking collectives: 22.8 us -> 17.5 us
    ppermute x48, waiting for transfers between devices: 231 us -> 137 us  [send(): got = lax.ppermute(value, self.axis, pairs)]
    ppermute x48, starting transfers between devices: 84.6 us -> 94.4 us  [send(): got = lax.ppermute(value, self.axis, pairs)]
    all_gather x1, blocking collectives: 22.8 us -> 17.5 us  [shards(): codes = lax.all_gather(route_places(routes, n_exp, capacity), 'dp')]
    dot_general x5 -> x4, matrix products: 10.7 us -> 7.98 us  [over_rows(): lax.dot_general(left, right, (((0,), (0,)), ((), ())), preferred_element_...]
  transfers between devices with their start and end apart: 48 -> 48, of which waited for: 19 -> 19; matrix products, arithmetic and copies ran while one was open for 10% -> 12% of each run, Pallas kernels for 0% -> 0%
where the time goes in v2:
time: 294 us; the launch traced here: 291 us
  waiting for transfers between devices  137 us (47%)
  starting transfers between devices  94.4 us (32%)
  matrix products  26.4 us (9%)
  blocking collectives  17.5 us (6%)
  other arithmetic  7.69 us (3%)
  local copies, waits for them, and re-layouts  6.74 us (2%)
    ppermute x48, waiting for transfers between devices, send(): got = lax.ppermute(value, self.axis, pairs)  137 us
    ppermute x48, starting transfers between devices, send(): got = lax.ppermute(value, self.axis, pairs)  94.4 us
    all_gather x1, blocking collectives, shards(): codes = lax.all_gather(route_places(routes, n_exp, capacity), 'dp')  17.5 us
    dot_general x8, matrix products, across(): lax.dot_general(left, right, (((1,), (1,)), ((), ())), preferred_element_...  8.69 us
    dot_general x4, matrix products, over_rows(): lax.dot_general(left, right, (((0,), (0,)), ((), ())), preferred_element_...  7.98 us
  transfers between devices with their start and end apart: 48, of which 19 were waited for; matrix products, arithmetic and copies ran while one was open for 12% of the time, Pallas kernels for 0%

profile of v2, /device:TPU:0, one launch (start us, length us, event | category | flops | bytes accessed | tf_op | source)
XLA Modules:
  0.0 290.8 jit_solution(14581879769434517701)
XLA Ops:
  9.4 17.5 %all-gather = s32[4,1,128]{2,1,0:T(1,128)S(1)} all-gather(s32[1,1,128]{2,1,0:T(1,128)S(1)} %fusion.137), channel_id=1, replica_groups=mesh['groups'=2,'expert'=4,'dp'=4] {'dp'}, dimensions={0}, use_global_device_ids=true | all-gather | bytes 2560 | tf_op jit(solution)/shard_map/all_gather | solution.py:81
  31.0 6.0 %collective-permute-start.3 = (bf16[192,2048]{1,0:T(8,128)(2,1)S(1)}, bf16[192,2048]{1,0:T(8,128)(2,1)S(1)}, u32[]{:S(2)}, u32[]{:S(2)}) collective-permute-start(bf16[192,2048]{1,0:T(8,128)(2,1)S(1)} %get-tuple-element.111), channel_id=1, source_target_pairs={{0,1},{3,2},{4,5},{7,6},{8,9},{11,10},{12,13},{15,14},{16,17},{19,... | collective-permute-start | bytes 2359304 | tf_op jit(solution)/shard_map/ppermute | solution.py:38
  37.1 3.7 %collective-permute-start.8 = (bf16[128,896]{1,0:T(8,128)(2,1)S(1)}, bf16[128,896]{1,0:T(8,128)(2,1)S(1)}, u32[]{:S(2)}, u32[]{:S(2)}) collective-permute-start(bf16[128,896]{1,0:T(8,128)(2,1)S(1)} %get-tuple-element.35), channel_id=1, source_target_pairs={{0,2},{1,3},{2,0},{3,1},{4,6},{5,7},{6,4},{7,5},{8,10},{9,11},{10,... | collective-permute-start | bytes 688136 | tf_op jit(solution)/shard_map/ppermute | solution.py:38
  41.6 18.2 %collective-permute-done.7 = bf16[128,896]{1,0:T(8,128)(2,1)S(1)} collective-permute-done((bf16[128,896]{1,0:T(8,128)(2,1)S(1)}, bf16[128,896]{1,0:T(8,128)(2,1)S(1)}, u32[]{:S(2)}, u32[]{:S(2)}) %collective-permute-start.7) | collective-permute-done | bytes 229408 | tf_op jit(solution)/shard_map/ppermute | solution.py:38
  64.3 6.1 %collective-permute-done.9 = bf16[128,896]{1,0:T(8,128)(2,1)S(1)} collective-permute-done((bf16[128,896]{1,0:T(8,128)(2,1)S(1)}, bf16[128,896]{1,0:T(8,128)(2,1)S(1)}, u32[]{:S(2)}, u32[]{:S(2)}) %collective-permute-start.9) | collective-permute-done | bytes 229408 | tf_op jit(solution)/shard_map/ppermute | solution.py:38
  78.7 5.8 %collective-permute-start.10 = (bf16[192,1024]{1,0:T(8,128)(2,1)S(1)}, bf16[192,1024]{1,0:T(8,128)(2,1)S(1)}, u32[]{:S(2)}, u32[]{:S(2)}) collective-permute-start(bf16[192,1024]{1,0:T(8,128)(2,1)S(1)} %get-tuple-element.37), channel_id=1, source_target_pairs={{0,1},{3,2},{4,5},{7,6},{8,9},{11,10},{12,13},{15,14},{16,17},{19,... | collective-permute-start | bytes 1179656 | tf_op jit(solution)/shard_map/ppermute | solution.py:38
  85.1 4.5 %collective-permute-done.40 = bf16[192,896]{1,0:T(8,128)(2,1)S(1)} collective-permute-done((bf16[192,896]{1,0:T(8,128)(2,1)S(1)}, bf16[192,896]{1,0:T(8,128)(2,1)S(1)}, u32[]{:S(2)}, u32[]{:S(2)}) %collective-permute-start.40) | collective-permute-done | bytes 344096 | tf_op jit(solution)/shard_map/ppermute | solution.py:38
  94.2 7.0 %collective-permute-start.11 = (bf16[192,2048]{1,0:T(8,128)(2,1)S(1)}, bf16[192,2048]{1,0:T(8,128)(2,1)S(1)}, u32[]{:S(2)}, u32[]{:S(2)}) collective-permute-start(bf16[192,2048]{1,0:T(8,128)(2,1)S(1)} %get-tuple-element.38), channel_id=1, source_target_pairs={{0,1},{3,2},{4,5},{7,6},{8,9},{11,10},{12,13},{15,14},{16,17},{19,... | collective-permute-start | bytes 2359304 | tf_op jit(solution)/shard_map/ppermute | solution.py:38
  102.9 13.9 %collective-permute-done.11 = bf16[192,2048]{1,0:T(8,128)(2,1)S(1)} collective-permute-done((bf16[192,2048]{1,0:T(8,128)(2,1)S(1)}, bf16[192,2048]{1,0:T(8,128)(2,1)S(1)}, u32[]{:S(2)}, u32[]{:S(2)}) %collective-permute-start.11) | collective-permute-done | bytes 786464 | tf_op jit(solution)/shard_map/ppermute | solution.py:38
  116.9 4.4 %collective-permute-start.19 = (bf16[192,1024]{1,0:T(8,128)(2,1)S(1)}, bf16[192,1024]{1,0:T(8,128)(2,1)S(1)}, u32[]{:S(2)}, u32[]{:S(2)}) collective-permute-start(bf16[192,1024]{1,0:T(8,128)(2,1)S(1)} %get-tuple-element.42), channel_id=1, source_target_pairs={{0,1},{3,2},{4,5},{7,6},{8,9},{11,10},{12,13},{15,14},{16,17},{19,... | collective-permute-start | bytes 1179656 | tf_op jit(solution)/shard_map/ppermute | solution.py:38
  123.5 4.0 %collective-permute-done.19 = bf16[192,1024]{1,0:T(8,128)(2,1)S(1)} collective-permute-done((bf16[192,1024]{1,0:T(8,128)(2,1)S(1)}, bf16[192,1024]{1,0:T(8,128)(2,1)S(1)}, u32[]{:S(2)}, u32[]{:S(2)}) %collective-permute-start.19) | collective-permute-done | bytes 393248 | tf_op jit(solution)/shard_map/ppermute | solution.py:38
  128.3 7.8 %collective-permute-start.20 = (bf16[192,2048]{1,0:T(8,128)(2,1)S(1)}, bf16[192,2048]{1,0:T(8,128)(2,1)S(1)}, u32[]{:S(2)}, u32[]{:S(2)}) collective-permute-start(bf16[192,2048]{1,0:T(8,128)(2,1)S(1)} %get-tuple-element.43), channel_id=1, source_target_pairs={{0,1},{3,2},{4,5},{7,6},{8,9},{11,10},{12,13},{15,14},{16,17},{19,... | collective-permute-start | bytes 2359304 | tf_op jit(solution)/shard_map/ppermute | solution.py:38
  141.1 9.1 %collective-permute-done.20 = bf16[192,2048]{1,0:T(8,128)(2,1)S(1)} collective-permute-done((bf16[192,2048]{1,0:T(8,128)(2,1)S(1)}, bf16[192,2048]{1,0:T(8,128)(2,1)S(1)}, u32[]{:S(2)}, u32[]{:S(2)}) %collective-permute-start.20) | collective-permute-done | bytes 786464 | tf_op jit(solution)/shard_map/ppermute | solution.py:38
  150.3 4.4 %collective-permute-start.27 = (bf16[192,2048]{1,0:T(8,128)(2,1)S(1)}, bf16[192,2048]{1,0:T(8,128)(2,1)S(1)}, u32[]{:S(2)}, u32[]{:S(2)}) collective-permute-start(bf16[192,2048]{1,0:T(8,128)(2,1)S(1)} %get-tuple-element.48), channel_id=1, source_target_pairs={{0,1},{3,2},{4,5},{7,6},{8,9},{11,10},{12,13},{15,14},{16,17},{19,... | collective-permute-start | bytes 2359304 | tf_op jit(solution)/shard_map/ppermute | solution.py:38
  158.8 9.1 %collective-permute-done.27 = bf16[192,2048]{1,0:T(8,128)(2,1)S(1)} collective-permute-done((bf16[192,2048]{1,0:T(8,128)(2,1)S(1)}, bf16[192,2048]{1,0:T(8,128)(2,1)S(1)}, u32[]{:S(2)}, u32[]{:S(2)}) %collective-permute-start.27) | collective-permute-done | bytes 786464 | tf_op jit(solution)/shard_map/ppermute | solution.py:38
  168.0 4.4 %collective-permute-start.36 = (bf16[192,1024]{1,0:T(8,128)(2,1)S(1)}, bf16[192,1024]{1,0:T(8,128)(2,1)S(1)}, u32[]{:S(2)}, u32[]{:S(2)}) collective-permute-start(bf16[192,1024]{1,0:T(8,128)(2,1)S(1)} %get-tuple-element.54), channel_id=1, source_target_pairs={{0,1},{3,2},{4,5},{7,6},{8,9},{11,10},{12,13},{15,14},{16,17},{19,... | collective-permute-start | bytes 1179656 | tf_op jit(solution)/shard_map/ppermute | solution.py:38
  179.0 14.8 %collective-permute-start.41 = (bf16[192,1024]{1,0:T(8,128)(2,1)S(1)}, bf16[192,1024]{1,0:T(8,128)(2,1)S(1)}, u32[]{:S(2)}, u32[]{:S(2)}) collective-permute-start(bf16[192,1024]{1,0:T(8,128)(2,1)S(1)} %get-tuple-element.57), channel_id=1, source_target_pairs={{0,1},{3,2},{4,5},{7,6},{8,9},{11,10},{12,13},{15,14},{16,17},{19,... | collective-permute-start | bytes 1179656 | tf_op jit(solution)/shard_map/ppermute | solution.py:38
  195.4 3.8 %collective-permute-done.41 = bf16[192,1024]{1,0:T(8,128)(2,1)S(1)} collective-permute-done((bf16[192,1024]{1,0:T(8,128)(2,1)S(1)}, bf16[192,1024]{1,0:T(8,128)(2,1)S(1)}, u32[]{:S(2)}, u32[]{:S(2)}) %collective-permute-start.41) | collective-permute-done | bytes 393248 | tf_op jit(solution)/shard_map/ppermute | solution.py:38
  200.6 11.5 %collective-permute-done.29 = bf16[192,2048]{1,0:T(8,128)(2,1)S(1)} collective-permute-done((bf16[192,2048]{1,0:T(8,128)(2,1)S(1)}, bf16[192,2048]{1,0:T(8,128)(2,1)S(1)}, u32[]{:S(2)}, u32[]{:S(2)}) %collective-permute-start.29) | collective-permute-done | bytes 786464 | tf_op jit(solution)/shard_map/ppermute | solution.py:38
  213.8 11.3 %collective-permute-done.38 = bf16[192,1024]{1,0:T(8,128)(2,1)S(1)} collective-permute-done((bf16[192,1024]{1,0:T(8,128)(2,1)S(1)}, bf16[192,1024]{1,0:T(8,128)(2,1)S(1)}, u32[]{:S(2)}, u32[]{:S(2)}) %collective-permute-start.38) | collective-permute-done | bytes 393248 | tf_op jit(solution)/shard_map/ppermute | solution.py:38
  256.2 3.7 %collective-permute-done.33 = bf16[128,896]{1,0:T(8,128)(2,1)S(1)} collective-permute-done((bf16[128,896]{1,0:T(8,128)(2,1)S(1)}, bf16[128,896]{1,0:T(8,128)(2,1)S(1)}, u32[]{:S(2)}, u32[]{:S(2)}) %collective-permute-start.33) | collective-permute-done | bytes 229408 | tf_op jit(solution)/shard_map/ppermute | solution.py:38
  259.9 10.3 %collective-permute-done.32 = bf16[128,896]{1,0:T(8,128)(2,1)S(1)} collective-permute-done((bf16[128,896]{1,0:T(8,128)(2,1)S(1)}, bf16[128,896]{1,0:T(8,128)(2,1)S(1)}, u32[]{:S(2)}, u32[]{:S(2)}) %collective-permute-start.32) | collective-permute-done | bytes 229408 | tf_op jit(solution)/shard_map/ppermute | solution.py:38
  271.4 10.5 %collective-permute-done.45 = bf16[128,896]{1,0:T(8,128)(2,1)S(1)} collective-permute-done((bf16[128,896]{1,0:T(8,128)(2,1)S(1)}, bf16[128,896]{1,0:T(8,128)(2,1)S(1)}, u32[]{:S(2)}, u32[]{:S(2)}) %collective-permute-start.45) | collective-permute-done | bytes 229408 | tf_op jit(solution)/shard_map/ppermute | solution.py:38
  281.9 7.9 %collective-permute-done.46 = bf16[128,896]{1,0:T(8,128)(2,1)S(1)} collective-permute-done((bf16[128,896]{1,0:T(8,128)(2,1)S(1)}, bf16[128,896]{1,0:T(8,128)(2,1)S(1)}, u32[]{:S(2)}, u32[]{:S(2)}) %collective-permute-start.46) | collective-permute-done | bytes 229408 | tf_op jit(solution)/shard_map/ppermute | solution.py:38
  (160 shorter events, 89.5 us)
Async XLA Ops:
  3.0 24.6 %collective-permute-start = (bf16[128,896]{1,0:T(8,128)(2,1)}, bf16[128,896]{1,0:T(8,128)(2,1)}, u32[]{:S(2)}, u32[]{:S(2)}) collective-permute-start(bf16[128,896]{1,0:T(8,128)(2,1)} %get-tuple-element.98), channel_id=1, source_target_pairs={{0,1},{1,0},{2,3},{3,2},{4,5},{5,4},{6,7},{7,6},{8,9},{9,8},{10,11... | collective-permute-start | bytes 688136 | tf_op jit(solution)/shard_map/ppermute | solution.py:38
  6.0 21.6 %collective-permute-start.1 = (bf16[128,896]{1,0:T(8,128)(2,1)}, bf16[128,896]{1,0:T(8,128)(2,1)}, u32[]{:S(2)}, u32[]{:S(2)}) collective-permute-start(bf16[128,896]{1,0:T(8,128)(2,1)} %get-tuple-element.100), channel_id=1, source_target_pairs={{0,2},{1,3},{2,0},{3,1},{4,6},{5,7},{6,4},{7,5},{8,10},{9,11},{10,... | collective-permute-start | bytes 688136 | tf_op jit(solution)/shard_map/ppermute | solution.py:38
  8.6 19.0 %collective-permute-start.2 = (bf16[128,896]{1,0:T(8,128)(2,1)S(1)}, bf16[128,896]{1,0:T(8,128)(2,1)}, u32[]{:S(2)}, u32[]{:S(2)}) collective-permute-start(bf16[128,896]{1,0:T(8,128)(2,1)S(1)} %get-tuple-element.99), channel_id=1, source_target_pairs={{0,3},{1,2},{2,1},{3,0},{4,7},{5,6},{6,5},{7,4},{8,11},{9,10},{10,... | collective-permute-start | bytes 688136 | tf_op jit(solution)/shard_map/ppermute | solution.py:38
  31.0 46.8 %collective-permute-start.3 = (bf16[192,2048]{1,0:T(8,128)(2,1)S(1)}, bf16[192,2048]{1,0:T(8,128)(2,1)S(1)}, u32[]{:S(2)}, u32[]{:S(2)}) collective-permute-start(bf16[192,2048]{1,0:T(8,128)(2,1)S(1)} %get-tuple-element.111), channel_id=1, source_target_pairs={{0,1},{3,2},{4,5},{7,6},{8,9},{11,10},{12,13},{15,14},{16,17},{19,... | collective-permute-start | bytes 2359304 | tf_op jit(solution)/shard_map/ppermute | solution.py:38
  37.0 22.8 %collective-permute-start.7 = (bf16[128,896]{1,0:T(8,128)(2,1)S(1)}, bf16[128,896]{1,0:T(8,128)(2,1)S(1)}, u32[]{:S(2)}, u32[]{:S(2)}) collective-permute-start(bf16[128,896]{1,0:T(8,128)(2,1)S(1)} %get-tuple-element.34), channel_id=1, source_target_pairs={{0,1},{1,0},{2,3},{3,2},{4,5},{5,4},{6,7},{7,6},{8,9},{9,8},{10,11... | collective-permute-start | bytes 688136 | tf_op jit(solution)/shard_map/ppermute | solution.py:38
  37.1 27.2 %collective-permute-start.8 = (bf16[128,896]{1,0:T(8,128)(2,1)S(1)}, bf16[128,896]{1,0:T(8,128)(2,1)S(1)}, u32[]{:S(2)}, u32[]{:S(2)}) collective-permute-start(bf16[128,896]{1,0:T(8,128)(2,1)S(1)} %get-tuple-element.35), channel_id=1, source_target_pairs={{0,2},{1,3},{2,0},{3,1},{4,6},{5,7},{6,4},{7,5},{8,10},{9,11},{10,... | collective-permute-start | bytes 688136 | tf_op jit(solution)/shard_map/ppermute | solution.py:38
  40.8 29.6 %collective-permute-start.9 = (bf16[128,896]{1,0:T(8,128)(2,1)S(1)}, bf16[128,896]{1,0:T(8,128)(2,1)S(1)}, u32[]{:S(2)}, u32[]{:S(2)}) collective-permute-start(bf16[128,896]{1,0:T(8,128)(2,1)S(1)} %get-tuple-element.36), channel_id=1, source_target_pairs={{0,3},{1,2},{2,1},{3,0},{4,7},{5,6},{6,5},{7,4},{8,11},{9,10},{10,... | collective-permute-start | bytes 688136 | tf_op jit(solution)/shard_map/ppermute | solution.py:38
  41.6 30.6 %collective-permute-start.6 = (bf16[192,896]{1,0:T(8,128)(2,1)S(1)}, bf16[192,896]{1,0:T(8,128)(2,1)S(1)}, u32[]{:S(2)}, u32[]{:S(2)}) collective-permute-start(bf16[192,896]{1,0:T(8,128)(2,1)S(1)} %get-tuple-element.84), channel_id=1, source_target_pairs={{0,4},{4,0},{8,12},{12,8},{1,5},{5,1},{9,13},{13,9},{2,6},{6,2},{1... | collective-permute-start | bytes 1032200 | tf_op jit(solution)/shard_map/ppermute | solution.py:38
  78.0 23.3 %collective-permute-start.4 = (bf16[192,2048]{1,0:T(8,128)(2,1)S(1)}, bf16[192,2048]{1,0:T(8,128)(2,1)S(1)}, u32[]{:S(2)}, u32[]{:S(2)}) collective-permute-start(bf16[192,2048]{1,0:T(8,128)(2,1)S(1)} %fusion.82), channel_id=1, source_target_pairs={{1,2},{2,1},{5,6},{6,5},{9,10},{10,9},{13,14},{14,13},{17,18},{18,... | collective-permute-start | bytes 2359304 | tf_op jit(solution)/shard_map/ppermute | solution.py:38
  94.2 22.6 %collective-permute-start.11 = (bf16[192,2048]{1,0:T(8,128)(2,1)S(1)}, bf16[192,2048]{1,0:T(8,128)(2,1)S(1)}, u32[]{:S(2)}, u32[]{:S(2)}) collective-permute-start(bf16[192,2048]{1,0:T(8,128)(2,1)S(1)} %get-tuple-element.38), channel_id=1, source_target_pairs={{0,1},{3,2},{4,5},{7,6},{8,9},{11,10},{12,13},{15,14},{16,17},{19,... | collective-permute-start | bytes 2359304 | tf_op jit(solution)/shard_map/ppermute | solution.py:38
  101.5 20.7 %collective-permute-start.5 = (bf16[192,2048]{1,0:T(8,128)(2,1)S(1)}, bf16[192,2048]{1,0:T(8,128)(2,1)S(1)}, u32[]{:S(2)}, u32[]{:S(2)}) collective-permute-start(bf16[192,2048]{1,0:T(8,128)(2,1)S(1)} %add_convert_fusion.3), channel_id=1, source_target_pairs={{1,0},{2,3},{5,4},{6,7},{9,8},{10,11},{13,12},{14,15},{17,16},{18,... | collective-permute-start | bytes 2359304 | tf_op jit(solution)/shard_map/ppermute | solution.py:38
  128.3 22.0 %collective-permute-start.20 = (bf16[192,2048]{1,0:T(8,128)(2,1)S(1)}, bf16[192,2048]{1,0:T(8,128)(2,1)S(1)}, u32[]{:S(2)}, u32[]{:S(2)}) collective-permute-start(bf16[192,2048]{1,0:T(8,128)(2,1)S(1)} %get-tuple-element.43), channel_id=1, source_target_pairs={{0,1},{3,2},{4,5},{7,6},{8,9},{11,10},{12,13},{15,14},{16,17},{19,... | collective-permute-start | bytes 2359304 | tf_op jit(solution)/shard_map/ppermute | solution.py:38
  136.7 20.3 %collective-permute-start.15 = (bf16[192,2048]{1,0:T(8,128)(2,1)S(1)}, bf16[192,2048]{1,0:T(8,128)(2,1)S(1)}, u32[]{:S(2)}, u32[]{:S(2)}) collective-permute-start(bf16[192,2048]{1,0:T(8,128)(2,1)S(1)} %add_convert_fusion.2), channel_id=1, source_target_pairs={{1,0},{2,3},{5,4},{6,7},{9,8},{10,11},{13,12},{14,15},{17,16},{18,... | collective-permute-start | bytes 2359304 | tf_op jit(solution)/shard_map/ppermute | solution.py:38
  154.9 18.4 %collective-permute-start.21 = (bf16[192,2048]{1,0:T(8,128)(2,1)S(1)}, bf16[192,2048]{1,0:T(8,128)(2,1)S(1)}, u32[]{:S(2)}, u32[]{:S(2)}) collective-permute-start(bf16[192,2048]{1,0:T(8,128)(2,1)S(1)} %fusion.84), channel_id=1, source_target_pairs={{1,2},{2,1},{5,6},{6,5},{9,10},{10,9},{13,14},{14,13},{17,18},{18,... | collective-permute-start | bytes 2359304 | tf_op jit(solution)/shard_map/ppermute | solution.py:38
  173.5 20.6 %collective-permute-start.24 = (bf16[192,2048]{1,0:T(8,128)(2,1)S(1)}, bf16[192,2048]{1,0:T(8,128)(2,1)S(1)}, u32[]{:S(2)}, u32[]{:S(2)}) collective-permute-start(bf16[192,2048]{1,0:T(8,128)(2,1)S(1)} %add_convert_fusion.1), channel_id=1, source_target_pairs={{1,0},{2,3},{5,4},{6,7},{9,8},{10,11},{13,12},{14,15},{17,16},{18,... | collective-permute-start | bytes 2359304 | tf_op jit(solution)/shard_map/ppermute | solution.py:38
  176.8 74.6 %collective-permute-start.34 = (bf16[192,896]{1,0:T(8,128)(2,1)S(1)}, bf16[192,896]{1,0:T(8,128)(2,1)S(1)}, u32[]{:S(2)}, u32[]{:S(2)}) collective-permute-start(bf16[192,896]{1,0:T(8,128)(2,1)S(1)} %convolution_convert_fusion.5), channel_id=1, source_target_pairs={{0,4},{4,0},{8,12},{12,8},{1,5},{5,1},{9,13},{13,9},{2,6},{6,2},{1... | collective-permute-start | bytes 1032200 | tf_op jit(solution)/shard_map/ppermute | solution.py:38
  177.7 68.2 %collective-permute-start.16 = (bf16[192,896]{1,0:T(8,128)(2,1)S(1)}, bf16[192,896]{1,0:T(8,128)(2,1)S(1)}, u32[]{:S(2)}, u32[]{:S(2)}) collective-permute-start(bf16[192,896]{1,0:T(8,128)(2,1)S(1)} %fusion.73), channel_id=1, source_target_pairs={{0,4},{4,0},{8,12},{12,8},{1,5},{5,1},{9,13},{13,9},{2,6},{6,2},{1... | collective-permute-start | bytes 1032200 | tf_op jit(solution)/shard_map/ppermute | solution.py:38
  178.3 22.1 %collective-permute-start.37 = (bf16[192,1024]{1,0:T(8,128)(2,1)S(1)}, bf16[192,1024]{1,0:T(8,128)(2,1)S(1)}, u32[]{:S(2)}, u32[]{:S(2)}) collective-permute-start(bf16[192,1024]{1,0:T(8,128)(2,1)S(1)} %fusion.122), channel_id=1, source_target_pairs={{1,2},{2,1},{5,6},{6,5},{9,10},{10,9},{13,14},{14,13},{17,18},{18,... | collective-permute-start | bytes 1179656 | tf_op jit(solution)/shard_map/ppermute | solution.py:38
  179.0 20.1 %collective-permute-start.41 = (bf16[192,1024]{1,0:T(8,128)(2,1)S(1)}, bf16[192,1024]{1,0:T(8,128)(2,1)S(1)}, u32[]{:S(2)}, u32[]{:S(2)}) collective-permute-start(bf16[192,1024]{1,0:T(8,128)(2,1)S(1)} %get-tuple-element.57), channel_id=1, source_target_pairs={{0,1},{3,2},{4,5},{7,6},{8,9},{11,10},{12,13},{15,14},{16,17},{19,... | collective-permute-start | bytes 1179656 | tf_op jit(solution)/shard_map/ppermute | solution.py:38
  228.6 24.8 %collective-permute-start.39 = (bf16[192,896]{1,0:T(8,128)(2,1)S(1)}, bf16[192,896]{1,0:T(8,128)(2,1)S(1)}, u32[]{:S(2)}, u32[]{:S(2)}) collective-permute-start(bf16[192,896]{1,0:T(8,128)(2,1)S(1)} %convolution_convert_fusion.4), channel_id=1, source_target_pairs={{0,8},{4,12},{8,0},{12,4},{1,9},{5,13},{9,1},{13,5},{2,10},{6,14},... | collective-permute-start | bytes 1032200 | tf_op jit(solution)/shard_map/ppermute | solution.py:38
  250.9 19.3 %collective-permute-start.32 = (bf16[128,896]{1,0:T(8,128)(2,1)S(1)}, bf16[128,896]{1,0:T(8,128)(2,1)S(1)}, u32[]{:S(2)}, u32[]{:S(2)}) collective-permute-start(bf16[128,896]{1,0:T(8,128)(2,1)S(1)} %get-tuple-element.52), channel_id=1, source_target_pairs={{0,2},{1,3},{2,0},{3,1},{4,6},{5,7},{6,4},{7,5},{8,10},{9,11},{10,... | collective-permute-start | bytes 688136 | tf_op jit(solution)/shard_map/ppermute | solution.py:38
  251.4 18.8 %collective-permute-start.31 = (bf16[128,896]{1,0:T(8,128)(2,1)S(1)}, bf16[128,896]{1,0:T(8,128)(2,1)S(1)}, u32[]{:S(2)}, u32[]{:S(2)}) collective-permute-start(bf16[128,896]{1,0:T(8,128)(2,1)S(1)} %get-tuple-element.51), channel_id=1, source_target_pairs={{0,3},{1,2},{2,1},{3,0},{4,7},{5,6},{6,5},{7,4},{8,11},{9,10},{10,... | collective-permute-start | bytes 688136 | tf_op jit(solution)/shard_map/ppermute | solution.py:38
  259.9 29.9 %collective-permute-start.47 = (bf16[128,896]{1,0:T(8,128)(2,1)S(1)}, bf16[128,896]{1,0:T(8,128)(2,1)S(1)}, u32[]{:S(2)}, u32[]{:S(2)}) collective-permute-start(bf16[128,896]{1,0:T(8,128)(2,1)S(1)} %get-tuple-element.62), channel_id=1, source_target_pairs={{0,1},{1,0},{2,3},{3,2},{4,5},{5,4},{6,7},{7,6},{8,9},{9,8},{10,11... | collective-permute-start | bytes 688136 | tf_op jit(solution)/shard_map/ppermute | solution.py:38
  270.2 19.6 %collective-permute-start.46 = (bf16[128,896]{1,0:T(8,128)(2,1)S(1)}, bf16[128,896]{1,0:T(8,128)(2,1)S(1)}, u32[]{:S(2)}, u32[]{:S(2)}) collective-permute-start(bf16[128,896]{1,0:T(8,128)(2,1)S(1)} %get-tuple-element.61), channel_id=1, source_target_pairs={{0,2},{1,3},{2,0},{3,1},{4,6},{5,7},{6,4},{7,5},{8,10},{9,11},{10,... | collective-permute-start | bytes 688136 | tf_op jit(solution)/shard_map/ppermute | solution.py:38
  (32 other events, 409.3 us)

commit v3 on v1

v3 whole, which is shorter than its diff:
```python
import jax
import jax.numpy as jnp
from jax import lax
from jax.sharding import PartitionSpec as P

F32 = jnp.float32
BF16 = jnp.bfloat16
GROUPS = 4
CODE_ROWS = 16
AHEAD = 1
ITEMS = (("pre", (0,)), ("pre", (2,)), ("pre", (3,)), ("pre", (1,)), ("hid", (2, 3)), ("hid", (0, 1)))


def route_places(routes, experts, capacity):
    flat_ids = routes.reshape(-1)
    onehot = (flat_ids[:, None] == jnp.arange(experts, dtype=jnp.int32)[None, :]).astype(jnp.int32)
    before = jnp.cumsum(onehot, axis=0) - onehot
    slot_pos = jnp.sum(before * onehot, axis=1)
    return flat_ids * capacity + slot_pos


def across(left, right):
    return lax.dot_general(left, right, (((1,), (1,)), ((), ())), preferred_element_type=F32)


def over_rows(left, right):
    return lax.dot_general(left, right, (((0,), (0,)), ((), ())), preferred_element_type=F32)


def joined(values, axis=0):
    return values[0] if len(values) == 1 else jnp.concatenate(values, axis=axis)


def after(value, *others):
    return lax.optimization_barrier((value, *others))[0]


class Queue:
    def __init__(self, axis, depth):
        self.axis, self.depth, self.arrived = axis, depth, []

    def turn(self, value):
        return after(value, *self.arrived[-self.depth :][:1]) if len(self.arrived) >= self.depth > 0 else value

    def send(self, value, pairs):
        got = lax.ppermute(self.turn(value), self.axis, pairs)
        self.arrived.append(got)
        return got

    def swap(self, value, distance):
        count = lax.axis_size(self.axis)
        return self.send(value, [(i, i ^ distance) for i in range(count)])


class LineSum:
    def __init__(self, axis, own):
        self.axis, self.count, self.own, self.total = axis, lax.axis_size(axis), own, own
        self.got = None

    def inward(self):
        for hop in range(self.count // 2 - 1):
            pairs = [(hop, hop + 1), (self.count - 1 - hop, self.count - 2 - hop)]
            arrived = lax.ppermute(self.total.astype(BF16), self.axis, pairs)
            self.total = self.total + arrived.astype(F32)
        return arrived

    def middle(self):
        mid = self.count // 2
        self.got = lax.ppermute(self.total.astype(BF16), self.axis, [(mid - 1, mid), (mid, mid - 1)])
        return self.got

    def outward(self, *others):
        got = after(self.got, *others)
        for hop in reversed(range(self.count // 2 - 1)):
            pairs = [(hop + 1, hop), (self.count - 2 - hop, self.count - 1 - hop)]
            got = got + lax.ppermute((self.own + got.astype(F32)).astype(BF16), self.axis, pairs)
        self.got = got

    def result(self, *others):
        return self.total + after(self.got, *others).astype(F32)


def shards(tokens, routes, gates, gate_weight, up_weight, down_weight, cotangent):
    n_exp = lax.axis_size("expert") * gate_weight.shape[0]
    n_dp = lax.axis_size("dp")
    me = lax.axis_index("expert")
    here = lax.axis_index("dp")
    tok_count, topk = routes.shape
    width = tokens.shape[1]
    part = width // n_dp
    hidden_units = gate_weight.shape[2]
    capacity = 3 * tok_count * topk // (2 * n_exp)
    chunk = n_dp * capacity
    per_group = n_exp // GROUPS
    w_gate, w_up, w_down = gate_weight[0], up_weight[0], down_weight[0]
    w_both = jnp.concatenate([w_gate, w_up], axis=1)
    distances = list(range(n_dp - 1, 0, -1))

    features, experts = Queue("dp", 0), Queue("expert", 0)
    blocks = here ^ jnp.arange(n_dp, dtype=jnp.int32)

    def columns(value, distance):
        return lax.dynamic_slice(value, (0, (here ^ distance) * part), (tok_count, part))

    def by_features(value, tail):
        pieces = [columns(value, k) for k in range(n_dp)]
        if tail is not None:
            pieces = [jnp.concatenate([piece, tail], axis=0) for piece in pieces]
        earlier = list(features.arrived)
        got = {k: features.swap(after(pieces[k], *earlier), k) for k in distances}
        return [pieces[0]] + [got[k] for k in range(1, n_dp)]

    codes = route_places(routes, n_exp, capacity).astype(BF16)
    tail = jnp.zeros((CODE_ROWS, part), BF16) + jnp.pad(codes, (0, part - tok_count))[None, :]
    weighted = (gates * cotangent.astype(F32)).astype(BF16)
    got_rows = by_features(tokens, tail)
    got_grads = by_features(weighted, None)

    codes = jnp.stack([piece[tok_count, :tok_count] for piece in got_rows]).astype(jnp.int32)
    places = ((codes // capacity) ^ me) * chunk + blocks[:, None] * capacity + codes % capacity
    select = (jnp.arange(n_exp * chunk, dtype=jnp.int32)[:, None] == places.reshape(-1)[None, :]).astype(BF16)

    def dispatch(pieces):
        gathered = jnp.concatenate([piece[:tok_count] for piece in pieces], axis=0)
        rows = jnp.dot(select, gathered, preferred_element_type=F32).astype(BF16)
        return rows.reshape(n_exp, chunk, part)

    def exchange(blocks, bits, *others):
        blocks = list(blocks)
        for bit in bits:
            moved = [k for k in range(n_exp) if k & bit]
            sent = jnp.concatenate([blocks[k] for k in moved], axis=0)
            got = experts.swap(after(sent, *others), bit)
            for i, k in enumerate(moved):
                blocks[k] = got[i * chunk : (i + 1) * chunk]
            last = got
        return blocks, last

    bits = [n_exp >> (i + 1) for i in range(n_exp.bit_length() - 1)]

    def grouped(blocks):
        return [joined(blocks[g * per_group : (g + 1) * per_group]) for g in range(GROUPS)]

    def blocks_of(values):
        return [None if v is None else v[i * chunk : (i + 1) * chunk] for v in values for i in range(per_group)]

    def pick(values):
        return over_rows(select, jnp.concatenate(values, axis=0)).astype(BF16).reshape(n_dp, tok_count, part)

    def give_back(picked):
        got = {k: features.swap(picked[k], k) for k in distances}
        return [picked[0]] + [got[k] for k in range(1, n_dp)]

    def placed(pieces):
        result = jnp.zeros((tok_count, width), BF16)
        for k, piece in enumerate(pieces):
            result = lax.dynamic_update_slice(result, piece, (0, (here ^ k) * part))
        return result

    rows = grouped(exchange(dispatch(got_rows), bits)[0])
    sent_grads = dispatch(got_grads)
    grads = None
    sums, pre = [], [None] * GROUPS
    hidden, out, both, back = [None] * GROUPS, [None] * GROUPS, [None] * GROUPS, [None] * GROUPS

    def finish(item, *others):
        kind, gs = ITEMS[item]
        got = sums[item].result(*others)
        size = got.shape[0] // len(gs)
        for i, g in enumerate(gs):
            value = got[i * size : (i + 1) * size]
            if kind == "pre":
                pre[g] = value
                pre_gate, pre_up = value[:, :hidden_units], value[:, hidden_units:]
                hidden[g] = after((pre_gate * jax.nn.sigmoid(pre_gate) * pre_up).astype(BF16))
                out[g] = across(hidden[g], w_down).astype(BF16)
            else:
                pre_gate, pre_up = pre[g][:, :hidden_units], pre[g][:, hidden_units:]
                sig = jax.nn.sigmoid(pre_gate)
                pg_grad = (value * pre_up * sig * (1.0 + pre_gate * (1.0 - sig))).astype(BF16)
                pu_grad = (value * (pre_gate * sig)).astype(BF16)
                both[g] = after(jnp.concatenate([pg_grad, pu_grad], axis=1))
                back[g] = across(both[g], w_both).astype(BF16)

    def start(item):
        kind, gs = ITEMS[item]
        moved = joined([(rows if kind == "pre" else grads)[g] for g in gs])
        moved = after(moved, inward[item - AHEAD] if item >= AHEAD else got_grads[1])
        sums.append(LineSum("dp", jnp.dot(moved, w_both if kind == "pre" else w_down, preferred_element_type=F32)))
        inward.append(sums[item].inward())
        middle.append(sums[item].middle())

    inward, middle = [], []
    start(0)
    grads = grouped(exchange(sent_grads, bits, inward[0])[0])
    start(1)
    sums[0].outward()
    start(2)
    sums[1].outward()
    finish(0)
    start(3)
    sums[2].outward()
    finish(1)
    start(4)
    sums[3].outward()
    finish(2)
    halfway, half_o = exchange(blocks_of(out), bits[:1])
    start(5)
    sums[4].outward()
    finish(3, inward[4])
    here_blocks = blocks_of(out)
    out, arrived = exchange([block if half is None else half for block, half in zip(here_blocks, halfway)], bits[1:])
    sums[5].outward()
    finish(4, inward[5], half_o)
    halfway, arrived = exchange(blocks_of(back), bits[:1])
    out = give_back(pick(out))
    finish(5, out[1])
    here_blocks = blocks_of(back)
    back, _ = exchange([block if half is None else half for block, half in zip(here_blocks, halfway)], bits[1:], *out[1:])
    picked = pick(back)
    back = give_back(picked)

    mixed = placed([(piece.astype(F32) * gates).astype(BF16) for piece in out])
    token_grad = placed(back)
    all_rows, all_grads = jnp.concatenate(rows, axis=0), jnp.concatenate(grads, axis=0)
    all_both, all_hidden = jnp.concatenate(both, axis=0), jnp.concatenate(hidden, axis=0)
    all_both, all_hidden, _ = lax.optimization_barrier((all_both, all_hidden, picked))
    gate_grad = over_rows(all_rows, all_both[:, :hidden_units]).astype(BF16)
    up_grad = over_rows(all_rows, all_both[:, hidden_units:]).astype(BF16)
    down_grad = over_rows(all_grads, all_hidden).astype(BF16)
    return (mixed, token_grad, gate_grad[None], up_grad[None], down_grad[None])


def solution(mesh):
    rows = P(("groups", "expert", "dp"), None)
    weights = P("expert", "dp", None)
    grads = P(("groups", "expert"), "dp", None)
    return jax.shard_map(
        shards,
        mesh=mesh,
        in_specs=(rows, rows, rows, weights, weights, weights, rows),
        out_specs=(rows, rows, grads, grads, grads),
        check_vma=False,
    )
```

time: 383 us -> 266 us (0.69)
  waiting for transfers between devices: 231 us -> 144 us
  blocking collectives: 22.8 us -> 0 us
  starting transfers between devices: 84.6 us -> 66.7 us
  other arithmetic: 7.45 us -> 14 us
  local copies, waits for them, and re-layouts: 4.69 us -> 9.68 us
    ppermute x48 -> x38, waiting for transfers between devices: 231 us -> 144 us  [the longest x20 76.5 us: send(): got = lax.ppermute(self.turn(value), self.axis, pairs)]
    all_gather x1 -> x0, blocking collectives: 22.8 us -> none  [shards(): codes = lax.all_gather(route_places(routes, n_exp, capacity), 'dp')]
    ppermute x48 -> x38, starting transfers between devices: 84.6 us -> 66.7 us  [the longest x6 28.9 us: inward(): arrived = lax.ppermute(self.total.astype(BF16), self.axis, pairs)]
    slice x7 -> x15, local copies, waits for them, and re-layouts: 0.53 us -> 5.43 us  [the longest x3 2.87 us: dispatch(): gathered = jnp.concatenate([piece[:tok_count] for piece in pieces], axis=0)]
  transfers between devices with their start and end apart: 48 -> 38, of which waited for: 19 -> 20; matrix products, arithmetic and copies ran while one was open for 10% -> 14% of each run, Pallas kernels for 0% -> 0%
where the time goes in v3:
time: 266 us; the launch traced here: 263 us
  waiting for transfers between devices  144 us (54%)
  starting transfers between devices  66.7 us (25%)
  matrix products  27.3 us (10%)
  other arithmetic  14 us (5%)
  local copies, waits for them, and re-layouts  9.68 us (4%)
    ppermute x20, waiting for transfers between devices, send(): got = lax.ppermute(self.turn(value), self.axis, pairs)  76.5 us
    ppermute x6, waiting for transfers between devices, outward(): lax.ppermute((self.own + got.astype(F32)).astype(BF16), self.axis, pairs)  43.1 us
    ppermute x6, starting transfers between devices, inward(): arrived = lax.ppermute(self.total.astype(BF16), self.axis, pairs)  28.9 us
    ppermute x20, starting transfers between devices, send(): got = lax.ppermute(self.turn(value), self.axis, pairs)  25.3 us
    ppermute x6, waiting for transfers between devices, inward(): arrived = lax.ppermute(self.total.astype(BF16), self.axis, pairs)  24.2 us
    dot_general x5, matrix products, over_rows(): lax.dot_general(left, right, (((0,), (0,)), ((), ())), preferred_element_...  10.7 us
    dot_general x8, matrix products, across(): lax.dot_general(left, right, (((1,), (1,)), ((), ())), preferred_element_...  8.65 us
    ppermute x6, starting transfers between devices, outward(): lax.ppermute((self.own + got.astype(F32)).astype(BF16), self.axis, pairs)  8.15 us
  transfers between devices with their start and end apart: 38, of which 20 were waited for; matrix products, arithmetic and copies ran while one was open for 14% of the time, Pallas kernels for 0%

profile of v3, /device:TPU:0, one launch (start us, length us, event | category | flops | bytes accessed | tf_op | source)
XLA Modules:
  0.0 263.0 jit_solution(397522765755794648)
XLA Ops:
  5.4 5.1 %collective-permute-start.2 = (bf16[144,896]{1,0:T(8,128)(2,1)S(1)}, bf16[144,896]{1,0:T(8,128)(2,1)}, u32[]{:S(2)}, u32[]{:S(2)}) collective-permute-start(bf16[144,896]{1,0:T(8,128)(2,1)S(1)} %get-tuple-element.89), channel_id=1, source_target_pairs={{0,3},{1,2},{2,1},{3,0},{4,7},{5,6},{6,5},{7,4},{8,11},{9,10},{10,... | collective-permute-start | bytes 774152 | tf_op jit(solution)/shard_map/ppermute | solution.py:46
  12.2 5.6 %collective-permute-done.2 = bf16[144,896]{1,0:T(8,128)(2,1)} collective-permute-done((bf16[144,896]{1,0:T(8,128)(2,1)S(1)}, bf16[144,896]{1,0:T(8,128)(2,1)}, u32[]{:S(2)}, u32[]{:S(2)}) %collective-permute-start.2) | collective-permute-done | bytes 258080 | tf_op jit(solution)/shard_map/ppermute | solution.py:46
  18.5 14.1 %collective-permute-done.1 = bf16[144,896]{1,0:T(8,128)(2,1)} collective-permute-done((bf16[144,896]{1,0:T(8,128)(2,1)S(1)}, bf16[144,896]{1,0:T(8,128)(2,1)}, u32[]{:S(2)}, u32[]{:S(2)}) %collective-permute-start.1) | collective-permute-done | bytes 258080 | tf_op jit(solution)/shard_map/ppermute | solution.py:46
  43.1 6.8 %collective-permute-done.3 = bf16[128,896]{1,0:T(8,128)(2,1)S(1)} collective-permute-done((bf16[128,896]{1,0:T(8,128)(2,1)S(1)}, bf16[128,896]{1,0:T(8,128)(2,1)S(1)}, u32[]{:S(2)}, u32[]{:S(2)}) %collective-permute-start.3) | collective-permute-done | bytes 229408 | tf_op jit(solution)/shard_map/ppermute | solution.py:46
  53.5 8.3 %collective-permute-done.14 = bf16[128,896]{1,0:T(8,128)(2,1)S(1)} collective-permute-done((bf16[128,896]{1,0:T(8,128)(2,1)S(1)}, bf16[128,896]{1,0:T(8,128)(2,1)S(1)}, u32[]{:S(2)}, u32[]{:S(2)}) %collective-permute-start.14) | collective-permute-done | bytes 229408 | tf_op jit(solution)/shard_map/ppermute | solution.py:46
  63.2 7.3 %collective-permute-done.4 = bf16[192,2048]{1,0:T(8,128)(2,1)S(1)} collective-permute-done((bf16[192,2048]{1,0:T(8,128)(2,1)S(1)}, bf16[192,2048]{1,0:T(8,128)(2,1)S(1)}, u32[]{:S(2)}, u32[]{:S(2)}) %collective-permute-start.4) | collective-permute-done | bytes 786464 | tf_op jit(solution)/shard_map/ppermute | solution.py:63
  71.4 4.4 %collective-permute-start.9 = (bf16[192,2048]{1,0:T(8,128)(2,1)S(1)}, bf16[192,2048]{1,0:T(8,128)(2,1)S(1)}, u32[]{:S(2)}, u32[]{:S(2)}) collective-permute-start(bf16[192,2048]{1,0:T(8,128)(2,1)S(1)} %get-tuple-element.92), channel_id=1, source_target_pairs={{0,1},{3,2},{4,5},{7,6},{8,9},{11,10},{12,13},{15,14},{16,17},{19,... | collective-permute-start | bytes 2359304 | tf_op jit(solution)/shard_map/ppermute | solution.py:63
  77.5 13.8 %collective-permute-done.16 = bf16[384,896]{1,0:T(8,128)(2,1)S(1)} collective-permute-done((bf16[384,896]{1,0:T(8,128)(2,1)S(1)}, bf16[384,896]{1,0:T(8,128)(2,1)S(1)}, u32[]{:S(2)}, u32[]{:S(2)}) %collective-permute-start.16) | collective-permute-done | bytes 688160 | tf_op jit(solution)/shard_map/ppermute | solution.py:46
  92.4 4.0 %collective-permute-start.10 = (bf16[192,2048]{1,0:T(8,128)(2,1)S(1)}, bf16[192,2048]{1,0:T(8,128)(2,1)S(1)}, u32[]{:S(2)}, u32[]{:S(2)}) collective-permute-start(bf16[192,2048]{1,0:T(8,128)(2,1)S(1)} %get-tuple-element.94), channel_id=1, source_target_pairs={{0,1},{3,2},{4,5},{7,6},{8,9},{11,10},{12,13},{15,14},{16,17},{19,... | collective-permute-start | bytes 2359304 | tf_op jit(solution)/shard_map/ppermute | solution.py:63
  99.1 12.3 %collective-permute-done.10 = bf16[192,2048]{1,0:T(8,128)(2,1)S(1)} collective-permute-done((bf16[192,2048]{1,0:T(8,128)(2,1)S(1)}, bf16[192,2048]{1,0:T(8,128)(2,1)S(1)}, u32[]{:S(2)}, u32[]{:S(2)}) %collective-permute-start.10) | collective-permute-done | bytes 786464 | tf_op jit(solution)/shard_map/ppermute | solution.py:63
  114.9 6.9 %collective-permute-start.11 = (bf16[192,2048]{1,0:T(8,128)(2,1)S(1)}, bf16[192,2048]{1,0:T(8,128)(2,1)S(1)}, u32[]{:S(2)}, u32[]{:S(2)}) collective-permute-start(bf16[192,2048]{1,0:T(8,128)(2,1)S(1)} %get-tuple-element.96), channel_id=1, source_target_pairs={{0,1},{3,2},{4,5},{7,6},{8,9},{11,10},{12,13},{15,14},{16,17},{19,... | collective-permute-start | bytes 2359304 | tf_op jit(solution)/shard_map/ppermute | solution.py:63
  125.1 10.8 %collective-permute-done.20 = bf16[192,2048]{1,0:T(8,128)(2,1)S(1)} collective-permute-done((bf16[192,2048]{1,0:T(8,128)(2,1)S(1)}, bf16[192,2048]{1,0:T(8,128)(2,1)S(1)}, u32[]{:S(2)}, u32[]{:S(2)}) %collective-permute-start.20) | collective-permute-done | bytes 786464 | tf_op jit(solution)/shard_map/ppermute | solution.py:76
  138.8 5.5 %collective-permute-start.18 = (bf16[384,1024]{1,0:T(8,128)(2,1)S(1)}, bf16[384,1024]{1,0:T(8,128)(2,1)S(1)}, u32[]{:S(2)}, u32[]{:S(2)}) collective-permute-start(bf16[384,1024]{1,0:T(8,128)(2,1)S(1)} %get-tuple-element.98), channel_id=1, source_target_pairs={{0,1},{3,2},{4,5},{7,6},{8,9},{11,10},{12,13},{15,14},{16,17},{19,... | collective-permute-start | bytes 2359304 | tf_op jit(solution)/shard_map/ppermute | solution.py:63
  145.0 5.4 %collective-permute-done.22 = bf16[192,2048]{1,0:T(8,128)(2,1)S(1)} collective-permute-done((bf16[192,2048]{1,0:T(8,128)(2,1)S(1)}, bf16[192,2048]{1,0:T(8,128)(2,1)S(1)}, u32[]{:S(2)}, u32[]{:S(2)}) %collective-permute-start.22) | collective-permute-done | bytes 786464 | tf_op jit(solution)/shard_map/ppermute | solution.py:76
  158.8 6.8 %collective-permute-start.28 = (bf16[384,1024]{1,0:T(8,128)(2,1)S(1)}, bf16[384,1024]{1,0:T(8,128)(2,1)S(1)}, u32[]{:S(2)}, u32[]{:S(2)}) collective-permute-start(bf16[384,1024]{1,0:T(8,128)(2,1)S(1)} %get-tuple-element.100), channel_id=1, source_target_pairs={{0,1},{3,2},{4,5},{7,6},{8,9},{11,10},{12,13},{15,14},{16,17},{19,... | collective-permute-start | bytes 2359304 | tf_op jit(solution)/shard_map/ppermute | solution.py:63
  167.4 4.4 %collective-permute-done.13 = bf16[192,2048]{1,0:T(8,128)(2,1)S(1)} collective-permute-done((bf16[192,2048]{1,0:T(8,128)(2,1)S(1)}, bf16[192,2048]{1,0:T(8,128)(2,1)S(1)}, u32[]{:S(2)}, u32[]{:S(2)}) %collective-permute-start.13) | collective-permute-done | bytes 786464 | tf_op jit(solution)/shard_map/ppermute | solution.py:76
  179.6 4.6 %collective-permute-start.25 = (bf16[128,896]{1,0:T(8,128)(2,1)S(1)}, bf16[128,896]{1,0:T(8,128)(2,1)S(1)}, u32[]{:S(2)}, u32[]{:S(2)}) collective-permute-start(bf16[128,896]{1,0:T(8,128)(2,1)S(1)} %get-tuple-element.61), channel_id=1, source_target_pairs={{0,1},{1,0},{2,3},{3,2},{4,5},{5,4},{6,7},{7,6},{8,9},{9,8},{10,11... | collective-permute-start | bytes 688136 | tf_op jit(solution)/shard_map/ppermute | solution.py:46
  186.6 14.4 %collective-permute-done.32 = bf16[384,1024]{1,0:T(8,128)(2,1)S(1)} collective-permute-done((bf16[384,1024]{1,0:T(8,128)(2,1)S(1)}, bf16[384,1024]{1,0:T(8,128)(2,1)S(1)}, u32[]{:S(2)}, u32[]{:S(2)}) %collective-permute-start.32) | collective-permute-done | bytes 786464 | tf_op jit(solution)/shard_map/ppermute | solution.py:76
  209.1 7.3 %collective-permute-done.26 = bf16[128,896]{1,0:T(8,128)(2,1)S(1)} collective-permute-done((bf16[128,896]{1,0:T(8,128)(2,1)S(1)}, bf16[128,896]{1,0:T(8,128)(2,1)S(1)}, u32[]{:S(2)}, u32[]{:S(2)}) %collective-permute-start.26) | collective-permute-done | bytes 229408 | tf_op jit(solution)/shard_map/ppermute | solution.py:46
  216.7 5.6 %collective-permute-done.33 = bf16[384,896]{1,0:T(8,128)(2,1)S(1)} collective-permute-done((bf16[384,896]{1,0:T(8,128)(2,1)S(1)}, bf16[384,896]{1,0:T(8,128)(2,1)S(1)}, u32[]{:S(2)}, u32[]{:S(2)}) %collective-permute-start.33) | collective-permute-done | bytes 688160 | tf_op jit(solution)/shard_map/ppermute | solution.py:46
  222.4 8.1 %collective-permute-done.30 = bf16[384,1024]{1,0:T(8,128)(2,1)S(1)} collective-permute-done((bf16[384,1024]{1,0:T(8,128)(2,1)S(1)}, bf16[384,1024]{1,0:T(8,128)(2,1)S(1)}, u32[]{:S(2)}, u32[]{:S(2)}) %collective-permute-start.30) | collective-permute-done | bytes 786464 | tf_op jit(solution)/shard_map/ppermute | solution.py:76
  234.3 2.9 %convert_bitcast_fusion.2 = bf16[1,896,1024]{2,1,0:T(8,128)(2,1)} fusion(bf16[768,2048]{1,0:T(8,128)(2,1)S(1)} %pad_maximum_fusion.1, bf16[192,896]{1,0:T(8,128)(2,1)S(1)} %get-tuple-element.25, bf16[192,896]{1,0:T(8,128)(2,1)S(1)} %get-tuple-element.24, bf16[192,896]{1,0:T(8,128)(2,1)S(1)} %get-tuple-element.26, bf16[192,896]{1,0:T(8,128)(2,1)S(1)} %get-tuple-element.23), kind=kOutput, calls=%fused_computation.16 | convolution fusion | flops 1415708672 | bytes 4784128 | tf_op jit(solution)/shard_map/dot_general | solution.py:27
  250.0 5.2 %collective-permute-done.35 = bf16[128,896]{1,0:T(8,128)(2,1)S(1)} collective-permute-done((bf16[128,896]{1,0:T(8,128)(2,1)S(1)}, bf16[128,896]{1,0:T(8,128)(2,1)S(1)}, u32[]{:S(2)}, u32[]{:S(2)}) %collective-permute-start.35) | collective-permute-done | bytes 229408 | tf_op jit(solution)/shard_map/ppermute | solution.py:46
  255.3 6.7 %collective-permute-done.36 = bf16[128,896]{1,0:T(8,128)(2,1)S(1)} collective-permute-done((bf16[128,896]{1,0:T(8,128)(2,1)S(1)}, bf16[128,896]{1,0:T(8,128)(2,1)S(1)}, u32[]{:S(2)}, u32[]{:S(2)}) %collective-permute-start.36) | collective-permute-done | bytes 229408 | tf_op jit(solution)/shard_map/ppermute | solution.py:46
  (178 shorter events, 84.9 us)
Async XLA Ops:
  10.5 22.1 %collective-permute-start.1 = (bf16[144,896]{1,0:T(8,128)(2,1)S(1)}, bf16[144,896]{1,0:T(8,128)(2,1)}, u32[]{:S(2)}, u32[]{:S(2)}) collective-permute-start(bf16[144,896]{1,0:T(8,128)(2,1)S(1)} %get-tuple-element.88), channel_id=1, source_target_pairs={{0,2},{1,3},{2,0},{3,1},{4,6},{5,7},{6,4},{7,5},{8,10},{9,11},{10,... | collective-permute-start | bytes 774152 | tf_op jit(solution)/shard_map/ppermute | solution.py:46
  10.5 22.7 %collective-permute-start = (bf16[144,896]{1,0:T(8,128)(2,1)S(1)}, bf16[144,896]{1,0:T(8,128)(2,1)}, u32[]{:S(2)}, u32[]{:S(2)}) collective-permute-start(bf16[144,896]{1,0:T(8,128)(2,1)S(1)} %get-tuple-element.87), channel_id=1, source_target_pairs={{0,1},{1,0},{2,3},{3,2},{4,5},{5,4},{6,7},{7,6},{8,9},{9,8},{10,11... | collective-permute-start | bytes 774152 | tf_op jit(solution)/shard_map/ppermute | solution.py:46
  37.9 25.0 %collective-permute-start.7 = (bf16[384,896]{1,0:T(8,128)(2,1)S(1)}, bf16[384,896]{1,0:T(8,128)(2,1)S(1)}, u32[]{:S(2)}, u32[]{:S(2)}) collective-permute-start(bf16[384,896]{1,0:T(8,128)(2,1)S(1)} %concatenate.104), channel_id=1, source_target_pairs={{0,8},{4,12},{8,0},{12,4},{1,9},{5,13},{9,1},{13,5},{2,10},{6,14},... | collective-permute-start | bytes 2064392 | tf_op jit(solution)/shard_map/ppermute | solution.py:46
  42.0 19.8 %collective-permute-start.14 = (bf16[128,896]{1,0:T(8,128)(2,1)S(1)}, bf16[128,896]{1,0:T(8,128)(2,1)S(1)}, u32[]{:S(2)}, u32[]{:S(2)}) collective-permute-start(bf16[128,896]{1,0:T(8,128)(2,1)S(1)} %get-tuple-element.27), channel_id=1, source_target_pairs={{0,2},{1,3},{2,0},{3,1},{4,6},{5,7},{6,4},{7,5},{8,10},{9,11},{10,... | collective-permute-start | bytes 688136 | tf_op jit(solution)/shard_map/ppermute | solution.py:46
  50.9 19.5 %collective-permute-start.4 = (bf16[192,2048]{1,0:T(8,128)(2,1)S(1)}, bf16[192,2048]{1,0:T(8,128)(2,1)S(1)}, u32[]{:S(2)}, u32[]{:S(2)}) collective-permute-start(bf16[192,2048]{1,0:T(8,128)(2,1)S(1)} %get-tuple-element.90), channel_id=1, source_target_pairs={{0,1},{3,2},{4,5},{7,6},{8,9},{11,10},{12,13},{15,14},{16,17},{19,... | collective-permute-start | bytes 2359304 | tf_op jit(solution)/shard_map/ppermute | solution.py:63
  71.4 20.0 %collective-permute-start.9 = (bf16[192,2048]{1,0:T(8,128)(2,1)S(1)}, bf16[192,2048]{1,0:T(8,128)(2,1)S(1)}, u32[]{:S(2)}, u32[]{:S(2)}) collective-permute-start(bf16[192,2048]{1,0:T(8,128)(2,1)S(1)} %get-tuple-element.92), channel_id=1, source_target_pairs={{0,1},{3,2},{4,5},{7,6},{8,9},{11,10},{12,13},{15,14},{16,17},{19,... | collective-permute-start | bytes 2359304 | tf_op jit(solution)/shard_map/ppermute | solution.py:63
  76.7 20.7 %collective-permute-start.5 = (bf16[192,2048]{1,0:T(8,128)(2,1)S(1)}, bf16[192,2048]{1,0:T(8,128)(2,1)S(1)}, u32[]{:S(2)}, u32[]{:S(2)}) collective-permute-start(bf16[192,2048]{1,0:T(8,128)(2,1)S(1)} %fusion.51), channel_id=1, source_target_pairs={{1,2},{2,1},{5,6},{6,5},{9,10},{10,9},{13,14},{14,13},{17,18},{18,... | collective-permute-start | bytes 2359304 | tf_op jit(solution)/shard_map/ppermute | solution.py:69
  92.4 19.0 %collective-permute-start.10 = (bf16[192,2048]{1,0:T(8,128)(2,1)S(1)}, bf16[192,2048]{1,0:T(8,128)(2,1)S(1)}, u32[]{:S(2)}, u32[]{:S(2)}) collective-permute-start(bf16[192,2048]{1,0:T(8,128)(2,1)S(1)} %get-tuple-element.94), channel_id=1, source_target_pairs={{0,1},{3,2},{4,5},{7,6},{8,9},{11,10},{12,13},{15,14},{16,17},{19,... | collective-permute-start | bytes 2359304 | tf_op jit(solution)/shard_map/ppermute | solution.py:63
  97.6 24.2 %collective-permute-start.6 = (bf16[192,2048]{1,0:T(8,128)(2,1)S(1)}, bf16[192,2048]{1,0:T(8,128)(2,1)S(1)}, u32[]{:S(2)}, u32[]{:S(2)}) collective-permute-start(bf16[192,2048]{1,0:T(8,128)(2,1)S(1)} %add_convert_fusion.5), channel_id=1, source_target_pairs={{1,0},{2,3},{5,4},{6,7},{9,8},{10,11},{13,12},{14,15},{17,16},{18,... | collective-permute-start | bytes 2359304 | tf_op jit(solution)/shard_map/ppermute | solution.py:76
  112.6 23.4 %collective-permute-start.20 = (bf16[192,2048]{1,0:T(8,128)(2,1)S(1)}, bf16[192,2048]{1,0:T(8,128)(2,1)S(1)}, u32[]{:S(2)}, u32[]{:S(2)}) collective-permute-start(bf16[192,2048]{1,0:T(8,128)(2,1)S(1)} %add_convert_fusion.3), channel_id=1, source_target_pairs={{1,0},{2,3},{5,4},{6,7},{9,8},{10,11},{13,12},{14,15},{17,16},{18,... | collective-permute-start | bytes 2359304 | tf_op jit(solution)/shard_map/ppermute | solution.py:76
  114.9 21.7 %collective-permute-start.11 = (bf16[192,2048]{1,0:T(8,128)(2,1)S(1)}, bf16[192,2048]{1,0:T(8,128)(2,1)S(1)}, u32[]{:S(2)}, u32[]{:S(2)}) collective-permute-start(bf16[192,2048]{1,0:T(8,128)(2,1)S(1)} %get-tuple-element.96), channel_id=1, source_target_pairs={{0,1},{3,2},{4,5},{7,6},{8,9},{11,10},{12,13},{15,14},{16,17},{19,... | collective-permute-start | bytes 2359304 | tf_op jit(solution)/shard_map/ppermute | solution.py:63
  123.6 26.8 %collective-permute-start.22 = (bf16[192,2048]{1,0:T(8,128)(2,1)S(1)}, bf16[192,2048]{1,0:T(8,128)(2,1)S(1)}, u32[]{:S(2)}, u32[]{:S(2)}) collective-permute-start(bf16[192,2048]{1,0:T(8,128)(2,1)S(1)} %add_convert_fusion.2), channel_id=1, source_target_pairs={{1,0},{2,3},{5,4},{6,7},{9,8},{10,11},{13,12},{14,15},{17,16},{18,... | collective-permute-start | bytes 2359304 | tf_op jit(solution)/shard_map/ppermute | solution.py:76
  138.8 18.1 %collective-permute-start.18 = (bf16[384,1024]{1,0:T(8,128)(2,1)S(1)}, bf16[384,1024]{1,0:T(8,128)(2,1)S(1)}, u32[]{:S(2)}, u32[]{:S(2)}) collective-permute-start(bf16[384,1024]{1,0:T(8,128)(2,1)S(1)} %get-tuple-element.98), channel_id=1, source_target_pairs={{0,1},{3,2},{4,5},{7,6},{8,9},{11,10},{12,13},{15,14},{16,17},{19,... | collective-permute-start | bytes 2359304 | tf_op jit(solution)/shard_map/ppermute | solution.py:63
  152.9 18.9 %collective-permute-start.13 = (bf16[192,2048]{1,0:T(8,128)(2,1)S(1)}, bf16[192,2048]{1,0:T(8,128)(2,1)S(1)}, u32[]{:S(2)}, u32[]{:S(2)}) collective-permute-start(bf16[192,2048]{1,0:T(8,128)(2,1)S(1)} %add_convert_fusion.4), channel_id=1, source_target_pairs={{1,0},{2,3},{5,4},{6,7},{9,8},{10,11},{13,12},{14,15},{17,16},{18,... | collective-permute-start | bytes 2359304 | tf_op jit(solution)/shard_map/ppermute | solution.py:76
  157.1 16.5 %collective-permute-start.31 = (bf16[384,1024]{1,0:T(8,128)(2,1)S(1)}, bf16[384,1024]{1,0:T(8,128)(2,1)S(1)}, u32[]{:S(2)}, u32[]{:S(2)}) collective-permute-start(bf16[384,1024]{1,0:T(8,128)(2,1)S(1)} %fusion.56), channel_id=1, source_target_pairs={{1,2},{2,1},{5,6},{6,5},{9,10},{10,9},{13,14},{14,13},{17,18},{18,... | collective-permute-start | bytes 2359304 | tf_op jit(solution)/shard_map/ppermute | solution.py:69
  158.8 18.3 %collective-permute-start.28 = (bf16[384,1024]{1,0:T(8,128)(2,1)S(1)}, bf16[384,1024]{1,0:T(8,128)(2,1)S(1)}, u32[]{:S(2)}, u32[]{:S(2)}) collective-permute-start(bf16[384,1024]{1,0:T(8,128)(2,1)S(1)} %get-tuple-element.100), channel_id=1, source_target_pairs={{0,1},{3,2},{4,5},{7,6},{8,9},{11,10},{12,13},{15,14},{16,17},{19,... | collective-permute-start | bytes 2359304 | tf_op jit(solution)/shard_map/ppermute | solution.py:63
  173.9 27.1 %collective-permute-start.32 = (bf16[384,1024]{1,0:T(8,128)(2,1)S(1)}, bf16[384,1024]{1,0:T(8,128)(2,1)S(1)}, u32[]{:S(2)}, u32[]{:S(2)}) collective-permute-start(bf16[384,1024]{1,0:T(8,128)(2,1)S(1)} %add_convert_fusion), channel_id=1, source_target_pairs={{1,0},{2,3},{5,4},{6,7},{9,8},{10,11},{13,12},{14,15},{17,16},{18,... | collective-permute-start | bytes 2359304 | tf_op jit(solution)/shard_map/ppermute | solution.py:76
  177.4 29.8 %collective-permute-start.29 = (bf16[384,1024]{1,0:T(8,128)(2,1)S(1)}, bf16[384,1024]{1,0:T(8,128)(2,1)S(1)}, u32[]{:S(2)}, u32[]{:S(2)}) collective-permute-start(bf16[384,1024]{1,0:T(8,128)(2,1)S(1)} %fusion.55), channel_id=1, source_target_pairs={{1,2},{2,1},{5,6},{6,5},{9,10},{10,9},{13,14},{14,13},{17,18},{18,... | collective-permute-start | bytes 2359304 | tf_op jit(solution)/shard_map/ppermute | solution.py:69
  179.6 29.4 %collective-permute-start.25 = (bf16[128,896]{1,0:T(8,128)(2,1)S(1)}, bf16[128,896]{1,0:T(8,128)(2,1)S(1)}, u32[]{:S(2)}, u32[]{:S(2)}) collective-permute-start(bf16[128,896]{1,0:T(8,128)(2,1)S(1)} %get-tuple-element.61), channel_id=1, source_target_pairs={{0,1},{1,0},{2,3},{3,2},{4,5},{5,4},{6,7},{7,6},{8,9},{9,8},{10,11... | collective-permute-start | bytes 688136 | tf_op jit(solution)/shard_map/ppermute | solution.py:46
  184.2 32.3 %collective-permute-start.26 = (bf16[128,896]{1,0:T(8,128)(2,1)S(1)}, bf16[128,896]{1,0:T(8,128)(2,1)S(1)}, u32[]{:S(2)}, u32[]{:S(2)}) collective-permute-start(bf16[128,896]{1,0:T(8,128)(2,1)S(1)} %get-tuple-element.60), channel_id=1, source_target_pairs={{0,2},{1,3},{2,0},{3,1},{4,6},{5,7},{6,4},{7,5},{8,10},{9,11},{10,... | collective-permute-start | bytes 688136 | tf_op jit(solution)/shard_map/ppermute | solution.py:46
  184.9 31.7 %collective-permute-start.27 = (bf16[128,896]{1,0:T(8,128)(2,1)S(1)}, bf16[128,896]{1,0:T(8,128)(2,1)S(1)}, u32[]{:S(2)}, u32[]{:S(2)}) collective-permute-start(bf16[128,896]{1,0:T(8,128)(2,1)S(1)} %get-tuple-element.59), channel_id=1, source_target_pairs={{0,3},{1,2},{2,1},{3,0},{4,7},{5,6},{6,5},{7,4},{8,11},{9,10},{10,... | collective-permute-start | bytes 688136 | tf_op jit(solution)/shard_map/ppermute | solution.py:46
  205.6 16.7 %collective-permute-start.33 = (bf16[384,896]{1,0:T(8,128)(2,1)S(1)}, bf16[384,896]{1,0:T(8,128)(2,1)S(1)}, u32[]{:S(2)}, u32[]{:S(2)}) collective-permute-start(bf16[384,896]{1,0:T(8,128)(2,1)S(1)} %pad_maximum_fusion.14), channel_id=1, source_target_pairs={{0,8},{4,12},{8,0},{12,4},{1,9},{5,13},{9,1},{13,5},{2,10},{6,14},... | collective-permute-start | bytes 2064392 | tf_op jit(solution)/shard_map/ppermute | solution.py:46
  207.5 23.0 %collective-permute-start.30 = (bf16[384,1024]{1,0:T(8,128)(2,1)S(1)}, bf16[384,1024]{1,0:T(8,128)(2,1)S(1)}, u32[]{:S(2)}, u32[]{:S(2)}) collective-permute-start(bf16[384,1024]{1,0:T(8,128)(2,1)S(1)} %add_convert_fusion.1), channel_id=1, source_target_pairs={{1,0},{2,3},{5,4},{6,7},{9,8},{10,11},{13,12},{14,15},{17,16},{18,... | collective-permute-start | bytes 2359304 | tf_op jit(solution)/shard_map/ppermute | solution.py:76
  242.8 19.2 %collective-permute-start.36 = (bf16[128,896]{1,0:T(8,128)(2,1)S(1)}, bf16[128,896]{1,0:T(8,128)(2,1)S(1)}, u32[]{:S(2)}, u32[]{:S(2)}) collective-permute-start(bf16[128,896]{1,0:T(8,128)(2,1)S(1)} %get-tuple-element.56), channel_id=1, source_target_pairs={{0,2},{1,3},{2,0},{3,1},{4,6},{5,7},{6,4},{7,5},{8,10},{9,11},{10,... | collective-permute-start | bytes 688136 | tf_op jit(solution)/shard_map/ppermute | solution.py:46
  (25 other events, 400.6 us)

commit v4 on v3

--- a/solution.py
+++ b/solution.py
@@ -7,16 +7,14 @@
 BF16 = jnp.bfloat16
 GROUPS = 4
 CODE_ROWS = 16
-AHEAD = 1
-ITEMS = (("pre", (0,)), ("pre", (2,)), ("pre", (3,)), ("pre", (1,)), ("hid", (2, 3)), ("hid", (0, 1)))
-
-
-def route_places(routes, experts, capacity):
-    flat_ids = routes.reshape(-1)
-    onehot = (flat_ids[:, None] == jnp.arange(experts, dtype=jnp.int32)[None, :]).astype(jnp.int32)
-    before = jnp.cumsum(onehot, axis=0) - onehot
-    slot_pos = jnp.sum(before * onehot, axis=1)
-    return flat_ids * capacity + slot_pos
+ITEMS = (('pre', (0,)), ('pre', (2,)), ('pre', (3,)), ('pre', (1,)), ('hid', (2, 3)), ('hid', (0, 1)))
+
+
+def route_codes(routes, capacity):
+    ids = routes.reshape(-1)
+    place = jnp.arange(ids.shape[0], dtype=jnp.int32)
+    before = (ids[:, None] == ids[None, :]) & (place[:, None] < place[None, :])
+    return ids * capacity + jnp.sum(before.astype(jnp.int32), axis=0)
 
 
 def across(left, right):
@@ -57,15 +55,16 @@
         self.axis, self.count, self.own, self.total = axis, lax.axis_size(axis), own, own
         self.got = None
 
-    def inward(self):
+    def inward(self, *others):
         for hop in range(self.count // 2 - 1):
             pairs = [(hop, hop + 1), (self.count - 1 - hop, self.count - 2 - hop)]
             arrived = lax.ppermute(self.total.astype(BF16), self.axis, pairs)
-            self.total = self.total + arrived.astype(F32)
+            self.total = self.total + after(arrived, *others).astype(F32)
         return arrived
 
-    def middle(self):
+    def middle(self, *others):
         mid = self.count // 2
+        self.total = after(self.total, *others)
         self.got = lax.ppermute(self.total.astype(BF16), self.axis, [(mid - 1, mid), (mid, mid - 1)])
         return self.got
 
@@ -73,8 +72,10 @@
         got = after(self.got, *others)
         for hop in reversed(range(self.count // 2 - 1)):
             pairs = [(hop + 1, hop), (self.count - 2 - hop, self.count - 1 - hop)]
-            got = got + lax.ppermute((self.own + got.astype(F32)).astype(BF16), self.axis, pairs)
+            arrived = lax.ppermute((self.own + got.astype(F32)).astype(BF16), self.axis, pairs)
+            got = got + arrived
         self.got = got
+        return arrived
 
     def result(self, *others):
         return self.total + after(self.got, *others).astype(F32)
@@ -110,19 +111,25 @@
         got = {k: features.swap(after(pieces[k], *earlier), k) for k in distances}
         return [pieces[0]] + [got[k] for k in range(1, n_dp)]
 
-    codes = route_places(routes, n_exp, capacity).astype(BF16)
+    codes = route_codes(routes, capacity).astype(BF16)
     tail = jnp.zeros((CODE_ROWS, part), BF16) + jnp.pad(codes, (0, part - tok_count))[None, :]
     weighted = (gates * cotangent.astype(F32)).astype(BF16)
     got_rows = by_features(tokens, tail)
     got_grads = by_features(weighted, None)
 
-    codes = jnp.stack([piece[tok_count, :tok_count] for piece in got_rows]).astype(jnp.int32)
+    gathered = jnp.concatenate(got_rows, axis=0)
+    codes = gathered.reshape(n_dp, tok_count + CODE_ROWS, part)[:, tok_count, :tok_count].astype(jnp.int32)
     places = ((codes // capacity) ^ me) * chunk + blocks[:, None] * capacity + codes % capacity
-    select = (jnp.arange(n_exp * chunk, dtype=jnp.int32)[:, None] == places.reshape(-1)[None, :]).astype(BF16)
-
-    def dispatch(pieces):
-        gathered = jnp.concatenate([piece[:tok_count] for piece in pieces], axis=0)
-        rows = jnp.dot(select, gathered, preferred_element_type=F32).astype(BF16)
+
+    def chooser(places):
+        return (jnp.arange(n_exp * chunk, dtype=jnp.int32)[:, None] == places.reshape(-1)[None, :]).astype(BF16)
+
+    select = chooser(places)
+    select_whole = chooser(places[blocks])
+    select_tailed = chooser(jnp.pad(places, ((0, 0), (0, CODE_ROWS)), constant_values=-1))
+
+    def dispatch(chosen, gathered):
+        rows = jnp.dot(chosen, gathered, preferred_element_type=F32).astype(BF16)
         return rows.reshape(n_exp, chunk, part)
 
     def exchange(blocks, bits, *others):
@@ -144,10 +151,15 @@
     def blocks_of(values):
         return [None if v is None else v[i * chunk : (i + 1) * chunk] for v in values for i in range(per_group)]
 
-    def pick(values):
-        return over_rows(select, jnp.concatenate(values, axis=0)).astype(BF16).reshape(n_dp, tok_count, part)
+    def pick(values, select=select):
+        return over_rows(select, jnp.concatenate(values, axis=0)).astype(BF16)
+
+    def give_back_whole(picked):
+        got = lax.all_to_all(picked.reshape(n_dp, tok_count, part), "dp", split_axis=0, concat_axis=0, tiled=False)
+        return [got] * n_dp
 
     def give_back(picked):
+        picked = picked.reshape(n_dp, tok_count, part)
         got = {k: features.swap(picked[k], k) for k in distances}
         return [picked[0]] + [got[k] for k in range(1, n_dp)]
 
@@ -157,8 +169,8 @@
             result = lax.dynamic_update_slice(result, piece, (0, (here ^ k) * part))
         return result
 
-    rows = grouped(exchange(dispatch(got_rows), bits)[0])
-    sent_grads = dispatch(got_grads)
+    rows = grouped(exchange(dispatch(select_tailed, gathered), bits)[0])
+    sent_grads = dispatch(select, jnp.concatenate(got_grads, axis=0))
     grads = None
     sums, pre = [], [None] * GROUPS
     hidden, out, both, back = [None] * GROUPS, [None] * GROUPS, [None] * GROUPS, [None] * GROUPS
@@ -185,46 +197,50 @@
     def start(item):
         kind, gs = ITEMS[item]
         moved = joined([(rows if kind == "pre" else grads)[g] for g in gs])
-        moved = after(moved, inward[item - AHEAD] if item >= AHEAD else got_grads[1])
+        ahead = 2
+        moved = after(moved, inward[item - ahead]) if item >= ahead else after(moved, got_grads[1])
         sums.append(LineSum("dp", jnp.dot(moved, w_both if kind == "pre" else w_down, preferred_element_type=F32)))
-        inward.append(sums[item].inward())
+        inward.append(sums[item].inward(*inward[-1:]))
         middle.append(sums[item].middle())
 
-    inward, middle = [], []
+    inward, middle, outward = [], [], []
     start(0)
     grads = grouped(exchange(sent_grads, bits, inward[0])[0])
     start(1)
-    sums[0].outward()
+    outward.append(sums[0].outward())
     start(2)
-    sums[1].outward()
+    outward.append(sums[1].outward(middle[0]))
     finish(0)
     start(3)
-    sums[2].outward()
+    outward.append(sums[2].outward(middle[1]))
     finish(1)
     start(4)
-    sums[3].outward()
+    outward.append(sums[3].outward(middle[2]))
     finish(2)
     halfway, half_o = exchange(blocks_of(out), bits[:1])
     start(5)
-    sums[4].outward()
+    outward.append(sums[4].outward(middle[3]))
     finish(3, inward[4])
-    here_blocks = blocks_of(out)
-    out, arrived = exchange([block if half is None else half for block, half in zip(here_blocks, halfway)], bits[1:])
-    sums[5].outward()
+    now = blocks_of(out)
+    out, late_o = exchange([block if half is None else half for block, half in zip(now, halfway)], bits[1:])
+    outward.append(sums[5].outward(middle[4]))
+    picked = pick(out)
+    sent_out = give_back(picked)
     finish(4, inward[5], half_o)
-    halfway, arrived = exchange(blocks_of(back), bits[:1])
-    out = give_back(pick(out))
-    finish(5, out[1])
-    here_blocks = blocks_of(back)
-    back, _ = exchange([block if half is None else half for block, half in zip(here_blocks, halfway)], bits[1:], *out[1:])
-    picked = pick(back)
+    halfway, half_g = exchange(blocks_of(back), bits[:1])
+    finish(5, sent_out[1])
+    now = blocks_of(back)
+    moved, late_g = exchange([block if half is None else half for block, half in zip(now, halfway)], bits[1:])
+    picked = pick(moved)
+    all_both, all_hidden = jnp.concatenate(both, axis=0), jnp.concatenate(hidden, axis=0)
+    all_both, all_hidden = lax.optimization_barrier((all_both, all_hidden))
     back = give_back(picked)
-
+    out = sent_out
+
+    all_both, all_hidden = after((all_both, all_hidden), back[1])
     mixed = placed([(piece.astype(F32) * gates).astype(BF16) for piece in out])
     token_grad = placed(back)
     all_rows, all_grads = jnp.concatenate(rows, axis=0), jnp.concatenate(grads, axis=0)
-    all_both, all_hidden = jnp.concatenate(both, axis=0), jnp.concatenate(hidden, axis=0)
-    all_both, all_hidden, _ = lax.optimization_barrier((all_both, all_hidden, picked))
     gate_grad = over_rows(all_rows, all_both[:, :hidden_units]).astype(BF16)
     up_grad = over_rows(all_rows, all_both[:, hidden_units:]).astype(BF16)
     down_grad = over_rows(all_grads, all_hidden).astype(BF16)

time: 266 us -> 250 us (0.940)
  waiting for transfers between devices: 144 us -> 129 us
  local copies, waits for them, and re-layouts: 9.68 us -> 6.94 us
    ppermute x20, waiting for transfers between devices: 76.5 us -> 41.7 us  [send(): got = lax.ppermute(self.turn(value), self.axis, pairs)]
    ppermute x6, waiting for transfers between devices: 24.2 us -> 48.3 us  [inward(): arrived = lax.ppermute(self.total.astype(BF16), self.axis, pairs)]
    slice x6 -> x0, local copies, waits for them, and re-layouts: 4.89 us -> none  [the longest x3 2.87 us: dispatch(): gathered = jnp.concatenate([piece[:tok_count] for piece in pieces], axis=0)]
    ppermute x6, waiting for transfers between devices: 43.1 us -> 38.6 us  [outward(): lax.ppermute((self.own + got.astype(F32)).astype(BF16), self.axis, pairs)]
  transfers between devices with their start and end apart: 38 -> 38, of which waited for: 20 -> 20; matrix products, arithmetic and copies ran while one was open for 14% -> 17% of each run, Pallas kernels for 0% -> 0%
where the time goes in v4:
time: 250 us; the launch traced here: 248 us
  waiting for transfers between devices  129 us (52%)
  starting transfers between devices  66.3 us (27%)
  matrix products  28.9 us (12%)
  other arithmetic  15.9 us (6%)
  local copies, waits for them, and re-layouts  6.94 us (3%)
    ppermute x6, waiting for transfers between devices, inward(): arrived = lax.ppermute(self.total.astype(BF16), self.axis, pairs)  48.3 us
    ppermute x20, waiting for transfers between devices, send(): got = lax.ppermute(self.turn(value), self.axis, pairs)  41.7 us
    ppermute x6, waiting for transfers between devices, outward(): lax.ppermute((self.own + got.astype(F32)).astype(BF16), self.axis, pairs)  38.6 us
    ppermute x6, starting transfers between devices, inward(): arrived = lax.ppermute(self.total.astype(BF16), self.axis, pairs)  29.9 us
    ppermute x20, starting transfers between devices, send(): got = lax.ppermute(self.turn(value), self.axis, pairs)  24.1 us
    dot_general x5, matrix products, over_rows(): lax.dot_general(left, right, (((0,), (0,)), ((), ())), preferred_element_...  10.7 us
    dot_general x8, matrix products, across(): lax.dot_general(left, right, (((1,), (1,)), ((), ())), preferred_element_...  8.65 us
    ppermute x6, starting transfers between devices, outward(): lax.ppermute((self.own + got.astype(F32)).astype(BF16), self.axis, pairs)  7.97 us
  transfers between devices with their start and end apart: 38, of which 20 were waited for; matrix products, arithmetic and copies ran while one was open for 17% of the time, Pallas kernels for 0%

profile of v4, /device:TPU:0, one launch (start us, length us, event | category | flops | bytes accessed | tf_op | source)
XLA Modules:
  0.0 248.3 jit_solution(14447923508019595744)
XLA Ops:
  5.2 3.0 %collective-permute-start = (bf16[144,896]{1,0:T(8,128)(2,1)}, bf16[144,896]{1,0:T(8,128)(2,1)S(1)}, u32[]{:S(2)}, u32[]{:S(2)}) collective-permute-start(bf16[144,896]{1,0:T(8,128)(2,1)} %get-tuple-element.111), channel_id=1, source_target_pairs={{0,1},{1,0},{2,3},{3,2},{4,5},{5,4},{6,7},{7,6},{8,9},{9,8},{10,11... | collective-permute-start | bytes 774152 | tf_op jit(solution)/shard_map/ppermute | solution.py:44
  11.8 7.6 %collective-permute-done = bf16[144,896]{1,0:T(8,128)(2,1)S(1)} collective-permute-done((bf16[144,896]{1,0:T(8,128)(2,1)}, bf16[144,896]{1,0:T(8,128)(2,1)S(1)}, u32[]{:S(2)}, u32[]{:S(2)}) %collective-permute-start) | collective-permute-done | bytes 258080 | tf_op jit(solution)/shard_map/ppermute | solution.py:44
  20.2 9.4 %collective-permute-done.1 = bf16[144,896]{1,0:T(8,128)(2,1)S(1)} collective-permute-done((bf16[144,896]{1,0:T(8,128)(2,1)}, bf16[144,896]{1,0:T(8,128)(2,1)S(1)}, u32[]{:S(2)}, u32[]{:S(2)}) %collective-permute-start.1) | collective-permute-done | bytes 258080 | tf_op jit(solution)/shard_map/ppermute | solution.py:44
  35.5 4.0 %collective-permute-start.3 = (bf16[128,896]{1,0:T(8,128)(2,1)S(1)}, bf16[128,896]{1,0:T(8,128)(2,1)S(1)}, u32[]{:S(2)}, u32[]{:S(2)}) collective-permute-start(bf16[128,896]{1,0:T(8,128)(2,1)S(1)} %get-tuple-element.33), channel_id=1, source_target_pairs={{0,1},{1,0},{2,3},{3,2},{4,5},{5,4},{6,7},{7,6},{8,9},{9,8},{10,11... | collective-permute-start | bytes 688136 | tf_op jit(solution)/shard_map/ppermute | solution.py:44
  45.5 4.4 %collective-permute-start.4 = (bf16[192,2048]{1,0:T(8,128)(2,1)S(1)}, bf16[192,2048]{1,0:T(8,128)(2,1)S(1)}, u32[]{:S(2)}, u32[]{:S(2)}) collective-permute-start(bf16[192,2048]{1,0:T(8,128)(2,1)S(1)} %get-tuple-element.112), channel_id=1, source_target_pairs={{0,1},{3,2},{4,5},{7,6},{8,9},{11,10},{12,13},{15,14},{16,17},{19,... | collective-permute-start | bytes 2359304 | tf_op jit(solution)/shard_map/ppermute | solution.py:61
  49.9 3.6 %collective-permute-done.16 = bf16[128,896]{1,0:T(8,128)(2,1)S(1)} collective-permute-done((bf16[128,896]{1,0:T(8,128)(2,1)S(1)}, bf16[128,896]{1,0:T(8,128)(2,1)S(1)}, u32[]{:S(2)}, u32[]{:S(2)}) %collective-permute-start.16) | collective-permute-done | bytes 229408 | tf_op jit(solution)/shard_map/ppermute | solution.py:44
  53.5 7.8 %collective-permute-done.15 = bf16[128,896]{1,0:T(8,128)(2,1)S(1)} collective-permute-done((bf16[128,896]{1,0:T(8,128)(2,1)S(1)}, bf16[128,896]{1,0:T(8,128)(2,1)S(1)}, u32[]{:S(2)}, u32[]{:S(2)}) %collective-permute-start.15) | collective-permute-done | bytes 229408 | tf_op jit(solution)/shard_map/ppermute | solution.py:44
  65.3 6.3 %collective-permute-done.4 = bf16[192,2048]{1,0:T(8,128)(2,1)S(1)} collective-permute-done((bf16[192,2048]{1,0:T(8,128)(2,1)S(1)}, bf16[192,2048]{1,0:T(8,128)(2,1)S(1)}, u32[]{:S(2)}, u32[]{:S(2)}) %collective-permute-start.4) | collective-permute-done | bytes 786464 | tf_op jit(solution)/shard_map/ppermute | solution.py:61
  76.0 7.2 %collective-permute-start.11 = (bf16[192,2048]{1,0:T(8,128)(2,1)S(1)}, bf16[192,2048]{1,0:T(8,128)(2,1)S(1)}, u32[]{:S(2)}, u32[]{:S(2)}) collective-permute-start(bf16[192,2048]{1,0:T(8,128)(2,1)S(1)} %get-tuple-element.114), channel_id=1, source_target_pairs={{0,1},{3,2},{4,5},{7,6},{8,9},{11,10},{12,13},{15,14},{16,17},{19,... | collective-permute-start | bytes 2359304 | tf_op jit(solution)/shard_map/ppermute | solution.py:61
  83.2 5.2 %collective-permute-done.9 = bf16[192,2048]{1,0:T(8,128)(2,1)S(1)} collective-permute-done((bf16[192,2048]{1,0:T(8,128)(2,1)S(1)}, bf16[192,2048]{1,0:T(8,128)(2,1)S(1)}, u32[]{:S(2)}, u32[]{:S(2)}) %collective-permute-start.9) | collective-permute-done | bytes 786464 | tf_op jit(solution)/shard_map/ppermute | solution.py:61
  90.5 7.9 %collective-permute-start.10 = (bf16[192,2048]{1,0:T(8,128)(2,1)S(1)}, bf16[192,2048]{1,0:T(8,128)(2,1)S(1)}, u32[]{:S(2)}, u32[]{:S(2)}) collective-permute-start(bf16[192,2048]{1,0:T(8,128)(2,1)S(1)} %get-tuple-element.118), channel_id=1, source_target_pairs={{0,1},{3,2},{4,5},{7,6},{8,9},{11,10},{12,13},{15,14},{16,17},{19,... | collective-permute-start | bytes 2359304 | tf_op jit(solution)/shard_map/ppermute | solution.py:61
  100.2 5.1 %collective-permute-done.11 = bf16[192,2048]{1,0:T(8,128)(2,1)S(1)} collective-permute-done((bf16[192,2048]{1,0:T(8,128)(2,1)S(1)}, bf16[192,2048]{1,0:T(8,128)(2,1)S(1)}, u32[]{:S(2)}, u32[]{:S(2)}) %collective-permute-start.11) | collective-permute-done | bytes 786464 | tf_op jit(solution)/shard_map/ppermute | solution.py:61
  107.9 12.7 %collective-permute-done.10 = bf16[192,2048]{1,0:T(8,128)(2,1)S(1)} collective-permute-done((bf16[192,2048]{1,0:T(8,128)(2,1)S(1)}, bf16[192,2048]{1,0:T(8,128)(2,1)S(1)}, u32[]{:S(2)}, u32[]{:S(2)}) %collective-permute-start.10) | collective-permute-done | bytes 786464 | tf_op jit(solution)/shard_map/ppermute | solution.py:61
  122.7 7.4 %collective-permute-start.19 = (bf16[384,1024]{1,0:T(8,128)(2,1)S(1)}, bf16[384,1024]{1,0:T(8,128)(2,1)S(1)}, u32[]{:S(2)}, u32[]{:S(2)}) collective-permute-start(bf16[384,1024]{1,0:T(8,128)(2,1)S(1)} %get-tuple-element.120), channel_id=1, source_target_pairs={{0,1},{3,2},{4,5},{7,6},{8,9},{11,10},{12,13},{15,14},{16,17},{19,... | collective-permute-start | bytes 2359304 | tf_op jit(solution)/shard_map/ppermute | solution.py:61
  141.0 6.8 %collective-permute-done.19 = bf16[384,1024]{1,0:T(8,128)(2,1)S(1)} collective-permute-done((bf16[384,1024]{1,0:T(8,128)(2,1)S(1)}, bf16[384,1024]{1,0:T(8,128)(2,1)S(1)}, u32[]{:S(2)}, u32[]{:S(2)}) %collective-permute-start.19) | collective-permute-done | bytes 786464 | tf_op jit(solution)/shard_map/ppermute | solution.py:61
  148.9 12.2 %collective-permute-done.28 = bf16[384,1024]{1,0:T(8,128)(2,1)S(1)} collective-permute-done((bf16[384,1024]{1,0:T(8,128)(2,1)S(1)}, bf16[384,1024]{1,0:T(8,128)(2,1)S(1)}, u32[]{:S(2)}, u32[]{:S(2)}) %collective-permute-start.28) | collective-permute-done | bytes 786464 | tf_op jit(solution)/shard_map/ppermute | solution.py:61
  165.4 5.8 %collective-permute-done.14 = bf16[192,2048]{1,0:T(8,128)(2,1)S(1)} collective-permute-done((bf16[192,2048]{1,0:T(8,128)(2,1)S(1)}, bf16[192,2048]{1,0:T(8,128)(2,1)S(1)}, u32[]{:S(2)}, u32[]{:S(2)}) %collective-permute-start.14) | collective-permute-done | bytes 786464 | tf_op jit(solution)/shard_map/ppermute | solution.py:75
  178.0 17.4 %collective-permute-done.32 = bf16[384,1024]{1,0:T(8,128)(2,1)S(1)} collective-permute-done((bf16[384,1024]{1,0:T(8,128)(2,1)S(1)}, bf16[384,1024]{1,0:T(8,128)(2,1)S(1)}, u32[]{:S(2)}, u32[]{:S(2)}) %collective-permute-start.32) | collective-permute-done | bytes 786464 | tf_op jit(solution)/shard_map/ppermute | solution.py:75
  202.9 12.9 %collective-permute-done.31 = bf16[384,1024]{1,0:T(8,128)(2,1)S(1)} collective-permute-done((bf16[384,1024]{1,0:T(8,128)(2,1)S(1)}, bf16[384,1024]{1,0:T(8,128)(2,1)S(1)}, u32[]{:S(2)}, u32[]{:S(2)}) %collective-permute-start.31) | collective-permute-done | bytes 786464 | tf_op jit(solution)/shard_map/ppermute | solution.py:75
  223.0 3.4 %collective-permute-done.26 = bf16[128,896]{1,0:T(8,128)(2,1)S(1)} collective-permute-done((bf16[128,896]{1,0:T(8,128)(2,1)S(1)}, bf16[128,896]{1,0:T(8,128)(2,1)S(1)}, u32[]{:S(2)}, u32[]{:S(2)}) %collective-permute-start.26) | collective-permute-done | bytes 229408 | tf_op jit(solution)/shard_map/ppermute | solution.py:44
  233.8 4.4 %collective-permute-done.35 = bf16[128,896]{1,0:T(8,128)(2,1)S(1)} collective-permute-done((bf16[128,896]{1,0:T(8,128)(2,1)S(1)}, bf16[128,896]{1,0:T(8,128)(2,1)S(1)}, u32[]{:S(2)}, u32[]{:S(2)}) %collective-permute-start.35) | collective-permute-done | bytes 229408 | tf_op jit(solution)/shard_map/ppermute | solution.py:44
  238.2 2.9 %convert_bitcast_fusion.2 = bf16[1,896,1024]{2,1,0:T(8,128)(2,1)} fusion(bf16[768,2048]{1,0:T(8,128)(2,1)S(1)} %pad_maximum_fusion.1, bf16[192,896]{1,0:T(8,128)(2,1)S(1)} %get-tuple-element.37, bf16[192,896]{1,0:T(8,128)(2,1)S(1)} %get-tuple-element.35, bf16[192,896]{1,0:T(8,128)(2,1)S(1)} %get-tuple-element.36, bf16[192,896]{1,0:T(8,128)(2,1)S(1)} %get-tuple-element.34), kind=kOutput, calls=%fused_computation.18 | convolution fusion | flops 1415708672 | bytes 4784128 | tf_op jit(solution)/shard_map/dot_general | solution.py:25
  241.0 2.9 %convert_bitcast_fusion.1 = bf16[1,896,1024]{2,1,0:T(8,128)(2,1)} fusion(bf16[768,2048]{1,0:T(8,128)(2,1)S(1)} %pad_maximum_fusion.1, bf16[192,896]{1,0:T(8,128)(2,1)S(1)} %get-tuple-element.37, bf16[192,896]{1,0:T(8,128)(2,1)S(1)} %get-tuple-element.35, bf16[192,896]{1,0:T(8,128)(2,1)S(1)} %get-tuple-element.36, bf16[192,896]{1,0:T(8,128)(2,1)S(1)} %get-tuple-element.34), kind=kOutput, calls=%fused_computation.17 | convolution fusion | flops 1415708672 | bytes 4784128 | tf_op jit(solution)/shard_map/dot_general | solution.py:25
  243.9 2.9 %convert_bitcast_fusion = bf16[1,896,1024]{2,1,0:T(8,128)(2,1)} fusion(bf16[768,1024]{1,0:T(8,128)(2,1)S(1)} %pad_maximum_fusion.2, bf16[192,896]{1,0:T(8,128)(2,1)S(1)} %get-tuple-element.98, bf16[192,896]{1,0:T(8,128)(2,1)S(1)} %get-tuple-element.103, bf16[192,896]{1,0:T(8,128)(2,1)S(1)} %get-tuple-element.97, bf16[192,896]{1,0:T(8,128)(2,1)S(1)} %get-tuple-element.73), kind=kOutput, calls=%fused_computation.16 | convolution fusion | flops 1415708672 | bytes 4784128 | tf_op jit(solution)/shard_map/dot_general | solution.py:25
  (179 shorter events, 83.3 us)
Async XLA Ops:
  8.2 21.3 %collective-permute-start.1 = (bf16[144,896]{1,0:T(8,128)(2,1)}, bf16[144,896]{1,0:T(8,128)(2,1)S(1)}, u32[]{:S(2)}, u32[]{:S(2)}) collective-permute-start(bf16[144,896]{1,0:T(8,128)(2,1)} %get-tuple-element.110), channel_id=1, source_target_pairs={{0,2},{1,3},{2,0},{3,1},{4,6},{5,7},{6,4},{7,5},{8,10},{9,11},{10,... | collective-permute-start | bytes 774152 | tf_op jit(solution)/shard_map/ppermute | solution.py:44
  10.8 19.4 %collective-permute-start.2 = (bf16[144,896]{1,0:T(8,128)(2,1)}, bf16[144,896]{1,0:T(8,128)(2,1)S(1)}, u32[]{:S(2)}, u32[]{:S(2)}) collective-permute-start(bf16[144,896]{1,0:T(8,128)(2,1)} %get-tuple-element.109), channel_id=1, source_target_pairs={{0,3},{1,2},{2,1},{3,0},{4,7},{5,6},{6,5},{7,4},{8,11},{9,10},{10,... | collective-permute-start | bytes 774152 | tf_op jit(solution)/shard_map/ppermute | solution.py:44
  39.6 22.8 %collective-permute-start.7 = (bf16[384,896]{1,0:T(8,128)(2,1)S(1)}, bf16[384,896]{1,0:T(8,128)(2,1)S(1)}, u32[]{:S(2)}, u32[]{:S(2)}) collective-permute-start(bf16[384,896]{1,0:T(8,128)(2,1)S(1)} %concatenate.104), channel_id=1, source_target_pairs={{0,8},{4,12},{8,0},{12,4},{1,9},{5,13},{9,1},{13,5},{2,10},{6,14},... | collective-permute-start | bytes 2064392 | tf_op jit(solution)/shard_map/ppermute | solution.py:44
  45.5 26.1 %collective-permute-start.4 = (bf16[192,2048]{1,0:T(8,128)(2,1)S(1)}, bf16[192,2048]{1,0:T(8,128)(2,1)S(1)}, u32[]{:S(2)}, u32[]{:S(2)}) collective-permute-start(bf16[192,2048]{1,0:T(8,128)(2,1)S(1)} %get-tuple-element.112), channel_id=1, source_target_pairs={{0,1},{3,2},{4,5},{7,6},{8,9},{11,10},{12,13},{15,14},{16,17},{19,... | collective-permute-start | bytes 2359304 | tf_op jit(solution)/shard_map/ppermute | solution.py:61
  63.7 24.7 %collective-permute-start.9 = (bf16[192,2048]{1,0:T(8,128)(2,1)S(1)}, bf16[192,2048]{1,0:T(8,128)(2,1)S(1)}, u32[]{:S(2)}, u32[]{:S(2)}) collective-permute-start(bf16[192,2048]{1,0:T(8,128)(2,1)S(1)} %get-tuple-element.116), channel_id=1, source_target_pairs={{0,1},{3,2},{4,5},{7,6},{8,9},{11,10},{12,13},{15,14},{16,17},{19,... | collective-permute-start | bytes 2359304 | tf_op jit(solution)/shard_map/ppermute | solution.py:61
  71.9 26.7 %collective-permute-start.5 = (bf16[192,2048]{1,0:T(8,128)(2,1)S(1)}, bf16[192,2048]{1,0:T(8,128)(2,1)S(1)}, u32[]{:S(2)}, u32[]{:S(2)}) collective-permute-start(bf16[192,2048]{1,0:T(8,128)(2,1)S(1)} %convert_element_type.246), channel_id=1, source_target_pairs={{1,2},{2,1},{5,6},{6,5},{9,10},{10,9},{13,14},{14,13},{17,18},{18,... | collective-permute-start | bytes 2359304 | tf_op jit(solution)/shard_map/ppermute | solution.py:68
  72.6 25.8 %collective-permute-start.17 = (bf16[384,896]{1,0:T(8,128)(2,1)S(1)}, bf16[384,896]{1,0:T(8,128)(2,1)S(1)}, u32[]{:S(2)}, u32[]{:S(2)}) collective-permute-start(bf16[384,896]{1,0:T(8,128)(2,1)S(1)} %concatenate.105), channel_id=1, source_target_pairs={{0,8},{4,12},{8,0},{12,4},{1,9},{5,13},{9,1},{13,5},{2,10},{6,14},... | collective-permute-start | bytes 2064392 | tf_op jit(solution)/shard_map/ppermute | solution.py:44
  76.0 29.3 %collective-permute-start.11 = (bf16[192,2048]{1,0:T(8,128)(2,1)S(1)}, bf16[192,2048]{1,0:T(8,128)(2,1)S(1)}, u32[]{:S(2)}, u32[]{:S(2)}) collective-permute-start(bf16[192,2048]{1,0:T(8,128)(2,1)S(1)} %get-tuple-element.114), channel_id=1, source_target_pairs={{0,1},{3,2},{4,5},{7,6},{8,9},{11,10},{12,13},{15,14},{16,17},{19,... | collective-permute-start | bytes 2359304 | tf_op jit(solution)/shard_map/ppermute | solution.py:61
  90.5 30.0 %collective-permute-start.10 = (bf16[192,2048]{1,0:T(8,128)(2,1)S(1)}, bf16[192,2048]{1,0:T(8,128)(2,1)S(1)}, u32[]{:S(2)}, u32[]{:S(2)}) collective-permute-start(bf16[192,2048]{1,0:T(8,128)(2,1)S(1)} %get-tuple-element.118), channel_id=1, source_target_pairs={{0,1},{3,2},{4,5},{7,6},{8,9},{11,10},{12,13},{15,14},{16,17},{19,... | collective-permute-start | bytes 2359304 | tf_op jit(solution)/shard_map/ppermute | solution.py:61
  98.6 23.0 %collective-permute-start.18 = (bf16[384,896]{1,0:T(8,128)(2,1)S(1)}, bf16[384,896]{1,0:T(8,128)(2,1)S(1)}, u32[]{:S(2)}, u32[]{:S(2)}) collective-permute-start(bf16[384,896]{1,0:T(8,128)(2,1)S(1)} %pad_maximum_fusion.9), channel_id=1, source_target_pairs={{0,4},{4,0},{8,12},{12,8},{1,5},{5,1},{9,13},{13,9},{2,6},{6,2},{1... | collective-permute-start | bytes 2064392 | tf_op jit(solution)/shard_map/ppermute | solution.py:44
  98.9 32.2 %collective-permute-start.6 = (bf16[192,2048]{1,0:T(8,128)(2,1)S(1)}, bf16[192,2048]{1,0:T(8,128)(2,1)S(1)}, u32[]{:S(2)}, u32[]{:S(2)}) collective-permute-start(bf16[192,2048]{1,0:T(8,128)(2,1)S(1)} %add_convert_fusion.5), channel_id=1, source_target_pairs={{1,0},{2,3},{5,4},{6,7},{9,8},{10,11},{13,12},{14,15},{17,16},{18,... | collective-permute-start | bytes 2359304 | tf_op jit(solution)/shard_map/ppermute | solution.py:75
  105.6 28.4 %collective-permute-start.13 = (bf16[192,2048]{1,0:T(8,128)(2,1)S(1)}, bf16[192,2048]{1,0:T(8,128)(2,1)S(1)}, u32[]{:S(2)}, u32[]{:S(2)}) collective-permute-start(bf16[192,2048]{1,0:T(8,128)(2,1)S(1)} %convert_element_type.258), channel_id=1, source_target_pairs={{1,2},{2,1},{5,6},{6,5},{9,10},{10,9},{13,14},{14,13},{17,18},{18,... | collective-permute-start | bytes 2359304 | tf_op jit(solution)/shard_map/ppermute | solution.py:68
  106.6 31.4 %collective-permute-start.21 = (bf16[192,2048]{1,0:T(8,128)(2,1)S(1)}, bf16[192,2048]{1,0:T(8,128)(2,1)S(1)}, u32[]{:S(2)}, u32[]{:S(2)}) collective-permute-start(bf16[192,2048]{1,0:T(8,128)(2,1)S(1)} %add_convert_fusion.3), channel_id=1, source_target_pairs={{1,0},{2,3},{5,4},{6,7},{9,8},{10,11},{13,12},{14,15},{17,16},{18,... | collective-permute-start | bytes 2359304 | tf_op jit(solution)/shard_map/ppermute | solution.py:75
  122.7 25.1 %collective-permute-start.19 = (bf16[384,1024]{1,0:T(8,128)(2,1)S(1)}, bf16[384,1024]{1,0:T(8,128)(2,1)S(1)}, u32[]{:S(2)}, u32[]{:S(2)}) collective-permute-start(bf16[384,1024]{1,0:T(8,128)(2,1)S(1)} %get-tuple-element.120), channel_id=1, source_target_pairs={{0,1},{3,2},{4,5},{7,6},{8,9},{11,10},{12,13},{15,14},{16,17},{19,... | collective-permute-start | bytes 2359304 | tf_op jit(solution)/shard_map/ppermute | solution.py:61
  131.1 30.0 %collective-permute-start.28 = (bf16[384,1024]{1,0:T(8,128)(2,1)S(1)}, bf16[384,1024]{1,0:T(8,128)(2,1)S(1)}, u32[]{:S(2)}, u32[]{:S(2)}) collective-permute-start(bf16[384,1024]{1,0:T(8,128)(2,1)S(1)} %get-tuple-element.122), channel_id=1, source_target_pairs={{0,1},{3,2},{4,5},{7,6},{8,9},{11,10},{12,13},{15,14},{16,17},{19,... | collective-permute-start | bytes 2359304 | tf_op jit(solution)/shard_map/ppermute | solution.py:61
  134.2 28.1 %collective-permute-start.22 = (bf16[192,2048]{1,0:T(8,128)(2,1)S(1)}, bf16[192,2048]{1,0:T(8,128)(2,1)S(1)}, u32[]{:S(2)}, u32[]{:S(2)}) collective-permute-start(bf16[192,2048]{1,0:T(8,128)(2,1)S(1)} %add_convert_fusion.2), channel_id=1, source_target_pairs={{1,0},{2,3},{5,4},{6,7},{9,8},{10,11},{13,12},{14,15},{17,16},{18,... | collective-permute-start | bytes 2359304 | tf_op jit(solution)/shard_map/ppermute | solution.py:75
  139.7 31.5 %collective-permute-start.14 = (bf16[192,2048]{1,0:T(8,128)(2,1)S(1)}, bf16[192,2048]{1,0:T(8,128)(2,1)S(1)}, u32[]{:S(2)}, u32[]{:S(2)}) collective-permute-start(bf16[192,2048]{1,0:T(8,128)(2,1)S(1)} %add_convert_fusion.4), channel_id=1, source_target_pairs={{1,0},{2,3},{5,4},{6,7},{9,8},{10,11},{13,12},{14,15},{17,16},{18,... | collective-permute-start | bytes 2359304 | tf_op jit(solution)/shard_map/ppermute | solution.py:75
  148.2 24.6 %collective-permute-start.30 = (bf16[384,1024]{1,0:T(8,128)(2,1)S(1)}, bf16[384,1024]{1,0:T(8,128)(2,1)S(1)}, u32[]{:S(2)}, u32[]{:S(2)}) collective-permute-start(bf16[384,1024]{1,0:T(8,128)(2,1)S(1)} %convert_element_type.291), channel_id=1, source_target_pairs={{1,2},{2,1},{5,6},{6,5},{9,10},{10,9},{13,14},{14,13},{17,18},{18,... | collective-permute-start | bytes 2359304 | tf_op jit(solution)/shard_map/ppermute | solution.py:68
  173.1 22.4 %collective-permute-start.32 = (bf16[384,1024]{1,0:T(8,128)(2,1)S(1)}, bf16[384,1024]{1,0:T(8,128)(2,1)S(1)}, u32[]{:S(2)}, u32[]{:S(2)}) collective-permute-start(bf16[384,1024]{1,0:T(8,128)(2,1)S(1)} %add_convert_fusion), channel_id=1, source_target_pairs={{1,0},{2,3},{5,4},{6,7},{9,8},{10,11},{13,12},{14,15},{17,16},{18,... | collective-permute-start | bytes 2359304 | tf_op jit(solution)/shard_map/ppermute | solution.py:75
  174.8 41.1 %collective-permute-start.31 = (bf16[384,1024]{1,0:T(8,128)(2,1)S(1)}, bf16[384,1024]{1,0:T(8,128)(2,1)S(1)}, u32[]{:S(2)}, u32[]{:S(2)}) collective-permute-start(bf16[384,1024]{1,0:T(8,128)(2,1)S(1)} %add_convert_fusion.1), channel_id=1, source_target_pairs={{1,0},{2,3},{5,4},{6,7},{9,8},{10,11},{13,12},{14,15},{17,16},{18,... | collective-permute-start | bytes 2359304 | tf_op jit(solution)/shard_map/ppermute | solution.py:75
  178.0 20.5 %collective-permute-start.24 = (bf16[384,896]{1,0:T(8,128)(2,1)S(1)}, bf16[384,896]{1,0:T(8,128)(2,1)S(1)}, u32[]{:S(2)}, u32[]{:S(2)}) collective-permute-start(bf16[384,896]{1,0:T(8,128)(2,1)S(1)} %pad_maximum_fusion.12), channel_id=1, source_target_pairs={{0,4},{4,0},{8,12},{12,8},{1,5},{5,1},{9,13},{13,9},{2,6},{6,2},{1... | collective-permute-start | bytes 2064392 | tf_op jit(solution)/shard_map/ppermute | solution.py:44
  199.8 19.2 %collective-permute-start.25 = (bf16[128,896]{1,0:T(8,128)(2,1)S(1)}, bf16[128,896]{1,0:T(8,128)(2,1)S(1)}, u32[]{:S(2)}, u32[]{:S(2)}) collective-permute-start(bf16[128,896]{1,0:T(8,128)(2,1)S(1)} %get-tuple-element.83), channel_id=1, source_target_pairs={{0,1},{1,0},{2,3},{3,2},{4,5},{5,4},{6,7},{7,6},{8,9},{9,8},{10,11... | collective-permute-start | bytes 688136 | tf_op jit(solution)/shard_map/ppermute | solution.py:44
  201.3 21.3 %collective-permute-start.33 = (bf16[384,896]{1,0:T(8,128)(2,1)S(1)}, bf16[384,896]{1,0:T(8,128)(2,1)S(1)}, u32[]{:S(2)}, u32[]{:S(2)}) collective-permute-start(bf16[384,896]{1,0:T(8,128)(2,1)S(1)} %pad_maximum_fusion.14), channel_id=1, source_target_pairs={{0,8},{4,12},{8,0},{12,4},{1,9},{5,13},{9,1},{13,5},{2,10},{6,14},... | collective-permute-start | bytes 2064392 | tf_op jit(solution)/shard_map/ppermute | solution.py:44
  229.3 18.0 %collective-permute-start.36 = (bf16[128,896]{1,0:T(8,128)(2,1)S(1)}, bf16[128,896]{1,0:T(8,128)(2,1)S(1)}, u32[]{:S(2)}, u32[]{:S(2)}) collective-permute-start(bf16[128,896]{1,0:T(8,128)(2,1)S(1)} %get-tuple-element.78), channel_id=1, source_target_pairs={{0,2},{1,3},{2,0},{3,1},{4,6},{5,7},{6,4},{7,5},{8,10},{9,11},{10,... | collective-permute-start | bytes 688136 | tf_op jit(solution)/shard_map/ppermute | solution.py:44
  (22 other events, 360.2 us)

commit v5 on v4

--- a/solution.py
+++ b/solution.py
@@ -95,7 +95,7 @@
     per_group = n_exp // GROUPS
     w_gate, w_up, w_down = gate_weight[0], up_weight[0], down_weight[0]
     w_both = jnp.concatenate([w_gate, w_up], axis=1)
-    distances = list(range(n_dp - 1, 0, -1))
+    distances = list(range(1, n_dp))
 
     features, experts = Queue("dp", 0), Queue("expert", 0)
     blocks = here ^ jnp.arange(n_dp, dtype=jnp.int32)
@@ -117,7 +117,7 @@
     got_rows = by_features(tokens, tail)
     got_grads = by_features(weighted, None)
 
-    gathered = jnp.concatenate(got_rows, axis=0)
+    gathered = after(jnp.concatenate(got_rows, axis=0), got_grads[1])
     codes = gathered.reshape(n_dp, tok_count + CODE_ROWS, part)[:, tok_count, :tok_count].astype(jnp.int32)
     places = ((codes // capacity) ^ me) * chunk + blocks[:, None] * capacity + codes % capacity
 
@@ -198,7 +198,7 @@
         kind, gs = ITEMS[item]
         moved = joined([(rows if kind == "pre" else grads)[g] for g in gs])
         ahead = 2
-        moved = after(moved, inward[item - ahead]) if item >= ahead else after(moved, got_grads[1])
+        moved = after(moved, inward[item - ahead]) if item >= ahead else moved
         sums.append(LineSum("dp", jnp.dot(moved, w_both if kind == "pre" else w_down, preferred_element_type=F32)))
         inward.append(sums[item].inward(*inward[-1:]))
         middle.append(sums[item].middle())

time: 250 us -> 240 us (0.960)
  waiting for transfers between devices: 129 us -> 108 us
  starting transfers between devices: 66.3 us -> 77.6 us
    ppermute x6, waiting for transfers between devices: 48.3 us -> 36.5 us  [inward(): arrived = lax.ppermute(self.total.astype(BF16), self.axis, pairs)]
    ppermute x6, starting transfers between devices: 29.9 us -> 36.8 us  [inward(): arrived = lax.ppermute(self.total.astype(BF16), self.axis, pairs)]
    ppermute x6, waiting for transfers between devices: 38.6 us -> 31.8 us  [outward(): lax.ppermute((self.own + got.astype(F32)).astype(BF16), self.axis, pairs)]
    ppermute x20, starting transfers between devices: 24.1 us -> 28.3 us  [send(): got = lax.ppermute(self.turn(value), self.axis, pairs)]
  transfers between devices with their start and end apart: 38 -> 38, of which waited for: 20 -> 18; matrix products, arithmetic and copies ran while one was open for 17% -> 20% of each run, Pallas kernels for 0% -> 0%
where the time goes in v5:
time: 240 us
  waiting for transfers between devices  108 us (45%)
  starting transfers between devices  77.6 us (32%)
  matrix products  30 us (12%)
  other arithmetic  15.7 us (7%)
  local copies, waits for them, and re-layouts  6.96 us (3%)
    ppermute x20, waiting for transfers between devices, send(): got = lax.ppermute(self.turn(value), self.axis, pairs)  39.5 us
    ppermute x6, starting transfers between devices, inward(): arrived = lax.ppermute(self.total.astype(BF16), self.axis, pairs)  36.8 us
    ppermute x6, waiting for transfers between devices, inward(): arrived = lax.ppermute(self.total.astype(BF16), self.axis, pairs)  36.5 us
    ppermute x6, waiting for transfers between devices, outward(): lax.ppermute((self.own + got.astype(F32)).astype(BF16), self.axis, pairs)  31.8 us
    ppermute x20, starting transfers between devices, send(): got = lax.ppermute(self.turn(value), self.axis, pairs)  28.3 us
    dot_general x5, matrix products, over_rows(): lax.dot_general(left, right, (((0,), (0,)), ((), ())), preferred_element_...  10.7 us
    dot_general x8, matrix products, across(): lax.dot_general(left, right, (((1,), (1,)), ((), ())), preferred_element_...  8.68 us
    ppermute x6, starting transfers between devices, outward(): lax.ppermute((self.own + got.astype(F32)).astype(BF16), self.axis, pairs)  7.97 us
  transfers between devices with their start and end apart: 38, of which 18 were waited for; matrix products, arithmetic and copies ran while one was open for 20% of the time, Pallas kernels for 0%

profile of v5, /device:TPU:0, one launch (start us, length us, event | category | flops | bytes accessed | tf_op | source)
XLA Modules:
  0.0 239.7 jit_solution(2929387390368717242)
XLA Ops:
  5.2 3.0 %collective-permute-start = (bf16[144,896]{1,0:T(8,128)(2,1)}, bf16[144,896]{1,0:T(8,128)(2,1)S(1)}, u32[]{:S(2)}, u32[]{:S(2)}) collective-permute-start(bf16[144,896]{1,0:T(8,128)(2,1)} %get-tuple-element.109), channel_id=1, source_target_pairs={{0,1},{1,0},{2,3},{3,2},{4,5},{5,4},{6,7},{7,6},{8,9},{9,8},{10,11... | collective-permute-start | bytes 774152 | tf_op jit(solution)/shard_map/ppermute | solution.py:44
  11.8 7.6 %collective-permute-done = bf16[144,896]{1,0:T(8,128)(2,1)S(1)} collective-permute-done((bf16[144,896]{1,0:T(8,128)(2,1)}, bf16[144,896]{1,0:T(8,128)(2,1)S(1)}, u32[]{:S(2)}, u32[]{:S(2)}) %collective-permute-start) | collective-permute-done | bytes 258080 | tf_op jit(solution)/shard_map/ppermute | solution.py:44
  19.4 10.1 %collective-permute-done.1 = bf16[144,896]{1,0:T(8,128)(2,1)S(1)} collective-permute-done((bf16[144,896]{1,0:T(8,128)(2,1)}, bf16[144,896]{1,0:T(8,128)(2,1)S(1)}, u32[]{:S(2)}, u32[]{:S(2)}) %collective-permute-start.1) | collective-permute-done | bytes 258080 | tf_op jit(solution)/shard_map/ppermute | solution.py:44
  29.6 4.7 %collective-permute-start.3 = (bf16[128,896]{1,0:T(8,128)(2,1)S(1)}, bf16[128,896]{1,0:T(8,128)(2,1)S(1)}, u32[]{:S(2)}, u32[]{:S(2)}) collective-permute-start(bf16[128,896]{1,0:T(8,128)(2,1)S(1)} %get-tuple-element.32), channel_id=1, source_target_pairs={{0,1},{1,0},{2,3},{3,2},{4,5},{5,4},{6,7},{7,6},{8,9},{9,8},{10,11... | collective-permute-start | bytes 688136 | tf_op jit(solution)/shard_map/ppermute | solution.py:44
  47.5 4.4 %collective-permute-start.4 = (bf16[192,2048]{1,0:T(8,128)(2,1)S(1)}, bf16[192,2048]{1,0:T(8,128)(2,1)S(1)}, u32[]{:S(2)}, u32[]{:S(2)}) collective-permute-start(bf16[192,2048]{1,0:T(8,128)(2,1)S(1)} %get-tuple-element.110), channel_id=1, source_target_pairs={{0,1},{3,2},{4,5},{7,6},{8,9},{11,10},{12,13},{15,14},{16,17},{19,... | collective-permute-start | bytes 2359304 | tf_op jit(solution)/shard_map/ppermute | solution.py:61
  60.2 3.6 %collective-permute-start.9 = (bf16[192,2048]{1,0:T(8,128)(2,1)S(1)}, bf16[192,2048]{1,0:T(8,128)(2,1)S(1)}, u32[]{:S(2)}, u32[]{:S(2)}) collective-permute-start(bf16[192,2048]{1,0:T(8,128)(2,1)S(1)} %get-tuple-element.114), channel_id=1, source_target_pairs={{0,1},{3,2},{4,5},{7,6},{8,9},{11,10},{12,13},{15,14},{16,17},{19,... | collective-permute-start | bytes 2359304 | tf_op jit(solution)/shard_map/ppermute | solution.py:61
  68.6 7.2 %collective-permute-start.11 = (bf16[192,2048]{1,0:T(8,128)(2,1)S(1)}, bf16[192,2048]{1,0:T(8,128)(2,1)S(1)}, u32[]{:S(2)}, u32[]{:S(2)}) collective-permute-start(bf16[192,2048]{1,0:T(8,128)(2,1)S(1)} %get-tuple-element.112), channel_id=1, source_target_pairs={{0,1},{3,2},{4,5},{7,6},{8,9},{11,10},{12,13},{15,14},{16,17},{19,... | collective-permute-start | bytes 2359304 | tf_op jit(solution)/shard_map/ppermute | solution.py:61
  75.8 6.0 %collective-permute-done.9 = bf16[192,2048]{1,0:T(8,128)(2,1)S(1)} collective-permute-done((bf16[192,2048]{1,0:T(8,128)(2,1)S(1)}, bf16[192,2048]{1,0:T(8,128)(2,1)S(1)}, u32[]{:S(2)}, u32[]{:S(2)}) %collective-permute-start.9) | collective-permute-done | bytes 786464 | tf_op jit(solution)/shard_map/ppermute | solution.py:61
  83.8 7.2 %collective-permute-start.10 = (bf16[192,2048]{1,0:T(8,128)(2,1)S(1)}, bf16[192,2048]{1,0:T(8,128)(2,1)S(1)}, u32[]{:S(2)}, u32[]{:S(2)}) collective-permute-start(bf16[192,2048]{1,0:T(8,128)(2,1)S(1)} %get-tuple-element.116), channel_id=1, source_target_pairs={{0,1},{3,2},{4,5},{7,6},{8,9},{11,10},{12,13},{15,14},{16,17},{19,... | collective-permute-start | bytes 2359304 | tf_op jit(solution)/shard_map/ppermute | solution.py:61
  92.7 5.9 %collective-permute-done.11 = bf16[192,2048]{1,0:T(8,128)(2,1)S(1)} collective-permute-done((bf16[192,2048]{1,0:T(8,128)(2,1)S(1)}, bf16[192,2048]{1,0:T(8,128)(2,1)S(1)}, u32[]{:S(2)}, u32[]{:S(2)}) %collective-permute-start.11) | collective-permute-done | bytes 786464 | tf_op jit(solution)/shard_map/ppermute | solution.py:61
  100.8 7.2 %collective-permute-start.19 = (bf16[384,1024]{1,0:T(8,128)(2,1)S(1)}, bf16[384,1024]{1,0:T(8,128)(2,1)S(1)}, u32[]{:S(2)}, u32[]{:S(2)}) collective-permute-start(bf16[384,1024]{1,0:T(8,128)(2,1)S(1)} %get-tuple-element.118), channel_id=1, source_target_pairs={{0,1},{3,2},{4,5},{7,6},{8,9},{11,10},{12,13},{15,14},{16,17},{19,... | collective-permute-start | bytes 2359304 | tf_op jit(solution)/shard_map/ppermute | solution.py:61
  109.6 5.9 %collective-permute-done.10 = bf16[192,2048]{1,0:T(8,128)(2,1)S(1)} collective-permute-done((bf16[192,2048]{1,0:T(8,128)(2,1)S(1)}, bf16[192,2048]{1,0:T(8,128)(2,1)S(1)}, u32[]{:S(2)}, u32[]{:S(2)}) %collective-permute-start.10) | collective-permute-done | bytes 786464 | tf_op jit(solution)/shard_map/ppermute | solution.py:61
  117.7 7.2 %collective-permute-start.28 = (bf16[384,1024]{1,0:T(8,128)(2,1)S(1)}, bf16[384,1024]{1,0:T(8,128)(2,1)S(1)}, u32[]{:S(2)}, u32[]{:S(2)}) collective-permute-start(bf16[384,1024]{1,0:T(8,128)(2,1)S(1)} %get-tuple-element.120), channel_id=1, source_target_pairs={{0,1},{3,2},{4,5},{7,6},{8,9},{11,10},{12,13},{15,14},{16,17},{19,... | collective-permute-start | bytes 2359304 | tf_op jit(solution)/shard_map/ppermute | solution.py:61
  128.0 4.3 %collective-permute-done.19 = bf16[384,1024]{1,0:T(8,128)(2,1)S(1)} collective-permute-done((bf16[384,1024]{1,0:T(8,128)(2,1)S(1)}, bf16[384,1024]{1,0:T(8,128)(2,1)S(1)}, u32[]{:S(2)}, u32[]{:S(2)}) %collective-permute-start.19) | collective-permute-done | bytes 786464 | tf_op jit(solution)/shard_map/ppermute | solution.py:61
  135.7 13.3 %collective-permute-done.28 = bf16[384,1024]{1,0:T(8,128)(2,1)S(1)} collective-permute-done((bf16[384,1024]{1,0:T(8,128)(2,1)S(1)}, bf16[384,1024]{1,0:T(8,128)(2,1)S(1)}, u32[]{:S(2)}, u32[]{:S(2)}) %collective-permute-start.28) | collective-permute-done | bytes 786464 | tf_op jit(solution)/shard_map/ppermute | solution.py:61
  155.7 10.3 %collective-permute-done.14 = bf16[192,2048]{1,0:T(8,128)(2,1)S(1)} collective-permute-done((bf16[192,2048]{1,0:T(8,128)(2,1)S(1)}, bf16[192,2048]{1,0:T(8,128)(2,1)S(1)}, u32[]{:S(2)}, u32[]{:S(2)}) %collective-permute-start.14) | collective-permute-done | bytes 786464 | tf_op jit(solution)/shard_map/ppermute | solution.py:75
  170.0 12.8 %collective-permute-done.32 = bf16[384,1024]{1,0:T(8,128)(2,1)S(1)} collective-permute-done((bf16[384,1024]{1,0:T(8,128)(2,1)S(1)}, bf16[384,1024]{1,0:T(8,128)(2,1)S(1)}, u32[]{:S(2)}, u32[]{:S(2)}) %collective-permute-start.32) | collective-permute-done | bytes 786464 | tf_op jit(solution)/shard_map/ppermute | solution.py:75
  189.0 8.7 %collective-permute-done.31 = bf16[384,1024]{1,0:T(8,128)(2,1)S(1)} collective-permute-done((bf16[384,1024]{1,0:T(8,128)(2,1)S(1)}, bf16[384,1024]{1,0:T(8,128)(2,1)S(1)}, u32[]{:S(2)}, u32[]{:S(2)}) %collective-permute-start.31) | collective-permute-done | bytes 786464 | tf_op jit(solution)/shard_map/ppermute | solution.py:75
  203.8 5.7 %collective-permute-done.25 = bf16[128,896]{1,0:T(8,128)(2,1)S(1)} collective-permute-done((bf16[128,896]{1,0:T(8,128)(2,1)S(1)}, bf16[128,896]{1,0:T(8,128)(2,1)S(1)}, u32[]{:S(2)}, u32[]{:S(2)}) %collective-permute-start.25) | collective-permute-done | bytes 229408 | tf_op jit(solution)/shard_map/ppermute | solution.py:44
  213.2 4.6 %collective-permute-done.26 = bf16[128,896]{1,0:T(8,128)(2,1)S(1)} collective-permute-done((bf16[128,896]{1,0:T(8,128)(2,1)S(1)}, bf16[128,896]{1,0:T(8,128)(2,1)S(1)}, u32[]{:S(2)}, u32[]{:S(2)}) %collective-permute-start.26) | collective-permute-done | bytes 229408 | tf_op jit(solution)/shard_map/ppermute | solution.py:44
  225.2 4.8 %collective-permute-done.35 = bf16[128,896]{1,0:T(8,128)(2,1)S(1)} collective-permute-done((bf16[128,896]{1,0:T(8,128)(2,1)S(1)}, bf16[128,896]{1,0:T(8,128)(2,1)S(1)}, u32[]{:S(2)}, u32[]{:S(2)}) %collective-permute-start.35) | collective-permute-done | bytes 229408 | tf_op jit(solution)/shard_map/ppermute | solution.py:44
  230.1 2.9 %convert_bitcast_fusion.2 = bf16[1,896,1024]{2,1,0:T(8,128)(2,1)} fusion(bf16[768,2048]{1,0:T(8,128)(2,1)S(1)} %pad_maximum_fusion.1, bf16[192,896]{1,0:T(8,128)(2,1)S(1)} %get-tuple-element.35, bf16[192,896]{1,0:T(8,128)(2,1)S(1)} %get-tuple-element.91, bf16[192,896]{1,0:T(8,128)(2,1)S(1)} %get-tuple-element.34, bf16[192,896]{1,0:T(8,128)(2,1)S(1)} %get-tuple-element.71), kind=kOutput, calls=%fused_computation.18 | convolution fusion | flops 1415708672 | bytes 4784128 | tf_op jit(solution)/shard_map/dot_general | solution.py:25
  232.9 2.9 %convert_bitcast_fusion.1 = bf16[1,896,1024]{2,1,0:T(8,128)(2,1)} fusion(bf16[768,2048]{1,0:T(8,128)(2,1)S(1)} %pad_maximum_fusion.1, bf16[192,896]{1,0:T(8,128)(2,1)S(1)} %get-tuple-element.35, bf16[192,896]{1,0:T(8,128)(2,1)S(1)} %get-tuple-element.91, bf16[192,896]{1,0:T(8,128)(2,1)S(1)} %get-tuple-element.34, bf16[192,896]{1,0:T(8,128)(2,1)S(1)} %get-tuple-element.71), kind=kOutput, calls=%fused_computation.17 | convolution fusion | flops 1415708672 | bytes 4784128 | tf_op jit(solution)/shard_map/dot_general | solution.py:25
  235.8 2.9 %convert_bitcast_fusion = bf16[1,896,1024]{2,1,0:T(8,128)(2,1)} fusion(bf16[768,1024]{1,0:T(8,128)(2,1)S(1)} %pad_maximum_fusion.2, bf16[192,896]{1,0:T(8,128)(2,1)S(1)} %get-tuple-element.98, bf16[192,896]{1,0:T(8,128)(2,1)S(1)} %get-tuple-element.103, bf16[192,896]{1,0:T(8,128)(2,1)S(1)} %get-tuple-element.97, bf16[192,896]{1,0:T(8,128)(2,1)S(1)} %get-tuple-element.73), kind=kOutput, calls=%fused_computation.16 | convolution fusion | flops 1415708672 | bytes 4784128 | tf_op jit(solution)/shard_map/dot_general | solution.py:25
  (183 shorter events, 84.8 us)
Async XLA Ops:
  8.2 21.3 %collective-permute-start.1 = (bf16[144,896]{1,0:T(8,128)(2,1)}, bf16[144,896]{1,0:T(8,128)(2,1)S(1)}, u32[]{:S(2)}, u32[]{:S(2)}) collective-permute-start(bf16[144,896]{1,0:T(8,128)(2,1)} %get-tuple-element.108), channel_id=1, source_target_pairs={{0,2},{1,3},{2,0},{3,1},{4,6},{5,7},{6,4},{7,5},{8,10},{9,11},{10,... | collective-permute-start | bytes 774152 | tf_op jit(solution)/shard_map/ppermute | solution.py:44
  10.8 18.7 %collective-permute-start.2 = (bf16[144,896]{1,0:T(8,128)(2,1)}, bf16[144,896]{1,0:T(8,128)(2,1)S(1)}, u32[]{:S(2)}, u32[]{:S(2)}) collective-permute-start(bf16[144,896]{1,0:T(8,128)(2,1)} %get-tuple-element.107), channel_id=1, source_target_pairs={{0,3},{1,2},{2,1},{3,0},{4,7},{5,6},{6,5},{7,4},{8,11},{9,10},{10,... | collective-permute-start | bytes 774152 | tf_op jit(solution)/shard_map/ppermute | solution.py:44
  36.7 18.0 %collective-permute-start.15 = (bf16[128,896]{1,0:T(8,128)(2,1)S(1)}, bf16[128,896]{1,0:T(8,128)(2,1)}, u32[]{:S(2)}, u32[]{:S(2)}) collective-permute-start(bf16[128,896]{1,0:T(8,128)(2,1)S(1)} %get-tuple-element.39), channel_id=1, source_target_pairs={{0,2},{1,3},{2,0},{3,1},{4,6},{5,7},{6,4},{7,5},{8,10},{9,11},{10,... | collective-permute-start | bytes 688136 | tf_op jit(solution)/shard_map/ppermute | solution.py:44
  60.2 21.6 %collective-permute-start.9 = (bf16[192,2048]{1,0:T(8,128)(2,1)S(1)}, bf16[192,2048]{1,0:T(8,128)(2,1)S(1)}, u32[]{:S(2)}, u32[]{:S(2)}) collective-permute-start(bf16[192,2048]{1,0:T(8,128)(2,1)S(1)} %get-tuple-element.114), channel_id=1, source_target_pairs={{0,1},{3,2},{4,5},{7,6},{8,9},{11,10},{12,13},{15,14},{16,17},{19,... | collective-permute-start | bytes 2359304 | tf_op jit(solution)/shard_map/ppermute | solution.py:61
  65.2 26.0 %collective-permute-start.5 = (bf16[192,2048]{1,0:T(8,128)(2,1)S(1)}, bf16[192,2048]{1,0:T(8,128)(2,1)S(1)}, u32[]{:S(2)}, u32[]{:S(2)}) collective-permute-start(bf16[192,2048]{1,0:T(8,128)(2,1)S(1)} %convert_element_type.246), channel_id=1, source_target_pairs={{1,2},{2,1},{5,6},{6,5},{9,10},{10,9},{13,14},{14,13},{17,18},{18,... | collective-permute-start | bytes 2359304 | tf_op jit(solution)/shard_map/ppermute | solution.py:68
  66.0 25.0 %collective-permute-start.17 = (bf16[384,896]{1,0:T(8,128)(2,1)S(1)}, bf16[384,896]{1,0:T(8,128)(2,1)S(1)}, u32[]{:S(2)}, u32[]{:S(2)}) collective-permute-start(bf16[384,896]{1,0:T(8,128)(2,1)S(1)} %concatenate.105), channel_id=1, source_target_pairs={{0,8},{4,12},{8,0},{12,4},{1,9},{5,13},{9,1},{13,5},{2,10},{6,14},... | collective-permute-start | bytes 2064392 | tf_op jit(solution)/shard_map/ppermute | solution.py:44
  68.6 30.0 %collective-permute-start.11 = (bf16[192,2048]{1,0:T(8,128)(2,1)S(1)}, bf16[192,2048]{1,0:T(8,128)(2,1)S(1)}, u32[]{:S(2)}, u32[]{:S(2)}) collective-permute-start(bf16[192,2048]{1,0:T(8,128)(2,1)S(1)} %get-tuple-element.112), channel_id=1, source_target_pairs={{0,1},{3,2},{4,5},{7,6},{8,9},{11,10},{12,13},{15,14},{16,17},{19,... | collective-permute-start | bytes 2359304 | tf_op jit(solution)/shard_map/ppermute | solution.py:61
  82.1 26.0 %collective-permute-start.20 = (bf16[192,2048]{1,0:T(8,128)(2,1)S(1)}, bf16[192,2048]{1,0:T(8,128)(2,1)S(1)}, u32[]{:S(2)}, u32[]{:S(2)}) collective-permute-start(bf16[192,2048]{1,0:T(8,128)(2,1)S(1)} %convert_element_type.267), channel_id=1, source_target_pairs={{1,2},{2,1},{5,6},{6,5},{9,10},{10,9},{13,14},{14,13},{17,18},{18,... | collective-permute-start | bytes 2359304 | tf_op jit(solution)/shard_map/ppermute | solution.py:68
  83.8 31.7 %collective-permute-start.10 = (bf16[192,2048]{1,0:T(8,128)(2,1)S(1)}, bf16[192,2048]{1,0:T(8,128)(2,1)S(1)}, u32[]{:S(2)}, u32[]{:S(2)}) collective-permute-start(bf16[192,2048]{1,0:T(8,128)(2,1)S(1)} %get-tuple-element.116), channel_id=1, source_target_pairs={{0,1},{3,2},{4,5},{7,6},{8,9},{11,10},{12,13},{15,14},{16,17},{19,... | collective-permute-start | bytes 2359304 | tf_op jit(solution)/shard_map/ppermute | solution.py:61
  91.4 26.3 %collective-permute-start.6 = (bf16[192,2048]{1,0:T(8,128)(2,1)S(1)}, bf16[192,2048]{1,0:T(8,128)(2,1)S(1)}, u32[]{:S(2)}, u32[]{:S(2)}) collective-permute-start(bf16[192,2048]{1,0:T(8,128)(2,1)S(1)} %add_convert_fusion.5), channel_id=1, source_target_pairs={{1,0},{2,3},{5,4},{6,7},{9,8},{10,11},{13,12},{14,15},{17,16},{18,... | collective-permute-start | bytes 2359304 | tf_op jit(solution)/shard_map/ppermute | solution.py:75
  98.9 27.6 %collective-permute-start.13 = (bf16[192,2048]{1,0:T(8,128)(2,1)S(1)}, bf16[192,2048]{1,0:T(8,128)(2,1)S(1)}, u32[]{:S(2)}, u32[]{:S(2)}) collective-permute-start(bf16[192,2048]{1,0:T(8,128)(2,1)S(1)} %convert_element_type.258), channel_id=1, source_target_pairs={{1,2},{2,1},{5,6},{6,5},{9,10},{10,9},{13,14},{14,13},{17,18},{18,... | collective-permute-start | bytes 2359304 | tf_op jit(solution)/shard_map/ppermute | solution.py:68
  100.8 31.6 %collective-permute-start.19 = (bf16[384,1024]{1,0:T(8,128)(2,1)S(1)}, bf16[384,1024]{1,0:T(8,128)(2,1)S(1)}, u32[]{:S(2)}, u32[]{:S(2)}) collective-permute-start(bf16[384,1024]{1,0:T(8,128)(2,1)S(1)} %get-tuple-element.118), channel_id=1, source_target_pairs={{0,1},{3,2},{4,5},{7,6},{8,9},{11,10},{12,13},{15,14},{16,17},{19,... | collective-permute-start | bytes 2359304 | tf_op jit(solution)/shard_map/ppermute | solution.py:61
  108.3 25.2 %collective-permute-start.21 = (bf16[192,2048]{1,0:T(8,128)(2,1)S(1)}, bf16[192,2048]{1,0:T(8,128)(2,1)S(1)}, u32[]{:S(2)}, u32[]{:S(2)}) collective-permute-start(bf16[192,2048]{1,0:T(8,128)(2,1)S(1)} %add_convert_fusion.3), channel_id=1, source_target_pairs={{1,0},{2,3},{5,4},{6,7},{9,8},{10,11},{13,12},{14,15},{17,16},{18,... | collective-permute-start | bytes 2359304 | tf_op jit(solution)/shard_map/ppermute | solution.py:75
  115.8 18.1 %collective-permute-start.12 = (bf16[192,2048]{1,0:T(8,128)(2,1)S(1)}, bf16[192,2048]{1,0:T(8,128)(2,1)S(1)}, u32[]{:S(2)}, u32[]{:S(2)}) collective-permute-start(bf16[192,2048]{1,0:T(8,128)(2,1)S(1)} %convert_element_type.256), channel_id=1, source_target_pairs={{1,2},{2,1},{5,6},{6,5},{9,10},{10,9},{13,14},{14,13},{17,18},{18,... | collective-permute-start | bytes 2359304 | tf_op jit(solution)/shard_map/ppermute | solution.py:68
  117.7 31.2 %collective-permute-start.28 = (bf16[384,1024]{1,0:T(8,128)(2,1)S(1)}, bf16[384,1024]{1,0:T(8,128)(2,1)S(1)}, u32[]{:S(2)}, u32[]{:S(2)}) collective-permute-start(bf16[384,1024]{1,0:T(8,128)(2,1)S(1)} %get-tuple-element.120), channel_id=1, source_target_pairs={{0,1},{3,2},{4,5},{7,6},{8,9},{11,10},{12,13},{15,14},{16,17},{19,... | collective-permute-start | bytes 2359304 | tf_op jit(solution)/shard_map/ppermute | solution.py:61
  126.7 24.2 %collective-permute-start.22 = (bf16[192,2048]{1,0:T(8,128)(2,1)S(1)}, bf16[192,2048]{1,0:T(8,128)(2,1)S(1)}, u32[]{:S(2)}, u32[]{:S(2)}) collective-permute-start(bf16[192,2048]{1,0:T(8,128)(2,1)S(1)} %add_convert_fusion.2), channel_id=1, source_target_pairs={{1,0},{2,3},{5,4},{6,7},{9,8},{10,11},{13,12},{14,15},{17,16},{18,... | collective-permute-start | bytes 2359304 | tf_op jit(solution)/shard_map/ppermute | solution.py:75
  132.7 21.4 %collective-permute-start.30 = (bf16[384,1024]{1,0:T(8,128)(2,1)S(1)}, bf16[384,1024]{1,0:T(8,128)(2,1)S(1)}, u32[]{:S(2)}, u32[]{:S(2)}) collective-permute-start(bf16[384,1024]{1,0:T(8,128)(2,1)S(1)} %convert_element_type.291), channel_id=1, source_target_pairs={{1,2},{2,1},{5,6},{6,5},{9,10},{10,9},{13,14},{14,13},{17,18},{18,... | collective-permute-start | bytes 2359304 | tf_op jit(solution)/shard_map/ppermute | solution.py:68
  134.4 31.6 %collective-permute-start.14 = (bf16[192,2048]{1,0:T(8,128)(2,1)S(1)}, bf16[192,2048]{1,0:T(8,128)(2,1)S(1)}, u32[]{:S(2)}, u32[]{:S(2)}) collective-permute-start(bf16[192,2048]{1,0:T(8,128)(2,1)S(1)} %add_convert_fusion.4), channel_id=1, source_target_pairs={{1,0},{2,3},{5,4},{6,7},{9,8},{10,11},{13,12},{14,15},{17,16},{18,... | collective-permute-start | bytes 2359304 | tf_op jit(solution)/shard_map/ppermute | solution.py:75
  154.4 28.4 %collective-permute-start.32 = (bf16[384,1024]{1,0:T(8,128)(2,1)S(1)}, bf16[384,1024]{1,0:T(8,128)(2,1)S(1)}, u32[]{:S(2)}, u32[]{:S(2)}) collective-permute-start(bf16[384,1024]{1,0:T(8,128)(2,1)S(1)} %add_convert_fusion), channel_id=1, source_target_pairs={{1,0},{2,3},{5,4},{6,7},{9,8},{10,11},{13,12},{14,15},{17,16},{18,... | collective-permute-start | bytes 2359304 | tf_op jit(solution)/shard_map/ppermute | solution.py:75
  167.0 30.7 %collective-permute-start.31 = (bf16[384,1024]{1,0:T(8,128)(2,1)S(1)}, bf16[384,1024]{1,0:T(8,128)(2,1)S(1)}, u32[]{:S(2)}, u32[]{:S(2)}) collective-permute-start(bf16[384,1024]{1,0:T(8,128)(2,1)S(1)} %add_convert_fusion.1), channel_id=1, source_target_pairs={{1,0},{2,3},{5,4},{6,7},{9,8},{10,11},{13,12},{14,15},{17,16},{18,... | collective-permute-start | bytes 2359304 | tf_op jit(solution)/shard_map/ppermute | solution.py:75
  169.9 28.1 %collective-permute-start.24 = (bf16[384,896]{1,0:T(8,128)(2,1)S(1)}, bf16[384,896]{1,0:T(8,128)(2,1)S(1)}, u32[]{:S(2)}, u32[]{:S(2)}) collective-permute-start(bf16[384,896]{1,0:T(8,128)(2,1)S(1)} %pad_maximum_fusion.12), channel_id=1, source_target_pairs={{0,4},{4,0},{8,12},{12,8},{1,5},{5,1},{9,13},{13,9},{2,6},{6,2},{1... | collective-permute-start | bytes 2064392 | tf_op jit(solution)/shard_map/ppermute | solution.py:44
  199.4 18.4 %collective-permute-start.26 = (bf16[128,896]{1,0:T(8,128)(2,1)S(1)}, bf16[128,896]{1,0:T(8,128)(2,1)S(1)}, u32[]{:S(2)}, u32[]{:S(2)}) collective-permute-start(bf16[128,896]{1,0:T(8,128)(2,1)S(1)} %get-tuple-element.80), channel_id=1, source_target_pairs={{0,2},{1,3},{2,0},{3,1},{4,6},{5,7},{6,4},{7,5},{8,10},{9,11},{10,... | collective-permute-start | bytes 688136 | tf_op jit(solution)/shard_map/ppermute | solution.py:44
  201.3 19.4 %collective-permute-start.27 = (bf16[128,896]{1,0:T(8,128)(2,1)S(1)}, bf16[128,896]{1,0:T(8,128)(2,1)S(1)}, u32[]{:S(2)}, u32[]{:S(2)}) collective-permute-start(bf16[128,896]{1,0:T(8,128)(2,1)S(1)} %get-tuple-element.79), channel_id=1, source_target_pairs={{0,3},{1,2},{2,1},{3,0},{4,7},{5,6},{6,5},{7,4},{8,11},{9,10},{10,... | collective-permute-start | bytes 688136 | tf_op jit(solution)/shard_map/ppermute | solution.py:44
  220.8 17.9 %collective-permute-start.36 = (bf16[128,896]{1,0:T(8,128)(2,1)S(1)}, bf16[128,896]{1,0:T(8,128)(2,1)S(1)}, u32[]{:S(2)}, u32[]{:S(2)}) collective-permute-start(bf16[128,896]{1,0:T(8,128)(2,1)S(1)} %get-tuple-element.76), channel_id=1, source_target_pairs={{0,2},{1,3},{2,0},{3,1},{4,6},{5,7},{6,4},{7,5},{8,10},{9,11},{10,... | collective-permute-start | bytes 688136 | tf_op jit(solution)/shard_map/ppermute | solution.py:44
  (24 other events, 336.9 us)

commit v6 on v5

--- a/solution.py
+++ b/solution.py
@@ -117,7 +117,8 @@
     got_rows = by_features(tokens, tail)
     got_grads = by_features(weighted, None)
 
-    gathered = after(jnp.concatenate(got_rows, axis=0), got_grads[1])
+    *tailed, _ = lax.optimization_barrier((*got_rows, got_grads[1]))
+    gathered = jnp.concatenate(tailed, axis=0)
     codes = gathered.reshape(n_dp, tok_count + CODE_ROWS, part)[:, tok_count, :tok_count].astype(jnp.int32)
     places = ((codes // capacity) ^ me) * chunk + blocks[:, None] * capacity + codes % capacity
 
@@ -125,7 +126,6 @@
         return (jnp.arange(n_exp * chunk, dtype=jnp.int32)[:, None] == places.reshape(-1)[None, :]).astype(BF16)
 
     select = chooser(places)
-    select_whole = chooser(places[blocks])
     select_tailed = chooser(jnp.pad(places, ((0, 0), (0, CODE_ROWS)), constant_values=-1))
 
     def dispatch(chosen, gathered):
@@ -151,12 +151,8 @@
     def blocks_of(values):
         return [None if v is None else v[i * chunk : (i + 1) * chunk] for v in values for i in range(per_group)]
 
-    def pick(values, select=select):
+    def pick(values):
         return over_rows(select, jnp.concatenate(values, axis=0)).astype(BF16)
-
-    def give_back_whole(picked):
-        got = lax.all_to_all(picked.reshape(n_dp, tok_count, part), "dp", split_axis=0, concat_axis=0, tiled=False)
-        return [got] * n_dp
 
     def give_back(picked):
         picked = picked.reshape(n_dp, tok_count, part)

time: 240 us -> 239 us (level)
  waiting for transfers between devices: 108 us -> 111 us
  transfers between devices with their start and end apart: 38 -> 38, of which waited for: 18 -> 17; matrix products, arithmetic and copies ran while one was open for 20% -> 18% of each run, Pallas kernels for 0% -> 0%
where the time goes in v6:
time: 239 us
  waiting for transfers between devices  111 us (46%)
  starting transfers between devices  77.4 us (32%)
  matrix products  30.3 us (13%)
  other arithmetic  13.4 us (6%)
  local copies, waits for them, and re-layouts  5.32 us (2%)
    ppermute x20, waiting for transfers between devices, send(): got = lax.ppermute(self.turn(value), self.axis, pairs)  40.8 us
    ppermute x6, waiting for transfers between devices, inward(): arrived = lax.ppermute(self.total.astype(BF16), self.axis, pairs)  37.1 us
    ppermute x6, starting transfers between devices, inward(): arrived = lax.ppermute(self.total.astype(BF16), self.axis, pairs)  36.6 us
    ppermute x6, waiting for transfers between devices, outward(): lax.ppermute((self.own + got.astype(F32)).astype(BF16), self.axis, pairs)  32.6 us
    ppermute x20, starting transfers between devices, send(): got = lax.ppermute(self.turn(value), self.axis, pairs)  28.4 us
    dot_general x5, matrix products, over_rows(): lax.dot_general(left, right, (((0,), (0,)), ((), ())), preferred_element_...  10.7 us
    dot_general x8, matrix products, across(): lax.dot_general(left, right, (((1,), (1,)), ((), ())), preferred_element_...  8.77 us
    ppermute x6, starting transfers between devices, outward(): lax.ppermute((self.own + got.astype(F32)).astype(BF16), self.axis, pairs)  7.97 us
  transfers between devices with their start and end apart: 38, of which 17 were waited for; matrix products, arithmetic and copies ran while one was open for 18% of the time, Pallas kernels for 0%

profile of v6, /device:TPU:0, one launch (start us, length us, event | category | flops | bytes accessed | tf_op | source)
XLA Modules:
  0.0 238.7 jit_solution(5086661334616300826)
XLA Ops:
  3.8 3.1 %collective-permute-start = (bf16[144,896]{1,0:T(8,128)(2,1)S(1)}, bf16[144,896]{1,0:T(8,128)(2,1)S(1)}, u32[]{:S(2)}, u32[]{:S(2)}) collective-permute-start(bf16[144,896]{1,0:T(8,128)(2,1)S(1)} %get-tuple-element.114), channel_id=1, source_target_pairs={{0,1},{1,0},{2,3},{3,2},{4,5},{5,4},{6,7},{7,6},{8,9},{9,8},{10,11... | collective-permute-start | bytes 774152 | tf_op jit(solution)/shard_map/ppermute | solution.py:44
  10.5 7.4 %collective-permute-done = bf16[144,896]{1,0:T(8,128)(2,1)S(1)} collective-permute-done((bf16[144,896]{1,0:T(8,128)(2,1)S(1)}, bf16[144,896]{1,0:T(8,128)(2,1)S(1)}, u32[]{:S(2)}, u32[]{:S(2)}) %collective-permute-start) | collective-permute-done | bytes 258080 | tf_op jit(solution)/shard_map/ppermute | solution.py:44
  17.9 10.1 %collective-permute-done.1 = bf16[144,896]{1,0:T(8,128)(2,1)S(1)} collective-permute-done((bf16[144,896]{1,0:T(8,128)(2,1)S(1)}, bf16[144,896]{1,0:T(8,128)(2,1)S(1)}, u32[]{:S(2)}, u32[]{:S(2)}) %collective-permute-start.1) | collective-permute-done | bytes 258080 | tf_op jit(solution)/shard_map/ppermute | solution.py:44
  28.0 4.7 %collective-permute-start.3 = (bf16[128,896]{1,0:T(8,128)(2,1)}, bf16[128,896]{1,0:T(8,128)(2,1)}, u32[]{:S(2)}, u32[]{:S(2)}) collective-permute-start(bf16[128,896]{1,0:T(8,128)(2,1)} %get-tuple-element.35), channel_id=1, source_target_pairs={{0,1},{1,0},{2,3},{3,2},{4,5},{5,4},{6,7},{7,6},{8,9},{9,8},{10,11... | collective-permute-start | bytes 688136 | tf_op jit(solution)/shard_map/ppermute | solution.py:44
  35.1 3.9 %collective-permute-done.3 = bf16[128,896]{1,0:T(8,128)(2,1)} collective-permute-done((bf16[128,896]{1,0:T(8,128)(2,1)}, bf16[128,896]{1,0:T(8,128)(2,1)}, u32[]{:S(2)}, u32[]{:S(2)}) %collective-permute-start.3) | collective-permute-done | bytes 229408 | tf_op jit(solution)/shard_map/ppermute | solution.py:44
  45.9 4.4 %collective-permute-start.4 = (bf16[192,2048]{1,0:T(8,128)(2,1)S(1)}, bf16[192,2048]{1,0:T(8,128)(2,1)S(1)}, u32[]{:S(2)}, u32[]{:S(2)}) collective-permute-start(bf16[192,2048]{1,0:T(8,128)(2,1)S(1)} %get-tuple-element.117), channel_id=1, source_target_pairs={{0,1},{3,2},{4,5},{7,6},{8,9},{11,10},{12,13},{15,14},{16,17},{19,... | collective-permute-start | bytes 2359304 | tf_op jit(solution)/shard_map/ppermute | solution.py:61
  58.4 3.4 %collective-permute-start.9 = (bf16[192,2048]{1,0:T(8,128)(2,1)S(1)}, bf16[192,2048]{1,0:T(8,128)(2,1)S(1)}, u32[]{:S(2)}, u32[]{:S(2)}) collective-permute-start(bf16[192,2048]{1,0:T(8,128)(2,1)S(1)} %get-tuple-element.121), channel_id=1, source_target_pairs={{0,1},{3,2},{4,5},{7,6},{8,9},{11,10},{12,13},{15,14},{16,17},{19,... | collective-permute-start | bytes 2359304 | tf_op jit(solution)/shard_map/ppermute | solution.py:61
  67.9 7.2 %collective-permute-start.11 = (bf16[192,2048]{1,0:T(8,128)(2,1)S(1)}, bf16[192,2048]{1,0:T(8,128)(2,1)S(1)}, u32[]{:S(2)}, u32[]{:S(2)}) collective-permute-start(bf16[192,2048]{1,0:T(8,128)(2,1)S(1)} %get-tuple-element.119), channel_id=1, source_target_pairs={{0,1},{3,2},{4,5},{7,6},{8,9},{11,10},{12,13},{15,14},{16,17},{19,... | collective-permute-start | bytes 2359304 | tf_op jit(solution)/shard_map/ppermute | solution.py:61
  75.1 5.9 %collective-permute-done.9 = bf16[192,2048]{1,0:T(8,128)(2,1)S(1)} collective-permute-done((bf16[192,2048]{1,0:T(8,128)(2,1)S(1)}, bf16[192,2048]{1,0:T(8,128)(2,1)S(1)}, u32[]{:S(2)}, u32[]{:S(2)}) %collective-permute-start.9) | collective-permute-done | bytes 786464 | tf_op jit(solution)/shard_map/ppermute | solution.py:61
  83.1 7.2 %collective-permute-start.10 = (bf16[192,2048]{1,0:T(8,128)(2,1)S(1)}, bf16[192,2048]{1,0:T(8,128)(2,1)S(1)}, u32[]{:S(2)}, u32[]{:S(2)}) collective-permute-start(bf16[192,2048]{1,0:T(8,128)(2,1)S(1)} %get-tuple-element.123), channel_id=1, source_target_pairs={{0,1},{3,2},{4,5},{7,6},{8,9},{11,10},{12,13},{15,14},{16,17},{19,... | collective-permute-start | bytes 2359304 | tf_op jit(solution)/shard_map/ppermute | solution.py:61
  92.0 5.9 %collective-permute-done.11 = bf16[192,2048]{1,0:T(8,128)(2,1)S(1)} collective-permute-done((bf16[192,2048]{1,0:T(8,128)(2,1)S(1)}, bf16[192,2048]{1,0:T(8,128)(2,1)S(1)}, u32[]{:S(2)}, u32[]{:S(2)}) %collective-permute-start.11) | collective-permute-done | bytes 786464 | tf_op jit(solution)/shard_map/ppermute | solution.py:61
  100.0 7.2 %collective-permute-start.19 = (bf16[384,1024]{1,0:T(8,128)(2,1)S(1)}, bf16[384,1024]{1,0:T(8,128)(2,1)S(1)}, u32[]{:S(2)}, u32[]{:S(2)}) collective-permute-start(bf16[384,1024]{1,0:T(8,128)(2,1)S(1)} %get-tuple-element.125), channel_id=1, source_target_pairs={{0,1},{3,2},{4,5},{7,6},{8,9},{11,10},{12,13},{15,14},{16,17},{19,... | collective-permute-start | bytes 2359304 | tf_op jit(solution)/shard_map/ppermute | solution.py:61
  108.8 5.9 %collective-permute-done.10 = bf16[192,2048]{1,0:T(8,128)(2,1)S(1)} collective-permute-done((bf16[192,2048]{1,0:T(8,128)(2,1)S(1)}, bf16[192,2048]{1,0:T(8,128)(2,1)S(1)}, u32[]{:S(2)}, u32[]{:S(2)}) %collective-permute-start.10) | collective-permute-done | bytes 786464 | tf_op jit(solution)/shard_map/ppermute | solution.py:61
  117.0 7.2 %collective-permute-start.28 = (bf16[384,1024]{1,0:T(8,128)(2,1)S(1)}, bf16[384,1024]{1,0:T(8,128)(2,1)S(1)}, u32[]{:S(2)}, u32[]{:S(2)}) collective-permute-start(bf16[384,1024]{1,0:T(8,128)(2,1)S(1)} %get-tuple-element.127), channel_id=1, source_target_pairs={{0,1},{3,2},{4,5},{7,6},{8,9},{11,10},{12,13},{15,14},{16,17},{19,... | collective-permute-start | bytes 2359304 | tf_op jit(solution)/shard_map/ppermute | solution.py:61
  127.3 4.3 %collective-permute-done.19 = bf16[384,1024]{1,0:T(8,128)(2,1)S(1)} collective-permute-done((bf16[384,1024]{1,0:T(8,128)(2,1)S(1)}, bf16[384,1024]{1,0:T(8,128)(2,1)S(1)}, u32[]{:S(2)}, u32[]{:S(2)}) %collective-permute-start.19) | collective-permute-done | bytes 786464 | tf_op jit(solution)/shard_map/ppermute | solution.py:61
  134.9 12.7 %collective-permute-done.28 = bf16[384,1024]{1,0:T(8,128)(2,1)S(1)} collective-permute-done((bf16[384,1024]{1,0:T(8,128)(2,1)S(1)}, bf16[384,1024]{1,0:T(8,128)(2,1)S(1)}, u32[]{:S(2)}, u32[]{:S(2)}) %collective-permute-start.28) | collective-permute-done | bytes 786464 | tf_op jit(solution)/shard_map/ppermute | solution.py:61
  154.3 10.9 %collective-permute-done.14 = bf16[192,2048]{1,0:T(8,128)(2,1)S(1)} collective-permute-done((bf16[192,2048]{1,0:T(8,128)(2,1)S(1)}, bf16[192,2048]{1,0:T(8,128)(2,1)S(1)}, u32[]{:S(2)}, u32[]{:S(2)}) %collective-permute-start.14) | collective-permute-done | bytes 786464 | tf_op jit(solution)/shard_map/ppermute | solution.py:75
  168.9 13.1 %collective-permute-done.32 = bf16[384,1024]{1,0:T(8,128)(2,1)S(1)} collective-permute-done((bf16[384,1024]{1,0:T(8,128)(2,1)S(1)}, bf16[384,1024]{1,0:T(8,128)(2,1)S(1)}, u32[]{:S(2)}, u32[]{:S(2)}) %collective-permute-start.32) | collective-permute-done | bytes 786464 | tf_op jit(solution)/shard_map/ppermute | solution.py:75
  188.2 8.6 %collective-permute-done.31 = bf16[384,1024]{1,0:T(8,128)(2,1)S(1)} collective-permute-done((bf16[384,1024]{1,0:T(8,128)(2,1)S(1)}, bf16[384,1024]{1,0:T(8,128)(2,1)S(1)}, u32[]{:S(2)}, u32[]{:S(2)}) %collective-permute-start.31) | collective-permute-done | bytes 786464 | tf_op jit(solution)/shard_map/ppermute | solution.py:75
  203.0 5.8 %collective-permute-done.25 = bf16[128,896]{1,0:T(8,128)(2,1)S(1)} collective-permute-done((bf16[128,896]{1,0:T(8,128)(2,1)S(1)}, bf16[128,896]{1,0:T(8,128)(2,1)S(1)}, u32[]{:S(2)}, u32[]{:S(2)}) %collective-permute-start.25) | collective-permute-done | bytes 229408 | tf_op jit(solution)/shard_map/ppermute | solution.py:44
  212.5 4.3 %collective-permute-done.26 = bf16[128,896]{1,0:T(8,128)(2,1)S(1)} collective-permute-done((bf16[128,896]{1,0:T(8,128)(2,1)S(1)}, bf16[128,896]{1,0:T(8,128)(2,1)S(1)}, u32[]{:S(2)}, u32[]{:S(2)}) %collective-permute-start.26) | collective-permute-done | bytes 229408 | tf_op jit(solution)/shard_map/ppermute | solution.py:44
  224.3 4.8 %collective-permute-done.35 = bf16[128,896]{1,0:T(8,128)(2,1)S(1)} collective-permute-done((bf16[128,896]{1,0:T(8,128)(2,1)S(1)}, bf16[128,896]{1,0:T(8,128)(2,1)S(1)}, u32[]{:S(2)}, u32[]{:S(2)}) %collective-permute-start.35) | collective-permute-done | bytes 229408 | tf_op jit(solution)/shard_map/ppermute | solution.py:44
  229.1 2.9 %convert_bitcast_fusion.2 = bf16[1,896,1024]{2,1,0:T(8,128)(2,1)} fusion(bf16[768,2048]{1,0:T(8,128)(2,1)S(1)} %pad_maximum_fusion.1, bf16[192,896]{1,0:T(8,128)(2,1)S(1)} %get-tuple-element.41, bf16[192,896]{1,0:T(8,128)(2,1)S(1)} %get-tuple-element.97, bf16[192,896]{1,0:T(8,128)(2,1)S(1)} %get-tuple-element.40, bf16[192,896]{1,0:T(8,128)(2,1)S(1)} %get-tuple-element.77), kind=kOutput, calls=%fused_computation.18 | convolution fusion | flops 1415708672 | bytes 4784128 | tf_op jit(solution)/shard_map/dot_general | solution.py:25
  231.9 2.9 %convert_bitcast_fusion.1 = bf16[1,896,1024]{2,1,0:T(8,128)(2,1)} fusion(bf16[768,2048]{1,0:T(8,128)(2,1)S(1)} %pad_maximum_fusion.1, bf16[192,896]{1,0:T(8,128)(2,1)S(1)} %get-tuple-element.41, bf16[192,896]{1,0:T(8,128)(2,1)S(1)} %get-tuple-element.97, bf16[192,896]{1,0:T(8,128)(2,1)S(1)} %get-tuple-element.40, bf16[192,896]{1,0:T(8,128)(2,1)S(1)} %get-tuple-element.77), kind=kOutput, calls=%fused_computation.17 | convolution fusion | flops 1415708672 | bytes 4784128 | tf_op jit(solution)/shard_map/dot_general | solution.py:25
  (187 shorter events, 83.2 us)
Async XLA Ops:
  6.9 21.1 %collective-permute-start.1 = (bf16[144,896]{1,0:T(8,128)(2,1)S(1)}, bf16[144,896]{1,0:T(8,128)(2,1)S(1)}, u32[]{:S(2)}, u32[]{:S(2)}) collective-permute-start(bf16[144,896]{1,0:T(8,128)(2,1)S(1)} %get-tuple-element.115), channel_id=1, source_target_pairs={{0,2},{1,3},{2,0},{3,1},{4,6},{5,7},{6,4},{7,5},{8,10},{9,11},{10,... | collective-permute-start | bytes 774152 | tf_op jit(solution)/shard_map/ppermute | solution.py:44
  9.5 18.5 %collective-permute-start.2 = (bf16[144,896]{1,0:T(8,128)(2,1)S(1)}, bf16[144,896]{1,0:T(8,128)(2,1)S(1)}, u32[]{:S(2)}, u32[]{:S(2)}) collective-permute-start(bf16[144,896]{1,0:T(8,128)(2,1)S(1)} %get-tuple-element.113), channel_id=1, source_target_pairs={{0,3},{1,2},{2,1},{3,0},{4,7},{5,6},{6,5},{7,4},{8,11},{9,10},{10,... | collective-permute-start | bytes 774152 | tf_op jit(solution)/shard_map/ppermute | solution.py:44
  35.1 18.1 %collective-permute-start.15 = (bf16[128,896]{1,0:T(8,128)(2,1)S(1)}, bf16[128,896]{1,0:T(8,128)(2,1)}, u32[]{:S(2)}, u32[]{:S(2)}) collective-permute-start(bf16[128,896]{1,0:T(8,128)(2,1)S(1)} %get-tuple-element.45), channel_id=1, source_target_pairs={{0,2},{1,3},{2,0},{3,1},{4,6},{5,7},{6,4},{7,5},{8,10},{9,11},{10,... | collective-permute-start | bytes 688136 | tf_op jit(solution)/shard_map/ppermute | solution.py:44
  45.9 18.3 %collective-permute-start.4 = (bf16[192,2048]{1,0:T(8,128)(2,1)S(1)}, bf16[192,2048]{1,0:T(8,128)(2,1)S(1)}, u32[]{:S(2)}, u32[]{:S(2)}) collective-permute-start(bf16[192,2048]{1,0:T(8,128)(2,1)S(1)} %get-tuple-element.117), channel_id=1, source_target_pairs={{0,1},{3,2},{4,5},{7,6},{8,9},{11,10},{12,13},{15,14},{16,17},{19,... | collective-permute-start | bytes 2359304 | tf_op jit(solution)/shard_map/ppermute | solution.py:61
  58.4 22.6 %collective-permute-start.9 = (bf16[192,2048]{1,0:T(8,128)(2,1)S(1)}, bf16[192,2048]{1,0:T(8,128)(2,1)S(1)}, u32[]{:S(2)}, u32[]{:S(2)}) collective-permute-start(bf16[192,2048]{1,0:T(8,128)(2,1)S(1)} %get-tuple-element.121), channel_id=1, source_target_pairs={{0,1},{3,2},{4,5},{7,6},{8,9},{11,10},{12,13},{15,14},{16,17},{19,... | collective-permute-start | bytes 2359304 | tf_op jit(solution)/shard_map/ppermute | solution.py:61
  64.5 26.0 %collective-permute-start.5 = (bf16[192,2048]{1,0:T(8,128)(2,1)S(1)}, bf16[192,2048]{1,0:T(8,128)(2,1)S(1)}, u32[]{:S(2)}, u32[]{:S(2)}) collective-permute-start(bf16[192,2048]{1,0:T(8,128)(2,1)S(1)} %convert_element_type.246), channel_id=1, source_target_pairs={{1,2},{2,1},{5,6},{6,5},{9,10},{10,9},{13,14},{14,13},{17,18},{18,... | collective-permute-start | bytes 2359304 | tf_op jit(solution)/shard_map/ppermute | solution.py:68
  65.2 25.1 %collective-permute-start.17 = (bf16[384,896]{1,0:T(8,128)(2,1)S(1)}, bf16[384,896]{1,0:T(8,128)(2,1)S(1)}, u32[]{:S(2)}, u32[]{:S(2)}) collective-permute-start(bf16[384,896]{1,0:T(8,128)(2,1)S(1)} %concatenate.109), channel_id=1, source_target_pairs={{0,8},{4,12},{8,0},{12,4},{1,9},{5,13},{9,1},{13,5},{2,10},{6,14},... | collective-permute-start | bytes 2064392 | tf_op jit(solution)/shard_map/ppermute | solution.py:44
  67.9 30.0 %collective-permute-start.11 = (bf16[192,2048]{1,0:T(8,128)(2,1)S(1)}, bf16[192,2048]{1,0:T(8,128)(2,1)S(1)}, u32[]{:S(2)}, u32[]{:S(2)}) collective-permute-start(bf16[192,2048]{1,0:T(8,128)(2,1)S(1)} %get-tuple-element.119), channel_id=1, source_target_pairs={{0,1},{3,2},{4,5},{7,6},{8,9},{11,10},{12,13},{15,14},{16,17},{19,... | collective-permute-start | bytes 2359304 | tf_op jit(solution)/shard_map/ppermute | solution.py:61
  81.3 26.0 %collective-permute-start.20 = (bf16[192,2048]{1,0:T(8,128)(2,1)S(1)}, bf16[192,2048]{1,0:T(8,128)(2,1)S(1)}, u32[]{:S(2)}, u32[]{:S(2)}) collective-permute-start(bf16[192,2048]{1,0:T(8,128)(2,1)S(1)} %convert_element_type.267), channel_id=1, source_target_pairs={{1,2},{2,1},{5,6},{6,5},{9,10},{10,9},{13,14},{14,13},{17,18},{18,... | collective-permute-start | bytes 2359304 | tf_op jit(solution)/shard_map/ppermute | solution.py:68
  83.1 31.7 %collective-permute-start.10 = (bf16[192,2048]{1,0:T(8,128)(2,1)S(1)}, bf16[192,2048]{1,0:T(8,128)(2,1)S(1)}, u32[]{:S(2)}, u32[]{:S(2)}) collective-permute-start(bf16[192,2048]{1,0:T(8,128)(2,1)S(1)} %get-tuple-element.123), channel_id=1, source_target_pairs={{0,1},{3,2},{4,5},{7,6},{8,9},{11,10},{12,13},{15,14},{16,17},{19,... | collective-permute-start | bytes 2359304 | tf_op jit(solution)/shard_map/ppermute | solution.py:61
  90.7 26.3 %collective-permute-start.6 = (bf16[192,2048]{1,0:T(8,128)(2,1)S(1)}, bf16[192,2048]{1,0:T(8,128)(2,1)S(1)}, u32[]{:S(2)}, u32[]{:S(2)}) collective-permute-start(bf16[192,2048]{1,0:T(8,128)(2,1)S(1)} %add_convert_fusion.5), channel_id=1, source_target_pairs={{1,0},{2,3},{5,4},{6,7},{9,8},{10,11},{13,12},{14,15},{17,16},{18,... | collective-permute-start | bytes 2359304 | tf_op jit(solution)/shard_map/ppermute | solution.py:75
  98.2 27.5 %collective-permute-start.13 = (bf16[192,2048]{1,0:T(8,128)(2,1)S(1)}, bf16[192,2048]{1,0:T(8,128)(2,1)S(1)}, u32[]{:S(2)}, u32[]{:S(2)}) collective-permute-start(bf16[192,2048]{1,0:T(8,128)(2,1)S(1)} %convert_element_type.258), channel_id=1, source_target_pairs={{1,2},{2,1},{5,6},{6,5},{9,10},{10,9},{13,14},{14,13},{17,18},{18,... | collective-permute-start | bytes 2359304 | tf_op jit(solution)/shard_map/ppermute | solution.py:68
  100.0 31.6 %collective-permute-start.19 = (bf16[384,1024]{1,0:T(8,128)(2,1)S(1)}, bf16[384,1024]{1,0:T(8,128)(2,1)S(1)}, u32[]{:S(2)}, u32[]{:S(2)}) collective-permute-start(bf16[384,1024]{1,0:T(8,128)(2,1)S(1)} %get-tuple-element.125), channel_id=1, source_target_pairs={{0,1},{3,2},{4,5},{7,6},{8,9},{11,10},{12,13},{15,14},{16,17},{19,... | collective-permute-start | bytes 2359304 | tf_op jit(solution)/shard_map/ppermute | solution.py:61
  107.5 25.2 %collective-permute-start.21 = (bf16[192,2048]{1,0:T(8,128)(2,1)S(1)}, bf16[192,2048]{1,0:T(8,128)(2,1)S(1)}, u32[]{:S(2)}, u32[]{:S(2)}) collective-permute-start(bf16[192,2048]{1,0:T(8,128)(2,1)S(1)} %add_convert_fusion.3), channel_id=1, source_target_pairs={{1,0},{2,3},{5,4},{6,7},{9,8},{10,11},{13,12},{14,15},{17,16},{18,... | collective-permute-start | bytes 2359304 | tf_op jit(solution)/shard_map/ppermute | solution.py:75
  115.1 18.1 %collective-permute-start.12 = (bf16[192,2048]{1,0:T(8,128)(2,1)S(1)}, bf16[192,2048]{1,0:T(8,128)(2,1)S(1)}, u32[]{:S(2)}, u32[]{:S(2)}) collective-permute-start(bf16[192,2048]{1,0:T(8,128)(2,1)S(1)} %convert_element_type.256), channel_id=1, source_target_pairs={{1,2},{2,1},{5,6},{6,5},{9,10},{10,9},{13,14},{14,13},{17,18},{18,... | collective-permute-start | bytes 2359304 | tf_op jit(solution)/shard_map/ppermute | solution.py:68
  117.0 30.6 %collective-permute-start.28 = (bf16[384,1024]{1,0:T(8,128)(2,1)S(1)}, bf16[384,1024]{1,0:T(8,128)(2,1)S(1)}, u32[]{:S(2)}, u32[]{:S(2)}) collective-permute-start(bf16[384,1024]{1,0:T(8,128)(2,1)S(1)} %get-tuple-element.127), channel_id=1, source_target_pairs={{0,1},{3,2},{4,5},{7,6},{8,9},{11,10},{12,13},{15,14},{16,17},{19,... | collective-permute-start | bytes 2359304 | tf_op jit(solution)/shard_map/ppermute | solution.py:61
  126.0 23.6 %collective-permute-start.22 = (bf16[192,2048]{1,0:T(8,128)(2,1)S(1)}, bf16[192,2048]{1,0:T(8,128)(2,1)S(1)}, u32[]{:S(2)}, u32[]{:S(2)}) collective-permute-start(bf16[192,2048]{1,0:T(8,128)(2,1)S(1)} %add_convert_fusion.2), channel_id=1, source_target_pairs={{1,0},{2,3},{5,4},{6,7},{9,8},{10,11},{13,12},{14,15},{17,16},{18,... | collective-permute-start | bytes 2359304 | tf_op jit(solution)/shard_map/ppermute | solution.py:75
  132.0 20.7 %collective-permute-start.30 = (bf16[384,1024]{1,0:T(8,128)(2,1)S(1)}, bf16[384,1024]{1,0:T(8,128)(2,1)S(1)}, u32[]{:S(2)}, u32[]{:S(2)}) collective-permute-start(bf16[384,1024]{1,0:T(8,128)(2,1)S(1)} %convert_element_type.291), channel_id=1, source_target_pairs={{1,2},{2,1},{5,6},{6,5},{9,10},{10,9},{13,14},{14,13},{17,18},{18,... | collective-permute-start | bytes 2359304 | tf_op jit(solution)/shard_map/ppermute | solution.py:68
  133.6 31.6 %collective-permute-start.14 = (bf16[192,2048]{1,0:T(8,128)(2,1)S(1)}, bf16[192,2048]{1,0:T(8,128)(2,1)S(1)}, u32[]{:S(2)}, u32[]{:S(2)}) collective-permute-start(bf16[192,2048]{1,0:T(8,128)(2,1)S(1)} %add_convert_fusion.4), channel_id=1, source_target_pairs={{1,0},{2,3},{5,4},{6,7},{9,8},{10,11},{13,12},{14,15},{17,16},{18,... | collective-permute-start | bytes 2359304 | tf_op jit(solution)/shard_map/ppermute | solution.py:75
  153.0 29.0 %collective-permute-start.32 = (bf16[384,1024]{1,0:T(8,128)(2,1)S(1)}, bf16[384,1024]{1,0:T(8,128)(2,1)S(1)}, u32[]{:S(2)}, u32[]{:S(2)}) collective-permute-start(bf16[384,1024]{1,0:T(8,128)(2,1)S(1)} %add_convert_fusion), channel_id=1, source_target_pairs={{1,0},{2,3},{5,4},{6,7},{9,8},{10,11},{13,12},{14,15},{17,16},{18,... | collective-permute-start | bytes 2359304 | tf_op jit(solution)/shard_map/ppermute | solution.py:75
  166.2 30.6 %collective-permute-start.31 = (bf16[384,1024]{1,0:T(8,128)(2,1)S(1)}, bf16[384,1024]{1,0:T(8,128)(2,1)S(1)}, u32[]{:S(2)}, u32[]{:S(2)}) collective-permute-start(bf16[384,1024]{1,0:T(8,128)(2,1)S(1)} %add_convert_fusion.1), channel_id=1, source_target_pairs={{1,0},{2,3},{5,4},{6,7},{9,8},{10,11},{13,12},{14,15},{17,16},{18,... | collective-permute-start | bytes 2359304 | tf_op jit(solution)/shard_map/ppermute | solution.py:75
  168.8 28.3 %collective-permute-start.24 = (bf16[384,896]{1,0:T(8,128)(2,1)S(1)}, bf16[384,896]{1,0:T(8,128)(2,1)S(1)}, u32[]{:S(2)}, u32[]{:S(2)}) collective-permute-start(bf16[384,896]{1,0:T(8,128)(2,1)S(1)} %pad_maximum_fusion.12), channel_id=1, source_target_pairs={{0,4},{4,0},{8,12},{12,8},{1,5},{5,1},{9,13},{13,9},{2,6},{6,2},{1... | collective-permute-start | bytes 2064392 | tf_op jit(solution)/shard_map/ppermute | solution.py:44
  198.5 18.3 %collective-permute-start.26 = (bf16[128,896]{1,0:T(8,128)(2,1)S(1)}, bf16[128,896]{1,0:T(8,128)(2,1)S(1)}, u32[]{:S(2)}, u32[]{:S(2)}) collective-permute-start(bf16[128,896]{1,0:T(8,128)(2,1)S(1)} %get-tuple-element.86), channel_id=1, source_target_pairs={{0,2},{1,3},{2,0},{3,1},{4,6},{5,7},{6,4},{7,5},{8,10},{9,11},{10,... | collective-permute-start | bytes 688136 | tf_op jit(solution)/shard_map/ppermute | solution.py:44
  200.5 19.3 %collective-permute-start.27 = (bf16[128,896]{1,0:T(8,128)(2,1)S(1)}, bf16[128,896]{1,0:T(8,128)(2,1)S(1)}, u32[]{:S(2)}, u32[]{:S(2)}) collective-permute-start(bf16[128,896]{1,0:T(8,128)(2,1)S(1)} %get-tuple-element.85), channel_id=1, source_target_pairs={{0,3},{1,2},{2,1},{3,0},{4,7},{5,6},{6,5},{7,4},{8,11},{9,10},{10,... | collective-permute-start | bytes 688136 | tf_op jit(solution)/shard_map/ppermute | solution.py:44
  (26 other events, 337.4 us)

commit v7 on v6

--- a/solution.py
+++ b/solution.py
@@ -165,7 +165,9 @@
             result = lax.dynamic_update_slice(result, piece, (0, (here ^ k) * part))
         return result
 
-    rows = grouped(exchange(dispatch(select_tailed, gathered), bits)[0])
+    sent_rows = dispatch(select_tailed, gathered)
+    ahead = (jnp.dot(sent_rows[0], w_both, preferred_element_type=F32),) if per_group == 1 else ()
+    rows = grouped(exchange(sent_rows, bits, *ahead)[0])
     sent_grads = dispatch(select, jnp.concatenate(got_grads, axis=0))
     grads = None
     sums, pre = [], [None] * GROUPS

time: 239 us -> 239 us (level)
  no operation moved by 1% of the time
where the time goes in v7:
time: 239 us
  waiting for transfers between devices  110 us (46%)
  starting transfers between devices  77.5 us (32%)
  matrix products  30.3 us (13%)
  other arithmetic  13.4 us (6%)
  local copies, waits for them, and re-layouts  5.32 us (2%)
    ppermute x20, waiting for transfers between devices, send(): got = lax.ppermute(self.turn(value), self.axis, pairs)  42 us
    ppermute x6, starting transfers between devices, inward(): arrived = lax.ppermute(self.total.astype(BF16), self.axis, pairs)  36.7 us
    ppermute x6, waiting for transfers between devices, inward(): arrived = lax.ppermute(self.total.astype(BF16), self.axis, pairs)  36.1 us
    ppermute x6, waiting for transfers between devices, outward(): lax.ppermute((self.own + got.astype(F32)).astype(BF16), self.axis, pairs)  32.1 us
    ppermute x20, starting transfers between devices, send(): got = lax.ppermute(self.turn(value), self.axis, pairs)  28.4 us
    dot_general x5, matrix products, over_rows(): lax.dot_general(left, right, (((0,), (0,)), ((), ())), preferred_element_...  10.6 us
    dot_general x8, matrix products, across(): lax.dot_general(left, right, (((1,), (1,)), ((), ())), preferred_element_...  8.76 us
    ppermute x6, starting transfers between devices, outward(): lax.ppermute((self.own + got.astype(F32)).astype(BF16), self.axis, pairs)  7.97 us
  transfers between devices with their start and end apart: 38, of which 17 were waited for; matrix products, arithmetic and copies ran while one was open for 18% of the time, Pallas kernels for 0%

profile of v7, /device:TPU:0, one launch (start us, length us, event | category | flops | bytes accessed | tf_op | source)
XLA Modules:
  0.0 238.5 jit_solution(6619678323722291751)
XLA Ops:
  3.8 3.1 %collective-permute-start = (bf16[144,896]{1,0:T(8,128)(2,1)S(1)}, bf16[144,896]{1,0:T(8,128)(2,1)S(1)}, u32[]{:S(2)}, u32[]{:S(2)}) collective-permute-start(bf16[144,896]{1,0:T(8,128)(2,1)S(1)} %get-tuple-element.118), channel_id=1, source_target_pairs={{0,1},{1,0},{2,3},{3,2},{4,5},{5,4},{6,7},{7,6},{8,9},{9,8},{10,11... | collective-permute-start | bytes 774152 | tf_op jit(solution)/shard_map/ppermute | solution.py:44
  10.5 7.4 %collective-permute-done = bf16[144,896]{1,0:T(8,128)(2,1)S(1)} collective-permute-done((bf16[144,896]{1,0:T(8,128)(2,1)S(1)}, bf16[144,896]{1,0:T(8,128)(2,1)S(1)}, u32[]{:S(2)}, u32[]{:S(2)}) %collective-permute-start) | collective-permute-done | bytes 258080 | tf_op jit(solution)/shard_map/ppermute | solution.py:44
  17.9 10.1 %collective-permute-done.1 = bf16[144,896]{1,0:T(8,128)(2,1)S(1)} collective-permute-done((bf16[144,896]{1,0:T(8,128)(2,1)S(1)}, bf16[144,896]{1,0:T(8,128)(2,1)S(1)}, u32[]{:S(2)}, u32[]{:S(2)}) %collective-permute-start.1) | collective-permute-done | bytes 258080 | tf_op jit(solution)/shard_map/ppermute | solution.py:44
  28.0 4.7 %collective-permute-start.3 = (bf16[128,896]{1,0:T(8,128)(2,1)}, bf16[128,896]{1,0:T(8,128)(2,1)}, u32[]{:S(2)}, u32[]{:S(2)}) collective-permute-start(bf16[128,896]{1,0:T(8,128)(2,1)} %get-tuple-element.37), channel_id=1, source_target_pairs={{0,1},{1,0},{2,3},{3,2},{4,5},{5,4},{6,7},{7,6},{8,9},{9,8},{10,11... | collective-permute-start | bytes 688136 | tf_op jit(solution)/shard_map/ppermute | solution.py:44
  35.1 3.9 %collective-permute-done.3 = bf16[128,896]{1,0:T(8,128)(2,1)} collective-permute-done((bf16[128,896]{1,0:T(8,128)(2,1)}, bf16[128,896]{1,0:T(8,128)(2,1)}, u32[]{:S(2)}, u32[]{:S(2)}) %collective-permute-start.3) | collective-permute-done | bytes 229408 | tf_op jit(solution)/shard_map/ppermute | solution.py:44
  46.0 4.4 %collective-permute-start.4 = (bf16[192,2048]{1,0:T(8,128)(2,1)S(1)}, bf16[192,2048]{1,0:T(8,128)(2,1)S(1)}, u32[]{:S(2)}, u32[]{:S(2)}) collective-permute-start(bf16[192,2048]{1,0:T(8,128)(2,1)S(1)} %get-tuple-element.121), channel_id=1, source_target_pairs={{0,1},{3,2},{4,5},{7,6},{8,9},{11,10},{12,13},{15,14},{16,17},{19,... | collective-permute-start | bytes 2359304 | tf_op jit(solution)/shard_map/ppermute | solution.py:61
  59.5 3.4 %collective-permute-start.9 = (bf16[192,2048]{1,0:T(8,128)(2,1)S(1)}, bf16[192,2048]{1,0:T(8,128)(2,1)S(1)}, u32[]{:S(2)}, u32[]{:S(2)}) collective-permute-start(bf16[192,2048]{1,0:T(8,128)(2,1)S(1)} %get-tuple-element.125), channel_id=1, source_target_pairs={{0,1},{3,2},{4,5},{7,6},{8,9},{11,10},{12,13},{15,14},{16,17},{19,... | collective-permute-start | bytes 2359304 | tf_op jit(solution)/shard_map/ppermute | solution.py:61
  67.0 7.2 %collective-permute-start.11 = (bf16[192,2048]{1,0:T(8,128)(2,1)S(1)}, bf16[192,2048]{1,0:T(8,128)(2,1)S(1)}, u32[]{:S(2)}, u32[]{:S(2)}) collective-permute-start(bf16[192,2048]{1,0:T(8,128)(2,1)S(1)} %get-tuple-element.123), channel_id=1, source_target_pairs={{0,1},{3,2},{4,5},{7,6},{8,9},{11,10},{12,13},{15,14},{16,17},{19,... | collective-permute-start | bytes 2359304 | tf_op jit(solution)/shard_map/ppermute | solution.py:61
  74.2 6.4 %collective-permute-done.9 = bf16[192,2048]{1,0:T(8,128)(2,1)S(1)} collective-permute-done((bf16[192,2048]{1,0:T(8,128)(2,1)S(1)}, bf16[192,2048]{1,0:T(8,128)(2,1)S(1)}, u32[]{:S(2)}, u32[]{:S(2)}) %collective-permute-start.9) | collective-permute-done | bytes 786464 | tf_op jit(solution)/shard_map/ppermute | solution.py:61
  82.7 7.2 %collective-permute-start.10 = (bf16[192,2048]{1,0:T(8,128)(2,1)S(1)}, bf16[192,2048]{1,0:T(8,128)(2,1)S(1)}, u32[]{:S(2)}, u32[]{:S(2)}) collective-permute-start(bf16[192,2048]{1,0:T(8,128)(2,1)S(1)} %get-tuple-element.127), channel_id=1, source_target_pairs={{0,1},{3,2},{4,5},{7,6},{8,9},{11,10},{12,13},{15,14},{16,17},{19,... | collective-permute-start | bytes 2359304 | tf_op jit(solution)/shard_map/ppermute | solution.py:61
  91.6 5.9 %collective-permute-done.11 = bf16[192,2048]{1,0:T(8,128)(2,1)S(1)} collective-permute-done((bf16[192,2048]{1,0:T(8,128)(2,1)S(1)}, bf16[192,2048]{1,0:T(8,128)(2,1)S(1)}, u32[]{:S(2)}, u32[]{:S(2)}) %collective-permute-start.11) | collective-permute-done | bytes 786464 | tf_op jit(solution)/shard_map/ppermute | solution.py:61
  99.7 7.2 %collective-permute-start.19 = (bf16[384,1024]{1,0:T(8,128)(2,1)S(1)}, bf16[384,1024]{1,0:T(8,128)(2,1)S(1)}, u32[]{:S(2)}, u32[]{:S(2)}) collective-permute-start(bf16[384,1024]{1,0:T(8,128)(2,1)S(1)} %get-tuple-element.129), channel_id=1, source_target_pairs={{0,1},{3,2},{4,5},{7,6},{8,9},{11,10},{12,13},{15,14},{16,17},{19,... | collective-permute-start | bytes 2359304 | tf_op jit(solution)/shard_map/ppermute | solution.py:61
  108.5 5.9 %collective-permute-done.10 = bf16[192,2048]{1,0:T(8,128)(2,1)S(1)} collective-permute-done((bf16[192,2048]{1,0:T(8,128)(2,1)S(1)}, bf16[192,2048]{1,0:T(8,128)(2,1)S(1)}, u32[]{:S(2)}, u32[]{:S(2)}) %collective-permute-start.10) | collective-permute-done | bytes 786464 | tf_op jit(solution)/shard_map/ppermute | solution.py:61
  116.6 7.2 %collective-permute-start.28 = (bf16[384,1024]{1,0:T(8,128)(2,1)S(1)}, bf16[384,1024]{1,0:T(8,128)(2,1)S(1)}, u32[]{:S(2)}, u32[]{:S(2)}) collective-permute-start(bf16[384,1024]{1,0:T(8,128)(2,1)S(1)} %get-tuple-element.131), channel_id=1, source_target_pairs={{0,1},{3,2},{4,5},{7,6},{8,9},{11,10},{12,13},{15,14},{16,17},{19,... | collective-permute-start | bytes 2359304 | tf_op jit(solution)/shard_map/ppermute | solution.py:61
  126.9 4.3 %collective-permute-done.19 = bf16[384,1024]{1,0:T(8,128)(2,1)S(1)} collective-permute-done((bf16[384,1024]{1,0:T(8,128)(2,1)S(1)}, bf16[384,1024]{1,0:T(8,128)(2,1)S(1)}, u32[]{:S(2)}, u32[]{:S(2)}) %collective-permute-start.19) | collective-permute-done | bytes 786464 | tf_op jit(solution)/shard_map/ppermute | solution.py:61
  134.5 13.1 %collective-permute-done.28 = bf16[384,1024]{1,0:T(8,128)(2,1)S(1)} collective-permute-done((bf16[384,1024]{1,0:T(8,128)(2,1)S(1)}, bf16[384,1024]{1,0:T(8,128)(2,1)S(1)}, u32[]{:S(2)}, u32[]{:S(2)}) %collective-permute-start.28) | collective-permute-done | bytes 786464 | tf_op jit(solution)/shard_map/ppermute | solution.py:61
  154.4 10.4 %collective-permute-done.14 = bf16[192,2048]{1,0:T(8,128)(2,1)S(1)} collective-permute-done((bf16[192,2048]{1,0:T(8,128)(2,1)S(1)}, bf16[192,2048]{1,0:T(8,128)(2,1)S(1)}, u32[]{:S(2)}, u32[]{:S(2)}) %collective-permute-start.14) | collective-permute-done | bytes 786464 | tf_op jit(solution)/shard_map/ppermute | solution.py:75
  168.6 13.1 %collective-permute-done.32 = bf16[384,1024]{1,0:T(8,128)(2,1)S(1)} collective-permute-done((bf16[384,1024]{1,0:T(8,128)(2,1)S(1)}, bf16[384,1024]{1,0:T(8,128)(2,1)S(1)}, u32[]{:S(2)}, u32[]{:S(2)}) %collective-permute-start.32) | collective-permute-done | bytes 786464 | tf_op jit(solution)/shard_map/ppermute | solution.py:75
  187.9 8.6 %collective-permute-done.31 = bf16[384,1024]{1,0:T(8,128)(2,1)S(1)} collective-permute-done((bf16[384,1024]{1,0:T(8,128)(2,1)S(1)}, bf16[384,1024]{1,0:T(8,128)(2,1)S(1)}, u32[]{:S(2)}, u32[]{:S(2)}) %collective-permute-start.31) | collective-permute-done | bytes 786464 | tf_op jit(solution)/shard_map/ppermute | solution.py:75
  202.6 5.7 %collective-permute-done.25 = bf16[128,896]{1,0:T(8,128)(2,1)S(1)} collective-permute-done((bf16[128,896]{1,0:T(8,128)(2,1)S(1)}, bf16[128,896]{1,0:T(8,128)(2,1)S(1)}, u32[]{:S(2)}, u32[]{:S(2)}) %collective-permute-start.25) | collective-permute-done | bytes 229408 | tf_op jit(solution)/shard_map/ppermute | solution.py:44
  212.0 4.5 %collective-permute-done.26 = bf16[128,896]{1,0:T(8,128)(2,1)S(1)} collective-permute-done((bf16[128,896]{1,0:T(8,128)(2,1)S(1)}, bf16[128,896]{1,0:T(8,128)(2,1)S(1)}, u32[]{:S(2)}, u32[]{:S(2)}) %collective-permute-start.26) | collective-permute-done | bytes 229408 | tf_op jit(solution)/shard_map/ppermute | solution.py:44
  223.9 4.9 %collective-permute-done.35 = bf16[128,896]{1,0:T(8,128)(2,1)S(1)} collective-permute-done((bf16[128,896]{1,0:T(8,128)(2,1)S(1)}, bf16[128,896]{1,0:T(8,128)(2,1)S(1)}, u32[]{:S(2)}, u32[]{:S(2)}) %collective-permute-start.35) | collective-permute-done | bytes 229408 | tf_op jit(solution)/shard_map/ppermute | solution.py:44
  228.9 2.9 %convert_bitcast_fusion.2 = bf16[1,896,1024]{2,1,0:T(8,128)(2,1)} fusion(bf16[768,2048]{1,0:T(8,128)(2,1)S(1)} %pad_maximum_fusion.1, bf16[192,896]{1,0:T(8,128)(2,1)S(1)} %get-tuple-element.45, bf16[192,896]{1,0:T(8,128)(2,1)S(1)} %get-tuple-element.101, bf16[192,896]{1,0:T(8,128)(2,1)S(1)} %get-tuple-element.44, bf16[192,896]{1,0:T(8,128)(2,1)S(1)} %get-tuple-element.81), kind=kOutput, calls=%fused_computation.18 | convolution fusion | flops 1415708672 | bytes 4784128 | tf_op jit(solution)/shard_map/dot_general | solution.py:25
  231.7 2.9 %convert_bitcast_fusion.1 = bf16[1,896,1024]{2,1,0:T(8,128)(2,1)} fusion(bf16[768,2048]{1,0:T(8,128)(2,1)S(1)} %pad_maximum_fusion.1, bf16[192,896]{1,0:T(8,128)(2,1)S(1)} %get-tuple-element.45, bf16[192,896]{1,0:T(8,128)(2,1)S(1)} %get-tuple-element.101, bf16[192,896]{1,0:T(8,128)(2,1)S(1)} %get-tuple-element.44, bf16[192,896]{1,0:T(8,128)(2,1)S(1)} %get-tuple-element.81), kind=kOutput, calls=%fused_computation.17 | convolution fusion | flops 1415708672 | bytes 4784128 | tf_op jit(solution)/shard_map/dot_general | solution.py:25
  (187 shorter events, 82.4 us)
Async XLA Ops:
  6.9 21.1 %collective-permute-start.1 = (bf16[144,896]{1,0:T(8,128)(2,1)S(1)}, bf16[144,896]{1,0:T(8,128)(2,1)S(1)}, u32[]{:S(2)}, u32[]{:S(2)}) collective-permute-start(bf16[144,896]{1,0:T(8,128)(2,1)S(1)} %get-tuple-element.119), channel_id=1, source_target_pairs={{0,2},{1,3},{2,0},{3,1},{4,6},{5,7},{6,4},{7,5},{8,10},{9,11},{10,... | collective-permute-start | bytes 774152 | tf_op jit(solution)/shard_map/ppermute | solution.py:44
  9.5 18.5 %collective-permute-start.2 = (bf16[144,896]{1,0:T(8,128)(2,1)S(1)}, bf16[144,896]{1,0:T(8,128)(2,1)S(1)}, u32[]{:S(2)}, u32[]{:S(2)}) collective-permute-start(bf16[144,896]{1,0:T(8,128)(2,1)S(1)} %get-tuple-element.117), channel_id=1, source_target_pairs={{0,3},{1,2},{2,1},{3,0},{4,7},{5,6},{6,5},{7,4},{8,11},{9,10},{10,... | collective-permute-start | bytes 774152 | tf_op jit(solution)/shard_map/ppermute | solution.py:44
  35.1 18.1 %collective-permute-start.15 = (bf16[128,896]{1,0:T(8,128)(2,1)S(1)}, bf16[128,896]{1,0:T(8,128)(2,1)}, u32[]{:S(2)}, u32[]{:S(2)}) collective-permute-start(bf16[128,896]{1,0:T(8,128)(2,1)S(1)} %get-tuple-element.49), channel_id=1, source_target_pairs={{0,2},{1,3},{2,0},{3,1},{4,6},{5,7},{6,4},{7,5},{8,10},{9,11},{10,... | collective-permute-start | bytes 688136 | tf_op jit(solution)/shard_map/ppermute | solution.py:44
  59.5 21.2 %collective-permute-start.9 = (bf16[192,2048]{1,0:T(8,128)(2,1)S(1)}, bf16[192,2048]{1,0:T(8,128)(2,1)S(1)}, u32[]{:S(2)}, u32[]{:S(2)}) collective-permute-start(bf16[192,2048]{1,0:T(8,128)(2,1)S(1)} %get-tuple-element.125), channel_id=1, source_target_pairs={{0,1},{3,2},{4,5},{7,6},{8,9},{11,10},{12,13},{15,14},{16,17},{19,... | collective-permute-start | bytes 2359304 | tf_op jit(solution)/shard_map/ppermute | solution.py:61
  63.6 26.5 %collective-permute-start.5 = (bf16[192,2048]{1,0:T(8,128)(2,1)S(1)}, bf16[192,2048]{1,0:T(8,128)(2,1)S(1)}, u32[]{:S(2)}, u32[]{:S(2)}) collective-permute-start(bf16[192,2048]{1,0:T(8,128)(2,1)S(1)} %convert_element_type.246), channel_id=1, source_target_pairs={{1,2},{2,1},{5,6},{6,5},{9,10},{10,9},{13,14},{14,13},{17,18},{18,... | collective-permute-start | bytes 2359304 | tf_op jit(solution)/shard_map/ppermute | solution.py:68
  64.4 25.6 %collective-permute-start.17 = (bf16[384,896]{1,0:T(8,128)(2,1)S(1)}, bf16[384,896]{1,0:T(8,128)(2,1)S(1)}, u32[]{:S(2)}, u32[]{:S(2)}) collective-permute-start(bf16[384,896]{1,0:T(8,128)(2,1)S(1)} %concatenate.109), channel_id=1, source_target_pairs={{0,8},{4,12},{8,0},{12,4},{1,9},{5,13},{9,1},{13,5},{2,10},{6,14},... | collective-permute-start | bytes 2064392 | tf_op jit(solution)/shard_map/ppermute | solution.py:44
  67.0 30.5 %collective-permute-start.11 = (bf16[192,2048]{1,0:T(8,128)(2,1)S(1)}, bf16[192,2048]{1,0:T(8,128)(2,1)S(1)}, u32[]{:S(2)}, u32[]{:S(2)}) collective-permute-start(bf16[192,2048]{1,0:T(8,128)(2,1)S(1)} %get-tuple-element.123), channel_id=1, source_target_pairs={{0,1},{3,2},{4,5},{7,6},{8,9},{11,10},{12,13},{15,14},{16,17},{19,... | collective-permute-start | bytes 2359304 | tf_op jit(solution)/shard_map/ppermute | solution.py:61
  81.0 26.0 %collective-permute-start.20 = (bf16[192,2048]{1,0:T(8,128)(2,1)S(1)}, bf16[192,2048]{1,0:T(8,128)(2,1)S(1)}, u32[]{:S(2)}, u32[]{:S(2)}) collective-permute-start(bf16[192,2048]{1,0:T(8,128)(2,1)S(1)} %convert_element_type.267), channel_id=1, source_target_pairs={{1,2},{2,1},{5,6},{6,5},{9,10},{10,9},{13,14},{14,13},{17,18},{18,... | collective-permute-start | bytes 2359304 | tf_op jit(solution)/shard_map/ppermute | solution.py:68
  82.7 31.7 %collective-permute-start.10 = (bf16[192,2048]{1,0:T(8,128)(2,1)S(1)}, bf16[192,2048]{1,0:T(8,128)(2,1)S(1)}, u32[]{:S(2)}, u32[]{:S(2)}) collective-permute-start(bf16[192,2048]{1,0:T(8,128)(2,1)S(1)} %get-tuple-element.127), channel_id=1, source_target_pairs={{0,1},{3,2},{4,5},{7,6},{8,9},{11,10},{12,13},{15,14},{16,17},{19,... | collective-permute-start | bytes 2359304 | tf_op jit(solution)/shard_map/ppermute | solution.py:61
  90.3 26.3 %collective-permute-start.6 = (bf16[192,2048]{1,0:T(8,128)(2,1)S(1)}, bf16[192,2048]{1,0:T(8,128)(2,1)S(1)}, u32[]{:S(2)}, u32[]{:S(2)}) collective-permute-start(bf16[192,2048]{1,0:T(8,128)(2,1)S(1)} %add_convert_fusion.5), channel_id=1, source_target_pairs={{1,0},{2,3},{5,4},{6,7},{9,8},{10,11},{13,12},{14,15},{17,16},{18,... | collective-permute-start | bytes 2359304 | tf_op jit(solution)/shard_map/ppermute | solution.py:75
  97.8 27.6 %collective-permute-start.13 = (bf16[192,2048]{1,0:T(8,128)(2,1)S(1)}, bf16[192,2048]{1,0:T(8,128)(2,1)S(1)}, u32[]{:S(2)}, u32[]{:S(2)}) collective-permute-start(bf16[192,2048]{1,0:T(8,128)(2,1)S(1)} %convert_element_type.258), channel_id=1, source_target_pairs={{1,2},{2,1},{5,6},{6,5},{9,10},{10,9},{13,14},{14,13},{17,18},{18,... | collective-permute-start | bytes 2359304 | tf_op jit(solution)/shard_map/ppermute | solution.py:68
  99.7 31.5 %collective-permute-start.19 = (bf16[384,1024]{1,0:T(8,128)(2,1)S(1)}, bf16[384,1024]{1,0:T(8,128)(2,1)S(1)}, u32[]{:S(2)}, u32[]{:S(2)}) collective-permute-start(bf16[384,1024]{1,0:T(8,128)(2,1)S(1)} %get-tuple-element.129), channel_id=1, source_target_pairs={{0,1},{3,2},{4,5},{7,6},{8,9},{11,10},{12,13},{15,14},{16,17},{19,... | collective-permute-start | bytes 2359304 | tf_op jit(solution)/shard_map/ppermute | solution.py:61
  107.2 25.1 %collective-permute-start.21 = (bf16[192,2048]{1,0:T(8,128)(2,1)S(1)}, bf16[192,2048]{1,0:T(8,128)(2,1)S(1)}, u32[]{:S(2)}, u32[]{:S(2)}) collective-permute-start(bf16[192,2048]{1,0:T(8,128)(2,1)S(1)} %add_convert_fusion.3), channel_id=1, source_target_pairs={{1,0},{2,3},{5,4},{6,7},{9,8},{10,11},{13,12},{14,15},{17,16},{18,... | collective-permute-start | bytes 2359304 | tf_op jit(solution)/shard_map/ppermute | solution.py:75
  114.7 18.1 %collective-permute-start.12 = (bf16[192,2048]{1,0:T(8,128)(2,1)S(1)}, bf16[192,2048]{1,0:T(8,128)(2,1)S(1)}, u32[]{:S(2)}, u32[]{:S(2)}) collective-permute-start(bf16[192,2048]{1,0:T(8,128)(2,1)S(1)} %convert_element_type.256), channel_id=1, source_target_pairs={{1,2},{2,1},{5,6},{6,5},{9,10},{10,9},{13,14},{14,13},{17,18},{18,... | collective-permute-start | bytes 2359304 | tf_op jit(solution)/shard_map/ppermute | solution.py:68
  116.6 31.1 %collective-permute-start.28 = (bf16[384,1024]{1,0:T(8,128)(2,1)S(1)}, bf16[384,1024]{1,0:T(8,128)(2,1)S(1)}, u32[]{:S(2)}, u32[]{:S(2)}) collective-permute-start(bf16[384,1024]{1,0:T(8,128)(2,1)S(1)} %get-tuple-element.131), channel_id=1, source_target_pairs={{0,1},{3,2},{4,5},{7,6},{8,9},{11,10},{12,13},{15,14},{16,17},{19,... | collective-permute-start | bytes 2359304 | tf_op jit(solution)/shard_map/ppermute | solution.py:61
  125.6 24.1 %collective-permute-start.22 = (bf16[192,2048]{1,0:T(8,128)(2,1)S(1)}, bf16[192,2048]{1,0:T(8,128)(2,1)S(1)}, u32[]{:S(2)}, u32[]{:S(2)}) collective-permute-start(bf16[192,2048]{1,0:T(8,128)(2,1)S(1)} %add_convert_fusion.2), channel_id=1, source_target_pairs={{1,0},{2,3},{5,4},{6,7},{9,8},{10,11},{13,12},{14,15},{17,16},{18,... | collective-permute-start | bytes 2359304 | tf_op jit(solution)/shard_map/ppermute | solution.py:75
  131.6 21.2 %collective-permute-start.30 = (bf16[384,1024]{1,0:T(8,128)(2,1)S(1)}, bf16[384,1024]{1,0:T(8,128)(2,1)S(1)}, u32[]{:S(2)}, u32[]{:S(2)}) collective-permute-start(bf16[384,1024]{1,0:T(8,128)(2,1)S(1)} %convert_element_type.291), channel_id=1, source_target_pairs={{1,2},{2,1},{5,6},{6,5},{9,10},{10,9},{13,14},{14,13},{17,18},{18,... | collective-permute-start | bytes 2359304 | tf_op jit(solution)/shard_map/ppermute | solution.py:68
  133.2 31.6 %collective-permute-start.14 = (bf16[192,2048]{1,0:T(8,128)(2,1)S(1)}, bf16[192,2048]{1,0:T(8,128)(2,1)S(1)}, u32[]{:S(2)}, u32[]{:S(2)}) collective-permute-start(bf16[192,2048]{1,0:T(8,128)(2,1)S(1)} %add_convert_fusion.4), channel_id=1, source_target_pairs={{1,0},{2,3},{5,4},{6,7},{9,8},{10,11},{13,12},{14,15},{17,16},{18,... | collective-permute-start | bytes 2359304 | tf_op jit(solution)/shard_map/ppermute | solution.py:75
  153.1 28.6 %collective-permute-start.32 = (bf16[384,1024]{1,0:T(8,128)(2,1)S(1)}, bf16[384,1024]{1,0:T(8,128)(2,1)S(1)}, u32[]{:S(2)}, u32[]{:S(2)}) collective-permute-start(bf16[384,1024]{1,0:T(8,128)(2,1)S(1)} %add_convert_fusion), channel_id=1, source_target_pairs={{1,0},{2,3},{5,4},{6,7},{9,8},{10,11},{13,12},{14,15},{17,16},{18,... | collective-permute-start | bytes 2359304 | tf_op jit(solution)/shard_map/ppermute | solution.py:75
  165.9 30.6 %collective-permute-start.31 = (bf16[384,1024]{1,0:T(8,128)(2,1)S(1)}, bf16[384,1024]{1,0:T(8,128)(2,1)S(1)}, u32[]{:S(2)}, u32[]{:S(2)}) collective-permute-start(bf16[384,1024]{1,0:T(8,128)(2,1)S(1)} %add_convert_fusion.1), channel_id=1, source_target_pairs={{1,0},{2,3},{5,4},{6,7},{9,8},{10,11},{13,12},{14,15},{17,16},{18,... | collective-permute-start | bytes 2359304 | tf_op jit(solution)/shard_map/ppermute | solution.py:75
  168.5 28.3 %collective-permute-start.24 = (bf16[384,896]{1,0:T(8,128)(2,1)S(1)}, bf16[384,896]{1,0:T(8,128)(2,1)S(1)}, u32[]{:S(2)}, u32[]{:S(2)}) collective-permute-start(bf16[384,896]{1,0:T(8,128)(2,1)S(1)} %pad_maximum_fusion.12), channel_id=1, source_target_pairs={{0,4},{4,0},{8,12},{12,8},{1,5},{5,1},{9,13},{13,9},{2,6},{6,2},{1... | collective-permute-start | bytes 2064392 | tf_op jit(solution)/shard_map/ppermute | solution.py:44
  198.2 18.3 %collective-permute-start.26 = (bf16[128,896]{1,0:T(8,128)(2,1)S(1)}, bf16[128,896]{1,0:T(8,128)(2,1)S(1)}, u32[]{:S(2)}, u32[]{:S(2)}) collective-permute-start(bf16[128,896]{1,0:T(8,128)(2,1)S(1)} %get-tuple-element.90), channel_id=1, source_target_pairs={{0,2},{1,3},{2,0},{3,1},{4,6},{5,7},{6,4},{7,5},{8,10},{9,11},{10,... | collective-permute-start | bytes 688136 | tf_op jit(solution)/shard_map/ppermute | solution.py:44
  200.1 19.3 %collective-permute-start.27 = (bf16[128,896]{1,0:T(8,128)(2,1)S(1)}, bf16[128,896]{1,0:T(8,128)(2,1)S(1)}, u32[]{:S(2)}, u32[]{:S(2)}) collective-permute-start(bf16[128,896]{1,0:T(8,128)(2,1)S(1)} %get-tuple-element.89), channel_id=1, source_target_pairs={{0,3},{1,2},{2,1},{3,0},{4,7},{5,6},{6,5},{7,4},{8,11},{9,10},{10,... | collective-permute-start | bytes 688136 | tf_op jit(solution)/shard_map/ppermute | solution.py:44
  219.5 18.0 %collective-permute-start.36 = (bf16[128,896]{1,0:T(8,128)(2,1)S(1)}, bf16[128,896]{1,0:T(8,128)(2,1)S(1)}, u32[]{:S(2)}, u32[]{:S(2)}) collective-permute-start(bf16[128,896]{1,0:T(8,128)(2,1)S(1)} %get-tuple-element.86), channel_id=1, source_target_pairs={{0,2},{1,3},{2,0},{3,1},{4,6},{5,7},{6,4},{7,5},{8,10},{9,11},{10,... | collective-permute-start | bytes 688136 | tf_op jit(solution)/shard_map/ppermute | solution.py:44
  (26 other events, 334.2 us)
